TPU v7x, 32 devices: a whole 2x2x4 slice. The times are simulated.
32 devices in a mesh: page: 4 (over y, x), strip: 8 (over z, core).
Axes of the slice: x: 2, y: 2, z: 4, core: 2. Of those that a mesh axis runs over, the one named last changes fastest.
Arguments:
- vis_tokens: bfloat16 [4, 96, 84, 768], P('page', 'strip'), may hold values from -6 to 6
- query_tokens: bfloat16 [4, 256, 768], P('page', 'strip'), may hold values from -6 to 6
- region_ids: int32 [4, 96, 84], P('page'), may hold values from 0 to 2
- query_mask: int32 [4, 256], P('page'), may hold values 0 or 1
- answer_len: int32 [4], P('page'), may hold values from 32 to 160, as said below
- norm1_gain: float32 [2, 768], replicated, may hold values from 0.5 to 1.5
- norm1_bias: float32 [2, 768], replicated, may hold values from -1.25 to 1.25
- qkv_weight: bfloat16 [2, 768, 2304], replicated, may hold values from -0.21875 to 0.21875
- out_weight: bfloat16 [2, 768, 768], replicated, may hold values from -4 to 4
- out_bias: float32 [2, 768], replicated, may hold values from -1.25 to 1.25
- norm2_gain: float32 [2, 768], replicated, may hold values from 0.5 to 1.5
- norm2_bias: float32 [2, 768], replicated, may hold values from -1.25 to 1.25
- up_weight: bfloat16 [2, 768, 3072], replicated, may hold values from -0.21875 to 0.21875
- up_bias: float32 [2, 3072], replicated, may hold values from -1.25 to 1.25
- down_weight: bfloat16 [2, 3072, 768], replicated, may hold values from -0.109375 to 0.109375
- down_bias: float32 [2, 768], replicated, may hold values from -1.25 to 1.25
- vis_cotangent: bfloat16 [4, 96, 84, 768], P('page', 'strip'), may hold values from -6 to 6
- query_cotangent: bfloat16 [4, 256, 768], P('page', 'strip'), may hold values from -6 to 6
Outputs:
- vis_out: bfloat16 [4, 96, 84, 768], P('page', 'strip')
- query_out: bfloat16 [4, 256, 768], P('page', 'strip')
- vis_grad: bfloat16 [4, 96, 84, 768], P('page', 'strip')
- query_grad: bfloat16 [4, 256, 768], P('page', 'strip')
- grad_norm1_gain: float32 [2, 768], P(None, 'strip')
- grad_norm1_bias: float32 [2, 768], P(None, 'strip')
- grad_qkv_weight: float32 [2, 768, 2304], P(None, 'strip')
- grad_out_weight: float32 [2, 768, 768], P(None, 'strip')
- grad_out_bias: float32 [2, 768], P(None, 'strip')
- grad_norm2_gain: float32 [2, 768], P(None, 'strip')
- grad_norm2_bias: float32 [2, 768], P(None, 'strip')
- grad_up_weight: float32 [2, 768, 3072], P(None, 'strip')
- grad_up_bias: float32 [2, 3072], P(None, 'strip')
- grad_down_weight: float32 [2, 3072, 768], P(None, 'strip')
- grad_down_bias: float32 [2, 768], P(None, 'strip')
Inputs may be any that keep to these rules, and one draw needn't show every extreme that they name: Some page's answer_len is exactly 160.
All inputs are finite; a program needn't handle non-finite values. No bound on the sum of `query_mask` on one device may be relied on, other than what follows from the above.
Results may differ from a plain program's by a relative error of at most 0.014.
Values may be sent and summed in bfloat16 or wider, within the bound.
No kernel may reach another device: no remote copies, remote signals or barrier semaphores. Data moves between devices by JAX's collectives and lax.ppermute only.
A program may use at most 448 MiB of HBM per device.

v0:
```python
import functools

import jax
import jax.numpy as jnp
from jax import lax
from jax.experimental import pallas as pl
from jax.experimental.pallas import tpu as pltpu
from jax.sharding import PartitionSpec as P

HEADS = 12
WIN = 12
SHIFT = 6
CELLS = WIN * WIN
PAIR = 128
MASKED = -1000000000.0
VMEM_LIMIT = 56 * 1024 * 1024

bf16 = jnp.bfloat16
f32 = jnp.float32


def params():
    return pltpu.CompilerParams(vmem_limit_bytes=VMEM_LIMIT)


def row_block(rows):
    for size in range(336, 15, -16):
        if rows % size == 0:
            return size
    return rows


def dot_nn(a, b):
    return lax.dot_general(a, b, (((1,), (0,)), ((), ())), preferred_element_type=f32)


def dot_nt(a, b):
    return lax.dot_general(a, b, (((1,), (1,)), ((), ())), preferred_element_type=f32)


def dot_tn(a, b):
    return lax.dot_general(a, b, (((0,), (0,)), ((), ())), preferred_element_type=f32)


def cost(flops, moved, special=0):
    share = 20000
    return pl.CostEstimate(
        flops=int(flops) // share,
        bytes_accessed=int(moved) // share,
        transcendentals=int(special) // share,
    )


def whole(shape):
    return pl.BlockSpec(shape, lambda *_: (0,) * len(shape))


def normalised(values):
    center = values - jnp.mean(values, -1, keepdims=True)
    spread = jnp.mean(center * center, -1, keepdims=True)
    rstd = lax.rsqrt(spread + 1e-05)
    return center * rstd, rstd


def norm_back(grad, hat, rstd, gain):
    scaled = grad * gain
    mean_one = jnp.mean(scaled, -1, keepdims=True)
    mean_two = jnp.mean(scaled * hat, -1, keepdims=True)
    return rstd * (scaled - mean_one - hat * mean_two)


def enter_kernel(own_ref, head_ref, out_ref, row_ref, cells_ref):
    columns = own_ref.shape[1]
    for r in range(WIN):
        row = own_ref[SHIFT + r] if r < WIN - SHIFT else head_ref[r - (WIN - SHIFT)]
        row_ref[0:columns, :] = row.astype(f32)
        row_ref[columns : columns + SHIFT, :] = row_ref[0:SHIFT, :]
        for w in range(columns // WIN):
            at = w * CELLS + r * WIN
            cells_ref[at : at + WIN, :] = row_ref[w * WIN + SHIFT : (w + 1) * WIN + SHIFT, :]
    for w in range(columns // WIN):
        at = slice(w * CELLS, (w + 1) * CELLS)
        out_ref[at, :] = cells_ref[at, :].astype(bf16)


def enter(own, head):
    rows, columns, width = own.shape
    cells = rows * columns
    return pl.pallas_call(
        enter_kernel,
        out_shape=jax.ShapeDtypeStruct((cells, width), bf16),
        scratch_shapes=[
            pltpu.VMEM((columns + 2 * WIN, width), f32),
            pltpu.VMEM((cells, width), f32),
        ],
        compiler_params=params(),
        cost_estimate=cost(0, 4 * cells * width),
        name="enter",
    )(own, head)


def leave_kernel(cells_ref, keep_ref, send_ref, row_ref, wide_ref):
    columns = keep_ref.shape[1]
    for w in range(columns // WIN):
        at = slice(w * CELLS, (w + 1) * CELLS)
        wide_ref[at, :] = cells_ref[at, :].astype(f32)
    for r in range(WIN):
        for w in range(columns // WIN):
            at = w * CELLS + r * WIN
            row_ref[w * WIN + SHIFT : (w + 1) * WIN + SHIFT, :] = wide_ref[at : at + WIN, :]
        row_ref[0:SHIFT, :] = row_ref[columns : columns + SHIFT, :]
        row = row_ref[0:columns, :].astype(bf16)
        if r < WIN - SHIFT:
            keep_ref[r] = row
        else:
            send_ref[r - (WIN - SHIFT)] = row


def leave(cells, columns):
    width = cells.shape[1]
    return pl.pallas_call(
        leave_kernel,
        out_shape=[
            jax.ShapeDtypeStruct((WIN - SHIFT, columns, width), bf16),
            jax.ShapeDtypeStruct((SHIFT, columns, width), bf16),
        ],
        scratch_shapes=[
            pltpu.VMEM((columns + 2 * WIN, width), f32),
            pltpu.VMEM(cells.shape, f32),
        ],
        compiler_params=params(),
        cost_estimate=cost(0, 4 * cells.size),
        name="leave",
    )(cells)


def qkv_kernel(stream, x_ref, gain_ref, bias_ref, w_ref, a_ref, out_ref):
    rows, width = x_ref.shape
    block = row_block(rows)
    row = slice(stream, stream + 1)
    ats = [slice(i * block, (i + 1) * block) for i in range(rows // block)]

    @pl.when(pl.program_id(0) == 0)
    def _():
        for at in ats:
            hat, _ = normalised(x_ref[at, :].astype(f32))
            low = (hat * gain_ref[row, :] + bias_ref[row, :]).astype(bf16)
            a_ref[at, :] = low
            out_ref[at, :] = dot_nn(low, w_ref[...]).astype(bf16)

    @pl.when(pl.program_id(0) != 0)
    def _():
        for at in ats:
            out_ref[at, :] = dot_nn(a_ref[at, :], w_ref[...]).astype(bf16)


def norm_qkv(x, gain, bias, weight, stream):
    rows, width = x.shape
    full = weight.shape[-1]
    return pl.pallas_call(
        functools.partial(qkv_kernel, stream),
        grid=(full // width,),
        in_specs=[
            whole((rows, width)),
            whole(gain.shape),
            whole(bias.shape),
            pl.BlockSpec((None, width, width), lambda j: (stream, 0, j)),
        ],
        out_specs=[whole((rows, width)), pl.BlockSpec((rows, width), lambda j: (0, j))],
        out_shape=[
            jax.ShapeDtypeStruct((rows, width), bf16),
            jax.ShapeDtypeStruct((rows, full), bf16),
        ],
        compiler_params=params(),
        cost_estimate=cost(2 * rows * width * full, 2 * rows * (2 * width + full) + 2 * width * full),
        name="norm_qkv",
    )(x, gain, bias, weight)


def first_half(shape):
    return lax.broadcasted_iota(jnp.int32, shape, len(shape) - 1) < PAIR // 2


def stacked(block):
    left = first_half(block.shape)
    zero = jnp.zeros_like(block)
    return jnp.concatenate([jnp.where(left, block, zero), jnp.where(left, zero, block)], 0)


def row_sums(values):
    ones = jnp.ones((8, PAIR), f32)
    return lax.dot_general(
        ones,
        values,
        (((1,), (1,)), ((), ())),
        precision=lax.Precision.HIGHEST,
        preferred_element_type=f32,
    )[:1]


def joined(upright):
    rows = upright.shape[0] // 2
    return jnp.where(first_half((rows, PAIR)), upright[:rows], upright[rows:])


def unstacked(turned):
    return joined(turned.T)


def query_forward_kernel(qq_ref, k_ref, v_ref, ko_ref, vo_ref, bias_ref, out_ref, lse_ref, s_ref):
    queries = qq_ref.shape[0]
    cells = k_ref.shape[0]
    own = ko_ref.shape[0]
    scaled = stacked(qq_ref[...] * 0.125)
    bias = bias_ref[...]
    self_score = dot_nt(ko_ref[...], scaled) + jnp.concatenate([bias, bias], 1)
    top = jnp.max(self_score, 0, keepdims=True)
    block = row_block(cells)
    blocks = [slice(i * block, (i + 1) * block) for i in range(cells // block)]
    for at in blocks:
        score = dot_nt(k_ref[at, :], scaled)
        s_ref[at, :] = score
        top = jnp.maximum(top, jnp.max(score, 0, keepdims=True))
    prob = jnp.exp(self_score - top)
    total = jnp.sum(prob, 0, keepdims=True)
    mixed = dot_nn(vo_ref[...].T, prob.astype(bf16))
    for at in blocks:
        prob = jnp.exp(s_ref[at, :] - top)
        total = total + jnp.sum(prob, 0, keepdims=True)
        mixed = mixed + dot_nn(v_ref[at, :].T, prob.astype(bf16))
    out_ref[...] = unstacked(mixed * (1.0 / total)).astype(bf16)
    lse_ref[...] = top + jnp.log(total)


def query_forward(query_qkv, own_qkv, vis_qkv, self_bias):
    cells = vis_qkv.shape[0]
    queries = query_qkv.shape[0]
    own = own_qkv.shape[0]
    width = query_qkv.shape[1] // 3
    pairs = width // PAIR
    keys = cells + own

    def part(rows, j):
        return pl.BlockSpec((rows, PAIR), lambda p, j=j: (0, j * pairs + p))

    return pl.pallas_call(
        query_forward_kernel,
        grid=(pairs,),
        in_specs=[
            part(queries, 0),
            part(cells, 1),
            part(cells, 2),
            part(own, 1),
            part(own, 2),
            whole(self_bias.shape),
        ],
        out_specs=[part(queries, 0), pl.BlockSpec((None, 1, 2 * queries), lambda p: (p, 0, 0))],
        out_shape=[
            jax.ShapeDtypeStruct((queries, width), bf16),
            jax.ShapeDtypeStruct((pairs, 1, 2 * queries), f32),
        ],
        scratch_shapes=[pltpu.VMEM((cells, 2 * queries), f32)],
        compiler_params=params(),
        cost_estimate=cost(
            4 * 2 * queries * keys * width, 4 * cells * width, 2 * queries * keys * pairs
        ),
        name="query_forward",
    )(query_qkv, vis_qkv, vis_qkv, own_qkv, own_qkv, self_bias)


def window_forward_kernel(
    windows,
    q_ref,
    k_ref,
    v_ref,
    kq_ref,
    vq_ref,
    row_ref,
    col_ref,
    open_ref,
    out_ref,
    lse_ref,
    scaled_ref,
    near_ref,
    mixed_ref,
    far_ref,
):
    cells = [slice(w * CELLS, (w + 1) * CELLS) for w in range(windows)]
    lanes = [slice(2 * w * CELLS, 2 * (w + 1) * CELLS) for w in range(windows)]
    tops = []
    for w in range(windows):
        scaled = stacked(q_ref[cells[w], :] * 0.125)
        scaled_ref[lanes[w], :] = scaled
        near = dot_nt(k_ref[cells[w], :], scaled)
        near = jnp.where(col_ref[w] == row_ref[w], near, MASKED)
        near_ref[w] = near
        tops.append(jnp.max(near, 0, keepdims=True))
    far = dot_nt(kq_ref[...], scaled_ref[...]) + open_ref[...]
    top = jnp.maximum(jnp.concatenate(tops, 1), jnp.max(far, 0, keepdims=True))
    far = jnp.exp(far - top)
    total = jnp.sum(far, 0, keepdims=True)
    far_mixed = dot_nn(vq_ref[...].T, far.astype(bf16))
    totals = []
    for w in range(windows):
        near = jnp.exp(near_ref[w] - top[:, lanes[w]])
        totals.append(jnp.sum(near, 0, keepdims=True))
        mixed_ref[w] = dot_nn(v_ref[cells[w], :].T, near.astype(bf16))
    total = total + jnp.concatenate(totals, 1)
    share = 1.0 / total
    lse_ref[...] = top + jnp.log(total)
    far_ref[...] = far_mixed
    for w in range(windows):
        turned = (mixed_ref[w] + far_ref[:, lanes[w]]) * share[:, lanes[w]]
        out_ref[cells[w], :] = joined(turned.astype(bf16).T)


def window_forward(vis_qkv, query_qkv, region_row, region_col, closed):
    cells = vis_qkv.shape[0]
    queries = query_qkv.shape[0]
    width = vis_qkv.shape[1] // 3
    pairs = width // PAIR
    windows = cells // CELLS

    def part(rows, j):
        return pl.BlockSpec((rows, PAIR), lambda p, j=j: (0, j * pairs + p))

    return pl.pallas_call(
        functools.partial(window_forward_kernel, windows),
        grid=(pairs,),
        in_specs=[
            part(cells, 0),
            part(cells, 1),
            part(cells, 2),
            part(queries, 1),
            part(queries, 2),
            whole(region_row.shape),
            whole(region_col.shape),
            whole(closed.shape),
        ],
        out_specs=[
            part(cells, 0),
            pl.BlockSpec((None, 1, 2 * cells), lambda p: (p, 0, 0)),
        ],
        out_shape=[
            jax.ShapeDtypeStruct((cells, width), bf16),
            jax.ShapeDtypeStruct((pairs, 1, 2 * cells), f32),
        ],
        scratch_shapes=[
            pltpu.VMEM((2 * cells, PAIR), bf16),
            pltpu.VMEM((windows, CELLS, 2 * CELLS), f32),
            pltpu.VMEM((windows, PAIR, 2 * CELLS), f32),
            pltpu.VMEM((PAIR, 2 * cells), f32),
        ],
        compiler_params=params(),
        cost_estimate=cost(
            8 * cells * (CELLS + queries) * width,
            8 * cells * width,
            2 * pairs * cells * (CELLS + queries),
        ),
        name="window_forward",
    )(vis_qkv, vis_qkv, vis_qkv, query_qkv, query_qkv, region_row, region_col, closed)


def attention_backward_kernel(
    windows,
    q_ref,
    k_ref,
    v_ref,
    do_ref,
    qq_ref,
    kq_ref,
    vq_ref,
    doq_ref,
    ko_ref,
    vo_ref,
    row_ref,
    col_ref,
    open_ref,
    bias_ref,
    lse_ref,
    lseq_ref,
    mixq_ref,
    *rest,
):
    if len(rest) > 15:
        rest = rest[3:]
    attention_backward_body(
        windows,
        q_ref,
        k_ref,
        v_ref,
        do_ref,
        qq_ref,
        kq_ref,
        vq_ref,
        doq_ref,
        ko_ref,
        vo_ref,
        row_ref,
        col_ref,
        open_ref,
        bias_ref,
        lse_ref,
        lseq_ref,
        mixq_ref,
        *rest,
    )


def attention_backward_body(
    windows,
    q_ref,
    k_ref,
    v_ref,
    do_ref,
    qq_ref,
    kq_ref,
    vq_ref,
    doq_ref,
    ko_ref,
    vo_ref,
    row_ref,
    col_ref,
    open_ref,
    bias_ref,
    lse_ref,
    lseq_ref,
    mixq_ref,
    dq_ref,
    dk_ref,
    dv_ref,
    dqq_ref,
    dkq_ref,
    dvq_ref,
    dko_ref,
    dvo_ref,
    scaled_ref,
    grad_ref,
    near_ref,
    neart_ref,
    seenk_ref,
    seenv_ref,
    far_ref,
):
    cells = [slice(w * CELLS, (w + 1) * CELLS) for w in range(windows)]
    lanes = [slice(2 * w * CELLS, 2 * (w + 1) * CELLS) for w in range(windows)]
    lse = lse_ref[...]

    deltas = []
    for w in range(windows):
        scaled = stacked(q_ref[cells[w], :] * 0.125)
        grad = stacked(do_ref[cells[w], :])
        scaled_ref[lanes[w], :] = scaled
        grad_ref[lanes[w], :] = grad
        near = dot_nt(k_ref[cells[w], :], scaled)
        near = jnp.exp(jnp.where(col_ref[w] == row_ref[w], near, MASKED) - lse[:, lanes[w]])
        near_t = near * dot_nt(v_ref[cells[w], :], grad)
        near_ref[w] = near
        neart_ref[w] = near_t
        deltas.append(jnp.sum(near_t, 0, keepdims=True))
    kq = kq_ref[...]
    far = jnp.exp(dot_nt(kq, scaled_ref[...]) + open_ref[...] - lse)
    far_t = far * dot_nt(vq_ref[...], grad_ref[...])
    delta = jnp.concatenate(deltas, 1) + jnp.sum(far_t, 0, keepdims=True)
    far_d = (far_t - far * delta).astype(bf16)
    dkq_ref[...] = dot_nn(far_d, scaled_ref[...]).astype(bf16)
    dvq_ref[...] = dot_nn(far.astype(bf16), grad_ref[...]).astype(bf16)
    far_ref[...] = dot_nn(kq.T, far_d).T

    scaled_q = stacked(qq_ref[...] * 0.125)
    grad_q = stacked(doq_ref[...])
    lse_q = lseq_ref[...]
    mix_q = mixq_ref[...]
    delta_q = row_sums(grad_q.astype(f32) * jnp.concatenate([mix_q, mix_q], 0))
    bias = bias_ref[...]
    prob = jnp.exp(dot_nt(ko_ref[...], scaled_q) + jnp.concatenate([bias, bias], 1) - lse_q)
    dscore = (prob * (dot_nt(vo_ref[...], grad_q) - delta_q)).astype(bf16)
    dko_ref[...] = dot_nn(dscore, scaled_q)
    dvo_ref[...] = dot_nn(prob.astype(bf16), grad_q)
    turned = dot_nn(ko_ref[...].T, dscore)
    rows = k_ref.shape[0]
    block = row_block(rows)
    for i in range(rows // block):
        at = slice(i * block, (i + 1) * block)
        k_rows = k_ref[at, :]
        prob = jnp.exp(dot_nt(k_rows, scaled_q) - lse_q)
        dscore = (prob * (dot_nt(v_ref[at, :], grad_q) - delta_q)).astype(bf16)
        seenk_ref[at, :] = dot_nn(dscore, scaled_q)
        seenv_ref[at, :] = dot_nn(prob.astype(bf16), grad_q)
        turned = turned + dot_nn(k_rows.T, dscore)
    dqq_ref[...] = (unstacked(turned) * 0.125).astype(bf16)

    for w in range(windows):
        near = near_ref[w]
        near_d = (neart_ref[w] - near * delta[:, lanes[w]]).astype(bf16)
        upright = dot_nn(k_ref[cells[w], :].T, near_d).T + far_ref[lanes[w], :]
        dq_ref[cells[w], :] = (joined(upright) * 0.125).astype(bf16)
        dk_ref[cells[w], :] = (
            dot_nn(near_d, scaled_ref[lanes[w], :]) + seenk_ref[cells[w], :]
        ).astype(bf16)
        dv_ref[cells[w], :] = (
            dot_nn(near.astype(bf16), grad_ref[lanes[w], :]) + seenv_ref[cells[w], :]
        ).astype(bf16)


def attention_backward(
    vis_qkv,
    query_qkv,
    own_qkv,
    grad,
    grad_q,
    region_row,
    region_col,
    closed,
    self_bias,
    lse,
    lse_q,
    mix_q,
    first,
    count,
    begun=(),
):
    cells = vis_qkv.shape[0]
    queries = query_qkv.shape[0]
    own = own_qkv.shape[0]
    width = vis_qkv.shape[1] // 3
    pairs = width // PAIR
    windows = cells // CELLS

    def part(rows, j):
        return pl.BlockSpec((rows, PAIR), lambda p, j=j: (0, j * pairs + first + p))

    def result(rows):
        return pl.BlockSpec((rows, PAIR), lambda p: (0, p))

    def filled(rows):
        return pl.BlockSpec((rows, PAIR), lambda p: (0, first + p))

    def stats(array):
        return pl.BlockSpec((None,) + array.shape[1:], lambda p: (first + p, 0, 0))

    span = count * PAIR
    return pl.pallas_call(
        functools.partial(attention_backward_kernel, windows),
        grid=(count,),
        in_specs=[
            part(cells, 0),
            part(cells, 1),
            part(cells, 2),
            part(cells, 0),
            part(queries, 0),
            part(queries, 1),
            part(queries, 2),
            part(queries, 0),
            part(own, 1),
            part(own, 2),
            whole(region_row.shape),
            whole(region_col.shape),
            whole(closed.shape),
            whole(self_bias.shape),
            stats(lse),
            stats(lse_q),
            part(queries, 0),
        ]
        + [pl.BlockSpec(memory_space=pl.ANY)] * len(begun),
        out_specs=[filled(cells)] * 3 + [result(queries)] * 3 + [result(own)] * 2,
        out_shape=[jax.ShapeDtypeStruct((cells, width), bf16)] * 3
        + [jax.ShapeDtypeStruct((queries, span), bf16)] * 3
        + [jax.ShapeDtypeStruct((own, span), f32)] * 2,
        scratch_shapes=[
            pltpu.VMEM((2 * cells, PAIR), bf16),
            pltpu.VMEM((2 * cells, PAIR), bf16),
            pltpu.VMEM((windows, CELLS, 2 * CELLS), f32),
            pltpu.VMEM((windows, CELLS, 2 * CELLS), f32),
            pltpu.VMEM((cells, PAIR), f32),
            pltpu.VMEM((cells, PAIR), f32),
            pltpu.VMEM((2 * cells, PAIR), f32),
        ],
        compiler_params=params(),
        cost_estimate=cost(
            20 * cells * (CELLS + 2 * queries) * span,
            14 * cells * span,
            2 * count * cells * (CELLS + 2 * queries),
        ),
        input_output_aliases={17 + i: i for i in range(len(begun))},
        name="attention_backward",
    )(
        vis_qkv,
        vis_qkv,
        vis_qkv,
        grad,
        query_qkv,
        query_qkv,
        query_qkv,
        grad_q,
        own_qkv,
        own_qkv,
        region_row,
        region_col,
        closed,
        self_bias,
        lse,
        lse_q,
        mix_q,
        *begun,
    )


def gelu_pair(z):
    below = 0.5 + 0.5 * lax.erf(z * 0.7071067811865476)
    bell = jnp.exp(-0.5 * z * z)
    return z * below, below + z * bell * 0.3989422804014327


def ffn_forward_kernel(
    stream,
    x_ref,
    o_ref,
    wo_ref,
    bo_ref,
    gain_ref,
    bias_ref,
    wu_ref,
    bu_ref,
    wd_ref,
    bd_ref,
    x1_ref,
    b_ref,
    hid_ref,
    slope_ref,
    out_ref,
    sum_ref,
):
    rows, width = x_ref.shape
    block = row_block(rows)
    count = rows // block
    ats = [slice(i * block, (i + 1) * block) for i in range(count)]
    step = pl.program_id(0)
    row = slice(stream, stream + 1)

    @pl.when(step == 0)
    def _():
        for at in ats:
            x1 = x_ref[at, :].astype(f32) + dot_nn(o_ref[at, :], wo_ref[...]) + bo_ref[row, :]
            x1_ref[at, :] = x1
            hat, _ = normalised(x1)
            b_ref[at, :] = (hat * gain_ref[row, :] + bias_ref[row, :]).astype(bf16)
            sum_ref[at, :] = x1 + bd_ref[row, :]

    def project(i):
        return dot_nn(b_ref[ats[i], :], wu_ref[...]) + bu_ref[row, :]

    z = project(0)
    for i in range(count):
        ahead = project(i + 1) if i + 1 < count else None
        hidden, slope = gelu_pair(z)
        hidden = hidden.astype(bf16)
        hid_ref[ats[i], :] = hidden
        slope_ref[ats[i], :] = slope.astype(bf16)
        sum_ref[ats[i], :] += dot_nn(hidden, wd_ref[...])
        z = ahead

    @pl.when(step == pl.num_programs(0) - 1)
    def _():
        out_ref[...] = sum_ref[...].astype(bf16)


def ffn_forward(x, attended, out_w, out_b, gain, bias, up_w, up_b, down_w, down_b, stream):
    rows, width = x.shape
    hidden = up_w.shape[-1]
    chunk = 768
    return pl.pallas_call(
        functools.partial(ffn_forward_kernel, stream),
        grid=(hidden // chunk,),
        in_specs=[
            whole((rows, width)),
            whole((rows, width)),
            pl.BlockSpec((None, width, width), lambda f: (stream, 0, 0)),
            whole(out_b.shape),
            whole(gain.shape),
            whole(bias.shape),
            pl.BlockSpec((None, width, chunk), lambda f: (stream, 0, f)),
            pl.BlockSpec((2, chunk), lambda f: (0, f)),
            pl.BlockSpec((None, chunk, width), lambda f: (stream, f, 0)),
            whole(down_b.shape),
        ],
        out_specs=[
            whole((rows, width)),
            whole((rows, width)),
            pl.BlockSpec((rows, chunk), lambda f: (0, f)),
            pl.BlockSpec((rows, chunk), lambda f: (0, f)),
            whole((rows, width)),
        ],
        out_shape=[
            jax.ShapeDtypeStruct((rows, width), f32),
            jax.ShapeDtypeStruct((rows, width), bf16),
            jax.ShapeDtypeStruct((rows, hidden), bf16),
            jax.ShapeDtypeStruct((rows, hidden), bf16),
            jax.ShapeDtypeStruct((rows, width), bf16),
        ],
        scratch_shapes=[pltpu.VMEM((rows, width), f32)],
        compiler_params=params(),
        cost_estimate=cost(
            2 * rows * width * (2 * hidden + width),
            4 * width * hidden + 4 * rows * hidden + 12 * rows * width,
            2 * rows * hidden,
        ),
        name="ffn_forward",
    )(x, attended, out_w, out_b, gain, bias, up_w, up_b, down_w, down_b)


def ffn_backward_kernel(
    stream,
    g_ref,
    slope_ref,
    x1_ref,
    wd_ref,
    wu_ref,
    wo_ref,
    gain_ref,
    dz_ref,
    dx1_ref,
    du_ref,
    do_ref,
    sums_ref,
    sum_ref,
):
    rows, width = g_ref.shape
    block = row_block(rows)
    count = rows // block
    ats = [slice(i * block, (i + 1) * block) for i in range(count)]
    step = pl.program_id(0)
    row = slice(stream, stream + 1)

    @pl.when(step == 0)
    def _():
        sum_ref[...] = jnp.zeros_like(sum_ref)

    up_bias = jnp.zeros((1, dz_ref.shape[1]), f32)

    def pulled(i):
        return dot_nt(g_ref[ats[i], :], wd_ref[...])

    grad = pulled(0)
    for i in range(count):
        ahead = pulled(i + 1) if i + 1 < count else None
        dz = grad * slope_ref[ats[i], :].astype(f32)
        low = dz.astype(bf16)
        dz_ref[ats[i], :] = low
        up_bias = up_bias + jnp.sum(dz, 0, keepdims=True)
        sum_ref[ats[i], :] += dot_nt(low, wu_ref[...])
        grad = ahead
    sums_ref[pl.ds(4 + step, 1), :] = up_bias

    @pl.when(step == pl.num_programs(0) - 1)
    def _():
        sums_ref[0:4, :] = jnp.zeros((4, width), f32)
        for at in ats:
            hat, rstd = normalised(x1_ref[at, :])
            db = sum_ref[at, :]
            g = g_ref[at, :].astype(f32)
            dx1 = g + norm_back(db, hat, rstd, gain_ref[row, :])
            dx1_ref[at, :] = dx1
            du = dx1.astype(bf16)
            du_ref[at, :] = du
            do_ref[at, :] = dot_nt(du, wo_ref[...]).astype(bf16)
            sums_ref[0:1, :] += jnp.sum(db * hat, 0, keepdims=True)
            sums_ref[1:2, :] += jnp.sum(db, 0, keepdims=True)
            sums_ref[2:3, :] += jnp.sum(dx1, 0, keepdims=True)
            sums_ref[3:4, :] += jnp.sum(g, 0, keepdims=True)


def ffn_backward(g, slope, x1, down_w, up_w, out_w, gain, stream):
    rows, width = g.shape
    hidden = up_w.shape[-1]
    chunk = width
    return pl.pallas_call(
        functools.partial(ffn_backward_kernel, stream),
        grid=(hidden // chunk,),
        in_specs=[
            whole((rows, width)),
            pl.BlockSpec((rows, chunk), lambda f: (0, f)),
            whole((rows, width)),
            pl.BlockSpec((None, chunk, width), lambda f: (stream, f, 0)),
            pl.BlockSpec((None, width, chunk), lambda f: (stream, 0, f)),
            pl.BlockSpec((None, width, width), lambda f: (stream, 0, 0)),
            whole(gain.shape),
        ],
        out_specs=[
            pl.BlockSpec((rows, chunk), lambda f: (0, f)),
            whole((rows, width)),
            whole((rows, width)),
            whole((rows, width)),
            whole((4 + hidden // chunk, width)),
        ],
        out_shape=[
            jax.ShapeDtypeStruct((rows, hidden), bf16),
            jax.ShapeDtypeStruct((rows, width), f32),
            jax.ShapeDtypeStruct((rows, width), bf16),
            jax.ShapeDtypeStruct((rows, width), bf16),
            jax.ShapeDtypeStruct((4 + hidden // chunk, width), f32),
        ],
        scratch_shapes=[pltpu.VMEM((rows, width), f32)],
        compiler_params=params(),
        cost_estimate=cost(
            2 * rows * width * (2 * hidden + width),
            4 * width * hidden + 4 * rows * hidden + 14 * rows * width,
        ),
        name="ffn_backward",
    )(g, slope, x1, down_w, up_w, out_w, gain)


def input_kernel(stream, dq_ref, dk_ref, dv_ref, w_ref, x_ref, dx1_ref, gain_ref, out_ref, sums_ref):
    width = x_ref.shape[1]

    @pl.when(pl.program_id(0) == 0)
    def _():
        sums_ref[...] = jnp.zeros_like(sums_ref)

    grad = dot_nt(dq_ref[...], w_ref[:, :width])
    grad = grad + dot_nt(dk_ref[...], w_ref[:, width : 2 * width])
    grad = grad + dot_nt(dv_ref[...], w_ref[:, 2 * width :])
    hat, rstd = normalised(x_ref[...].astype(f32))
    out_ref[...] = (
        dx1_ref[...] + norm_back(grad, hat, rstd, gain_ref[stream : stream + 1, :])
    ).astype(bf16)
    sums_ref[0:1, :] += jnp.sum(grad * hat, 0, keepdims=True)
    sums_ref[1:2, :] += jnp.sum(grad, 0, keepdims=True)


def input_grad(dq, dk, dv, weight, x, dx1, gain, stream):
    rows, width = x.shape
    block = row_block(rows)
    rows_spec = pl.BlockSpec((block, width), lambda i: (i, 0))
    return pl.pallas_call(
        functools.partial(input_kernel, stream),
        grid=(rows // block,),
        in_specs=[rows_spec] * 3
        + [
            pl.BlockSpec((None, width, 3 * width), lambda i: (stream, 0, 0)),
            rows_spec,
            rows_spec,
            whole(gain.shape),
        ],
        out_specs=[rows_spec, whole((8, width))],
        out_shape=[
            jax.ShapeDtypeStruct((rows, width), bf16),
            jax.ShapeDtypeStruct((8, width), f32),
        ],
        compiler_params=params(),
        cost_estimate=cost(6 * rows * width * width, 14 * rows * width + 6 * width * width),
        name="input_grad",
    )(dq, dk, dv, weight, x, dx1, gain)


def after(value, *before):
    return lax.optimization_barrier((value,) + before)[0]


def beside(made, *flights):
    return lax.optimization_barrier((made,) + flights)


def moved(block, axis, step):
    size = lax.axis_size(axis)
    return lax.ppermute(block, axis, [(i, (i + step) % size) for i in range(size)])


def swapped(block, axis, mask):
    size = lax.axis_size(axis)
    return lax.ppermute(block, axis, [(i, i ^ mask) for i in range(size)])


def other_core(block):
    return swapped(block, "strip", 1)


def place():
    strip = lax.axis_index("strip")
    return lax.axis_size("strip") // 2, strip // 2, strip % 2


def pick(block, index, axis=0):
    return lax.dynamic_index_in_dim(block, index, axis, keepdims=False)


def added(blocks, kind=bf16):
    total = blocks[0].astype(f32)
    for block in blocks[1:]:
        total = total + block.astype(f32)
    return total.astype(kind)


def bit_of(axis, mask):
    return (lax.axis_index(axis) // mask) % 2


class Phase:
    def __init__(self, blocks, dims, axis, mask):
        bit = bit_of(axis, mask)
        self.mine = [[pick(term, bit, dim) for term in terms] for terms, dim in zip(blocks, dims)]
        theirs = [
            added([pick(term, 1 - bit, dim) for term in terms]) for terms, dim in zip(blocks, dims)
        ]
        self.shapes = [block.shape for block in theirs]
        self.sent, self.got = exchange(theirs, axis, mask)

    def terms(self):
        got = parted(self.got, self.shapes)
        return [[added(mine + [more])] for mine, more in zip(self.mine, got)]


def mapped(change, terms):
    return [change(term) for term in terms]


class Gather:
    def __init__(self, blocks, dims, axis, mask):
        self.bit = bit_of(axis, mask)
        self.blocks, self.dims = blocks, dims
        self.shapes = [block.shape for block in blocks]
        self.sent, self.got = exchange(blocks, axis, mask)

    def pairs(self):
        first = self.bit == 0
        return [
            jnp.stack([jnp.where(first, one, two), jnp.where(first, two, one)], dim)
            for one, two, dim in zip(self.blocks, parted(self.got, self.shapes), self.dims)
        ]


def parted(rows, shapes):
    if len(shapes) == 1:
        return [rows]
    blocks, at = [], 0
    for shape in shapes:
        count = 1
        for size in shape[:-1]:
            count *= size
        blocks.append(rows[at : at + count].reshape(shape))
        at += count
    return blocks


def exchange(blocks, axis, mask):
    if len(blocks) == 1:
        sent = blocks[0]
    else:
        sent = jnp.concatenate([block.reshape(-1, block.shape[-1]) for block in blocks], 0)
    return sent, swapped(sent, axis, mask)


def by_core(grad):
    strips = lax.axis_size("strip")
    return grad.reshape(strips // 2, 2, grad.shape[0] // strips, grad.shape[1])


def tiled(grad, width):
    count = grad.shape[-1] // width
    return jnp.stack([grad[..., i * width : (i + 1) * width] for i in range(count)], -3)


def untiled(blocks):
    return jnp.concatenate([blocks[i] for i in range(blocks.shape[0])], -1)


def by_page(blocks):
    rows = blocks.shape[-2]
    return blocks.reshape(blocks.shape[:-2] + (2, 2, rows // 4, blocks.shape[-1]))


def from_page(blocks):
    return blocks.reshape(blocks.shape[:-4] + (-1, blocks.shape[-1]))


def by_chip(blocks):
    return blocks.reshape((blocks.shape[0] // 2, 2) + blocks.shape[1:])


def line_masks():
    size, _, _ = place()
    return [2 << i for i in range(size.bit_length() - 1)]


def line_phase(blocks, mask):
    return Phase([mapped(by_chip, terms) for terms in blocks], [1] * len(blocks), "strip", mask)


def line_first(blocks):
    masks = line_masks()
    for mask in masks[:-2]:
        blocks = line_phase(blocks, mask).terms()
    return line_phase(blocks, masks[-2])


def line_last(blocks):
    return line_phase(blocks, line_masks()[-1])


def line_exchange(block):
    size, z, _ = place()
    return [pick(block, z)] + [
        moved(pick(block, (z + step) % size), "strip", 2 * step) for step in range(1, size)
    ]


def line_gather(block):
    size, _, _ = place()
    return [block] + [moved(block, "strip", 2 * step) for step in range(1, size)]


def line_order(blocks):
    size, z, _ = place()
    double = jnp.stack(blocks[:1] + blocks[:0:-1] + blocks[:1] + blocks[:0:-1])
    return lax.dynamic_slice_in_dim(double, (size - z) % size, size, 0)


def page_exchange(block):
    size = lax.axis_size("page")
    page = lax.axis_index("page")
    shares = block.reshape(size, block.shape[0] // size, block.shape[1])
    return [pick(shares, page)] + [
        swapped(pick(shares, page ^ mask), "page", mask) for mask in range(1, size)
    ]


def page_gather(block):
    size = lax.axis_size("page")
    return [block] + [swapped(block, "page", mask) for mask in range(1, size)]


def page_order(blocks):
    size = len(blocks)
    page = lax.axis_index("page")
    rows, columns = blocks[0].shape
    joined = jnp.zeros((size * rows, columns), f32)
    for mask, block in enumerate(blocks):
        joined = lax.dynamic_update_slice_in_dim(
            joined, block.astype(f32), (page ^ mask) * rows, 0
        )
    return joined


def core_order(mine, other):
    _, _, core = place()
    pair = jnp.stack(
        [jnp.where(core == 0, mine, other), jnp.where(core == 0, other, mine)], 1
    )
    return pair.reshape(-1, pair.shape[-1])


def packed(mix, lse):
    rows = mix.shape[0]
    pairs = lse.shape[0]
    stats = lse.reshape(pairs, 2, rows).transpose(2, 0, 1).reshape(rows, 2 * pairs)
    stats = jnp.pad(stats, ((0, 0), (0, PAIR - 2 * pairs)))
    return jnp.concatenate([mix.astype(f32), stats], 1)


def merged(blocks):
    width = blocks[0].shape[-1] - PAIR
    lead = blocks[0].shape[:-1]
    tops = [block[..., width : width + HEADS] for block in blocks]
    top = functools.reduce(jnp.maximum, tops)
    shares = [jnp.exp(each - top) for each in tops]
    total = functools.reduce(jnp.add, shares)
    mix = 0.0
    for block, share in zip(blocks, shares):
        heads = block[..., :width].reshape(lead + (HEADS, width // HEADS))
        mix = mix + heads * (share / total)[..., None]
    stats = jnp.pad(top + jnp.log(total), [(0, 0)] * len(lead) + [(0, PAIR - HEADS)])
    return jnp.concatenate([mix.reshape(lead + (width,)), stats], -1)


def region_windows(rows):
    across = rows.shape[1] // WIN
    rolled = jnp.roll(rows, -SHIFT, axis=1)
    return rolled.reshape(WIN, across, WIN).transpose(1, 0, 2).reshape(across, CELLS)


def weight_grad(left, right):
    return dot_tn(left, right).astype(bf16)


def body(
    vis_tokens,
    query_tokens,
    region_ids,
    query_mask,
    answer_len,
    norm1_gain,
    norm1_bias,
    qkv_weight,
    out_weight,
    out_bias,
    norm2_gain,
    norm2_bias,
    up_weight,
    up_bias,
    down_weight,
    down_bias,
    vis_cotangent,
    query_cotangent,
):
    strips = lax.axis_size("strip")
    strip = lax.axis_index("strip")
    chips, z, core = place()
    local_rows, columns, features = vis_tokens.shape[1:]
    own_count = query_tokens.shape[1]
    query_count = query_mask.shape[1]
    total_rows = region_ids.shape[1]
    own_start = strip * own_count

    def own_rows(values):
        return lax.dynamic_slice_in_dim(values, own_start, own_count, 0)

    def own_columns(values):
        span = values.shape[1] // strips
        return lax.dynamic_slice_in_dim(values, strip * span, span, 1)

    tokens = line_gather(query_tokens[0])
    head_rows = moved(vis_tokens[0, :SHIFT], "strip", -1)
    tokens = line_order(tokens)
    query = core_order(tokens, other_core(tokens))

    key_open = query_mask[0] > 0
    key_ids = jnp.arange(query_count, dtype=jnp.int32)
    prompt = key_ids < query_count - answer_len[0]
    closed = jnp.where(key_open & prompt, 0.0, MASKED).astype(f32)[:, None]
    own_ids = own_start + jnp.arange(own_count, dtype=jnp.int32)
    allowed = own_rows(key_open)[:, None] & (
        own_rows(prompt)[:, None] | (own_ids[:, None] <= key_ids[None, :])
    )
    self_bias = jnp.where(allowed, 0.0, MASKED).astype(f32)
    row_ids = (strip * local_rows + SHIFT + jnp.arange(local_rows, dtype=jnp.int32)) % total_rows
    region = region_windows(jnp.take(region_ids[0], row_ids, axis=0))
    region_row = jnp.concatenate([region, region], 1)[:, None, :]
    region_col = region[:, :, None]

    query_norm, query_qkv = norm_qkv(query, norm1_gain, norm1_bias, qkv_weight, 1)
    (query_norm, query_qkv), head_rows = beside((query_norm, query_qkv), head_rows)
    own_qkv = own_rows(query_qkv)
    vis = enter(vis_tokens[0], head_rows)
    head_cot = moved(after(vis_cotangent[0, :SHIFT], vis), "strip", -1)
    vis_norm, vis_qkv = norm_qkv(vis, norm1_gain, norm1_bias, qkv_weight, 0)
    (vis_norm, vis_qkv), head_cot = beside((vis_norm, vis_qkv), head_cot)

    part = by_core(packed(*query_forward(query_qkv, own_qkv, vis_qkv, self_bias)))
    mine, theirs = pick(part, core, 1), pick(part, 1 - core, 1)
    others = other_core(theirs)
    vis_cot = enter(after(vis_cotangent[0], theirs), head_cot)
    vis_cot, mine, others = beside(vis_cot, mine, others)
    part = merged([mine, others])
    others = swapped(part, "strip", 2)

    vis_windows = window_forward(after(vis_qkv, part), query_qkv, region_row, region_col, closed)
    (vis_attn, vis_lse), part, others = beside(vis_windows, part, others)
    part = merged([part, others])
    mask = 4
    while 2 * mask < strips:
        part = merged([part, swapped(part, "strip", mask)])
        mask = 2 * mask
    others = swapped(part, "strip", mask)
    cotangents = line_gather(after(query_cotangent[0], vis_attn))

    weights = (out_weight, out_bias, norm2_gain, norm2_bias, up_weight, up_bias, down_weight, down_bias)
    made = ffn_forward(vis, after(vis_attn, part), *weights, 0)
    made, part, others, cotangents = beside(made, part, others, cotangents)
    vis_x1, vis_b, vis_hid, vis_slope, vis_result = made
    part = merged([part, others])
    others = other_core(part)
    cotangents = line_order(cotangents)
    cot_others = other_core(cotangents)
    vis_down = weight_grad(after(vis_hid, part, cotangents), vis_cot)
    vis_down, part, others, cotangents, cot_others = beside(
        vis_down, part, others, cotangents, cot_others
    )
    down = by_core(vis_down)
    down = Phase([[down.reshape(chips, 2, -1, features // strips, features)]], [1], "strip", 1)

    made = ffn_backward(
        after(vis_cot, down.sent), vis_slope, vis_x1, down_weight, up_weight, out_weight, norm2_gain, 0
    )
    made, down.got = beside(made, down.got)
    vis_dz, vis_dx1, vis_du, vis_do, vis_sums = made
    (down,) = down.terms()
    down = Phase([mapped(by_page, down)], [3], "page", 1)
    vis_up = weight_grad(after(vis_b, down.sent), vis_dz)
    vis_outg = weight_grad(vis_attn, vis_du)
    up = jnp.concatenate(
        [tiled(by_core(vis_up), features), tiled(by_core(vis_outg), features)], 2
    )
    up = Phase([[up]], [1], "strip", 1)
    made = leave(after(vis_result, up.sent), columns)
    (vis_keep, vis_send), up.got = beside(made, up.got)
    vis_first = moved(vis_send, "strip", 1)
    (up,) = up.terms()
    up_a = line_first([mapped(lambda term: term[:, :3], up)])

    every = core_order(part, others)
    query_cot = core_order(cotangents, cot_others)
    query_mix = every[:, :features]
    stats = every[:, features : features + HEADS]
    query_lse = stats.T.reshape(HEADS // 2, 1, 2 * query_count)
    query_attn = query_mix.astype(bf16)
    made = ffn_forward(query, after(query_attn, up_a.sent), *weights, 1)
    made, down.got = beside(made, down.got)
    query_x1, query_b, query_hid, query_slope, query_result = made
    (down,) = down.terms()
    up_b = Phase([mapped(lambda term: by_page(term[:, 3:]), up)], [3], "page", 1)
    made = ffn_backward(
        query_cot,
        after(query_slope, up_b.sent),
        query_x1,
        down_weight,
        up_weight,
        out_weight,
        norm2_gain,
        1,
    )
    made, up_a.got, up_b.got, vis_first = beside(made, up_a.got, up_b.got, vis_first)
    query_dz, query_dx1, query_du, query_do, query_sums = made
    (up_a,) = up_a.terms()
    (up_b,) = up_b.terms()
    up_a = Phase([mapped(by_page, up_a)], [3], "page", 1)
    low = Phase([down, up_b], [2, 2], "page", 2)

    def query_grads(left, right):
        return weight_grad(own_columns(left), right)

    up_rows = features // strips
    one = jnp.concatenate(
        [
            tiled(query_grads(query_b, after(query_dz, up_a.sent, low.sent)), features),
            query_grads(query_attn, query_du)[None],
            query_grads(query_hid, query_cot).reshape(-1, up_rows, features),
        ],
        0,
    )
    one = Phase([[by_page(one)]], [2], "page", 1)

    pairs = HEADS // 2
    half = pairs // 2

    def backward(values, first, begun=()):
        return attention_backward(
            values,
            query_qkv,
            own_qkv,
            vis_do,
            query_do,
            region_row,
            region_col,
            closed,
            self_bias,
            vis_lse,
            query_lse,
            query_mix,
            first,
            half,
            begun,
        )

    def head_grads(normed, grads, first):
        span = half * PAIR
        return jnp.stack(
            [
                by_core(weight_grad(normed, each[:, first * PAIR : first * PAIR + span]))
                for each in grads
            ],
            2,
        )

    back_one = backward(after(vis_qkv, one.sent), 0)
    back_one, up_a.got, low.got = beside(back_one, up_a.got, low.got)
    (up_a,) = up_a.terms()
    low = low.terms()
    up_a = Phase([up_a], [2], "page", 2)
    low = line_first(low)
    first = Phase(
        [[head_grads(after(vis_norm, up_a.sent, low.sent), back_one[:3], 0)]], [1], "strip", 1
    )
    first.sent, one.got = beside(first.sent, one.got)
    (one,) = one.terms()
    one = Phase([one], [1], "page", 2)

    back_two = backward(after(vis_qkv, first.sent, one.sent), half, back_one[:3])
    back_two, first.got, up_a.got, low.got, one.got = beside(
        back_two, first.got, up_a.got, low.got, one.got
    )
    (up_a,) = up_a.terms()
    low = low.terms()
    line = line_last([up_a] + low)
    (one,) = one.terms()
    one_gather = Gather([one[0]], [1], "page", 1)
    part = jnp.stack(
        [by_core(each) for pair in zip(back_one[3:6], back_two[3:6]) for each in pair], 2
    )
    part = Phase([[part]], [1], "strip", 1)
    second = Phase(
        [
            [
                head_grads(
                    after(vis_norm, part.sent, line.sent, one_gather.sent), back_two[:3], half
                )
            ]
        ],
        [1],
        "strip",
        1,
    )
    second.sent, part.got = beside(second.sent, part.got)
    (part,) = part.terms()
    part = line_first([part])
    (first,) = first.terms()
    first = Phase([mapped(by_page, after(first, part.sent))], [3], "page", 1)
    first.sent, second.got = beside(first.sent, second.got)
    (second,) = second.terms()

    made = input_grad(
        after(back_two[0], second, part.sent, first.sent),
        back_two[1],
        back_two[2],
        qkv_weight,
        vis,
        vis_dx1,
        norm1_gain,
        0,
    )
    made, first.got, part.got, line.got, one_gather.got = beside(
        made, first.got, part.got, line.got, one_gather.got
    )
    vis_input, vis_head = made
    (part,) = part.terms()
    part = line_last([part])
    second = Phase([mapped(by_page, after(second, part.sent))], [3], "page", 1)
    one_gather = Gather(one_gather.pairs(), [1], "page", 2)
    all_gather = Gather([terms[0][0] for terms in line.terms()], [1, 1, 1], "page", 1)
    made = leave(after(vis_input, part.sent, second.sent, all_gather.sent), columns)
    made, part.got = beside(made, part.got)
    grad_keep, grad_send = made
    (part,) = part.terms()
    own_self = [jnp.zeros_like(back_one[6])] * 2 + [back_one[6], back_two[6], back_one[7], back_two[7]]
    own_dqkv = added(mapped(lambda term: term[0], part) + [jnp.stack(own_self)])
    masks = line_masks()
    lined = own_dqkv[None]
    for mask in reversed(masks[1:-1]):
        lined = Gather([lined], [1], "strip", mask).pairs()[0]
        lined = lined.reshape((-1,) + own_dqkv.shape)
    lined = Gather([lined], [0], "strip", masks[-1])
    made = input_grad(
        untiled(after(own_dqkv, lined.sent)[0:2]),
        untiled(own_dqkv[2:4]),
        untiled(own_dqkv[4:6]),
        qkv_weight,
        query_tokens[0],
        own_rows(query_dx1),
        norm1_gain,
        1,
    )
    made, lined.got, second.got, all_gather.got = beside(
        made, lined.got, second.got, all_gather.got
    )
    own_input, own_head = made
    lined = lined.pairs()[0].reshape((-1,) + own_dqkv.shape)
    lined = Gather([lined], [1], "strip", masks[0])
    (first,) = first.terms()
    (second,) = second.terms()
    qkv = Phase([first, second], [2, 2], "page", 2)
    up_a, down, up_b = all_gather.pairs()
    up_gather = Gather([up_a, up_b], [1, 1], "page", 2)

    once = jnp.where(strip == 0, 1.0, 0.0)
    small = jnp.concatenate([vis_sums, vis_head, once * query_sums, own_head], 0)
    lined.got, small, one_gather.got = beside(lined.got, small, one_gather.got)
    lined = lined.pairs()[0].reshape((-1,) + own_dqkv.shape)
    lined_others = other_core(lined)
    small_others = other_core(small)
    lined_others, small_others, qkv.got = beside(lined_others, small_others, qkv.got)
    small = small + small_others
    query_dqkv = jnp.stack(
        [jnp.where(core == 0, lined, lined_others), jnp.where(core == 0, lined_others, lined)], 1
    )
    query_dqkv = [query_dqkv[:, :, i].reshape(query_count, -1) for i in range(6)]
    qkv = line_first(qkv.terms())
    three = query_grads(query_norm, jnp.concatenate(query_dqkv, 1))
    three = page_exchange(three)
    for mask in masks[:-2]:
        small = small + swapped(small, "strip", mask)
    small_others = swapped(small, "strip", masks[-2])
    three, qkv.got, small_others, up_gather.got = beside(
        three, qkv.got, small_others, up_gather.got
    )
    three = page_gather(added(three))
    qkv = line_last(qkv.terms())
    small = small + small_others
    small_others = swapped(small, "strip", masks[-1])
    down_gather = Gather([down], [1], "page", 2)
    three, qkv.got, small_others, down_gather.got = beside(
        three, qkv.got, small_others, down_gather.got
    )
    qkv = [terms[0][0] for terms in qkv.terms()]
    late = Gather(qkv, [1, 1], "page", 1)
    small = small + small_others
    small_others = swapped(small, "page", 1)
    grad_first = moved(after(grad_send, late.sent), "strip", 1)
    three = page_order(three)
    late.got, small_others = beside(late.got, small_others)
    late = Gather(late.pairs(), [1, 1], "page", 2)
    small = small + small_others
    small_others = swapped(small, "page", 2)
    small = small + small_others

    up_a, up_b = [from_page(each) for each in up_gather.pairs()]
    (one,) = [from_page(each) for each in one_gather.pairs()]
    (down,) = [from_page(each) for each in down_gather.pairs()]
    hidden = up_weight.shape[-1] // features
    up = jnp.concatenate([up_a, up_b], 0)
    up_grad = jnp.stack([untiled(up[:hidden]), untiled(one[:hidden])]).astype(f32)
    out_grad = jnp.stack([up[hidden], one[hidden]]).astype(f32)
    down_grad = jnp.stack([down, one[hidden + 1 :]]).astype(f32).reshape(2, -1, features)
    first, second = [from_page(each) for each in late.pairs()]
    vis_qkv_grad = jnp.concatenate(
        [each[i] for i in range(3) for each in (first, second)], 1
    )
    qkv_grad = jnp.stack([vis_qkv_grad.astype(f32), three])

    count = vis_sums.shape[0]
    small = small.reshape(2, count + 8, features)
    gain_two, bias_two, obias, dbias = [own_columns(small[:, i]) for i in range(4)]
    gain_one, bias_one = [own_columns(small[:, count + i]) for i in range(2)]
    ubias = own_columns(small[:, 4:count].reshape(2, -1))

    return (
        jnp.concatenate([vis_first, vis_keep], 0)[None],
        own_rows(query_result)[None],
        jnp.concatenate([grad_first, grad_keep], 0)[None],
        own_input[None],
        gain_one,
        bias_one,
        qkv_grad,
        out_grad,
        obias,
        gain_two,
        bias_two,
        up_grad,
        ubias,
        down_grad,
        dbias,
    )


def solution(mesh):
    return jax.shard_map(
        body,
        mesh=mesh,
        in_specs=(
            P("page", "strip", None, None),
            P("page", "strip", None),
            P("page", None, None),
            P("page", None),
            P("page"),
            P(),
            P(),
            P(),
            P(),
            P(),
            P(),
            P(),
            P(),
            P(),
            P(),
            P(),
            P("page", "strip", None, None),
            P("page", "strip", None),
        ),
        out_specs=(
            P("page", "strip", None, None),
            P("page", "strip", None),
            P("page", "strip", None, None),
            P("page", "strip", None),
            P(None, "strip"),
            P(None, "strip"),
            P(None, "strip", None),
            P(None, "strip", None),
            P(None, "strip"),
            P(None, "strip"),
            P(None, "strip"),
            P(None, "strip", None),
            P(None, "strip"),
            P(None, "strip", None),
            P(None, "strip"),
        ),
        check_vma=False,
    )
```

profile of v0, /device:TPU:0, one launch (start us, length us, event | category | flops | bytes accessed | tf_op | source)
XLA Modules:
  0.0 377.7 jit_solution(15949029013322708067)
XLA Ops:
  0.7 5.1 %collective-permute-start = (bf16[32,768]{1,0:T(8,128)(2,1)}, bf16[32,768]{1,0:T(8,128)(2,1)S(1)}, u32[]{:S(2)}, u32[]{:S(2)}) collective-permute-start(bf16[32,768]{1,0:T(8,128)(2,1)} %bitcast.549), channel_id=1, source_target_pairs={{0,6},{1,7},{2,0},{3,1},{4,2},{5,3},{6,4},{7,5},{8,14},{9,15},{10,... | collective-permute-start | bytes 147464 | tf_op jit(solution)/shard_map/ppermute | solution.py:866
  14.3 4.9 %norm_qkv.2 = (bf16[256,768]{1,0:T(8,128)(2,1)}, bf16[256,2304]{1,0:T(8,128)(2,1)}) custom-call(bf16[256,768]{1,0:T(8,128)(2,1)} %bitcast.462, f32[2,768]{1,0:T(2,128)} %gain_ref.15, f32[2,768]{1,0:T(2,128)} %bias_ref.5, bf16[2,768,2304]{2,1,0:T(8,128)(2,1)} %w_ref.7), custom_call_target="tpu_custom_call" | custom-call | flops 45298 | bytes 275 | tf_op jit(solution)/shard_map/norm_qkv/pallas_call | solution.py:160
  20.4 3.5 enter.2.x_ref
  23.9 4.2 %collective-permute-start.5 = (bf16[6,84,768]{2,1,0:T(8,128)(2,1)S(1)}, bf16[6,84,768]{2,1,0:T(8,128)(2,1)S(1)}, u32[]{:S(2)}, u32[]{:S(2)}) collective-permute-start(bf16[6,84,768]{2,1,0:T(8,128)(2,1)S(1)} %slice_bitcast_fusion), channel_id=1, source_target_pairs={{0,7},{1,0},{2,1},{3,2},{4,3},{5,4},{6,5},{7,6},{8,15},{9,8},{10,9... | collective-permute-start | bytes 2322440 | tf_op jit(solution)/shard_map/ppermute | solution.py:866
  28.9 8.4 %norm_qkv.3 = (bf16[1008,768]{1,0:T(8,128)(2,1)}, bf16[1008,2304]{1,0:T(8,128)(2,1)}) custom-call(bf16[1008,768]{1,0:T(8,128)(2,1)} %enter.2.x_ref, f32[2,768]{1,0:T(2,128)} %gain_ref.15, f32[2,768]{1,0:T(2,128)} %bias_ref.5, bf16[2,768,2304]{2,1,0:T(8,128)(2,1)} %w_ref.7), custom_call_target="tpu_custom_call" | custom-call | flops 178362 | bytes 564 | tf_op jit(solution)/shard_map/norm_qkv/pallas_call | solution.py:160
  38.8 10.2 %query_forward.1 = (bf16[256,768]{1,0:T(8,128)(2,1)}, f32[6,1,512]{2,1,0:T(1,128)}) custom-call(bf16[256,2304]{1,0:T(8,128)(2,1)} %get-tuple-element.209.qq_ref.kq_ref.vq_ref, bf16[1008,2304]{1,0:T(8,128)(2,1)} %get-tuple-element.307.k_ref.v_ref.q_ref, bf16[1008,2304]{1,0:T(8,128)(2,1)} %get-tuple-element.307.k_ref.v_ref.q_ref, ...), custom_call_target="tpu_custom_call" | custom-call | flops 81788 | bytes 154 | tf_op jit(solution)/shard_map/query_forward/pallas_call | solution.py:246
  52.4 3.5 enter.3.g_ref
  60.4 13.3 %window_forward.1 = (bf16[1008,768]{1,0:T(8,128)(2,1)}, f32[6,1,2016]{2,1,0:T(1,128)}) custom-call(bf16[1008,2304]{1,0:T(8,128)(2,1)} %get-tuple-element.307.k_ref.v_ref.q_ref, bf16[1008,2304]{1,0:T(8,128)(2,1)} %get-tuple-element.307.k_ref.v_ref.q_ref, bf16[1008,2304]{1,0:T(8,128)(2,1)} %get-tuple-element.307.k_ref.v_ref.q_ref, ...), custom_call_target="tpu_custom_call" | custom-call | flops 123863 | bytes 309 | tf_op jit(solution)/shard_map/window_forward/pallas_call | solution.py:327
  75.2 3.2 collective-permute-start.8
  82.3 19.9 %ffn_forward.2 = (f32[1008,768]{1,0:T(8,128)}, bf16[1008,768]{1,0:T(8,128)(2,1)}, bf16[1008,3072]{1,0:T(8,128)(2,1)}, bf16[1008,3072]{1,0:T(8,128)(2,1)}, bf16[1008,768]{1,0:T(8,128)(2,1)}) custom-call(bf16[1008,768]{1,0:T(8,128)(2,1)} %enter.2.x_ref, bf16[1008,768]{1,0:T(8,128)(2,1)} %get-tuple-element.222.o_ref, bf16[2,768,768]{2,1,0:T(8,128)(2,1)} %wo_ref.7, ...), custom_call_target="tpu_custom_call" | custom-call | flops 535088 | bytes 1555 | tf_op jit(solution)/shard_map/ffn_forward/pallas_call | solution.py:672
  105.5 8.5 %convolution_convert_fusion.1 = bf16[3072,768]{1,0:T(8,128)(2,1)S(1)} fusion(bf16[1008,3072]{1,0:T(8,128)(2,1)} %get-tuple-element.236, bf16[1008,768]{1,0:T(8,128)(2,1)S(1)} %copy-done.7), kind=kOutput, calls=%fused_computation.4 | convolution fusion | flops 4758700032 | bytes 12460032 | tf_op jit(solution)/shard_map/dot_general | solution.py:42
  117.0 21.6 %ffn_backward.2 = (bf16[1008,3072]{1,0:T(8,128)(2,1)}, f32[1008,768]{1,0:T(8,128)}, bf16[1008,768]{1,0:T(8,128)(2,1)}, bf16[1008,768]{1,0:T(8,128)(2,1)}, f32[8,768]{1,0:T(8,128)}) custom-call(bf16[1008,768]{1,0:T(8,128)(2,1)} %enter.3.g_ref, bf16[1008,3072]{1,0:T(8,128)(2,1)} %get-tuple-element.245.slope_ref, f32[1008,768]{1,0:T(8,128)} %get-tuple-element.246.x1_ref, ...), custom_call_target="tpu_custom_call" | custom-call | flops 535088 | bytes 1633 | tf_op jit(solution)/shard_map/ffn_backward/pallas_call | solution.py:777
  140.0 3.2 fusion.1
  145.3 5.6 %convolution_convert_fusion = bf16[768,3072]{1,0:T(8,128)(2,1)S(1)} fusion(bf16[1008,768]{1,0:T(8,128)(2,1)S(1)} %copy-done.53, bf16[1008,3072]{1,0:T(8,128)(2,1)S(1)} %copy-done.50), kind=kOutput, calls=%fused_computation.3 | convolution fusion | flops 4758700032 | bytes 12460032 | tf_op jit(solution)/shard_map/dot_general | solution.py:42
  166.7 3.1 leave.2
  169.8 3.7 fusion
  176.0 9.7 %ffn_forward.3 = (f32[256,768]{1,0:T(8,128)}, bf16[256,768]{1,0:T(8,128)(2,1)}, bf16[256,3072]{1,0:T(8,128)(2,1)}, bf16[256,3072]{1,0:T(8,128)(2,1)}, bf16[256,768]{1,0:T(8,128)(2,1)}) custom-call(bf16[256,768]{1,0:T(8,128)(2,1)} %bitcast.463, bf16[256,768]{1,0:T(8,128)(2,1)} %slice.655.o_ref, bf16[2,768,768]{2,1,0:T(8,128)(2,1)} %wo_ref.7, ...), custom_call_target="tpu_custom_call" | custom-call | flops 135895 | bytes 747 | tf_op jit(solution)/shard_map/ffn_forward/pallas_call | solution.py:672
  185.7 2.6 collective-permute-done.16
  190.6 10.6 %ffn_backward.3 = (bf16[256,3072]{1,0:T(8,128)(2,1)}, f32[256,768]{1,0:T(8,128)}, bf16[256,768]{1,0:T(8,128)(2,1)}, bf16[256,768]{1,0:T(8,128)(2,1)}, f32[8,768]{1,0:T(8,128)}) custom-call(bf16[256,768]{1,0:T(8,128)(2,1)} %bitcast.470, bf16[256,3072]{1,0:T(8,128)(2,1)} %get-tuple-element.268.slope_ref, f32[256,768]{1,0:T(8,128)} %get-tuple-element.269.x1_ref, ...), custom_call_target="tpu_custom_call" | custom-call | flops 135895 | bytes 766 | tf_op jit(solution)/shard_map/ffn_backward/pallas_call | solution.py:777
  217.5 17.3 %attention_backward.2 = (bf16[1008,768]{1,0:T(8,128)(2,1)}, bf16[1008,768]{1,0:T(8,128)(2,1)}, bf16[1008,768]{1,0:T(8,128)(2,1)}, bf16[256,384]{1,0:T(8,128)(2,1...) custom-call(bf16[1008,2304]{1,0:T(8,128)(2,1)} %get-tuple-element.307.k_ref.v_re, ...), custom_call_target="tpu_custom_call" | custom-call | flops 253919 | bytes 270 | tf_op jit(solution)/shard_map/attention_backward/pallas_call | solution.py:543
  236.3 2.5 maximum_bitcast_fusion
  250.5 17.4 %attention_backward.3 = (bf16[1008,768]{1,0:T(8,128)(2,1)}, bf16[1008,768]{1,0:T(8,128)(2,1)}, bf16[1008,768]{1,0:T(8,128)(2,1)}, bf16[256,384]{1,0:T(8,128)(2,1...) custom-call(bf16[1008,2304]{1,0:T(8,128)(2,1)} %get-tuple-element.30, ...), custom_call_target="tpu_custom_call", output_to_operand_aliasing={{0}: (17, {}), {1}: (18, {}), {2}: (19, {})} | custom-call | flops 253919 | bytes 270 | tf_op jit(solution)/shard_map/attention_backward/pallas_call | solution.py:543
  282.9 9.9 %input_grad.2 = (bf16[1008,768]{1,0:T(8,128)(2,1)}, f32[8,768]{1,0:T(8,128)}) custom-call(bf16[1008,768]{1,0:T(8,128)(2,1)} %get-tuple-element.333.dq_ref, bf16[1008,768]{1,0:T(8,128)(2,1)} %get-tuple-element.327.dk_ref, bf16[1008,768]{1,0:T(8,128)(2,1)} %get-tuple-element.328.dv_ref, bf16[2,768,2304]{2,1,0:T(8,128)(2,1)} %w_ref.7, ...), custom_call_target="tpu_custom_call" | custom-call | flops 178362 | bytes 718 | tf_op jit(solution)/shard_map/input_grad/pallas_call | solution.py:835
  292.8 2.6 collective-permute-done.30
  298.2 3.1 leave.3
  307.1 3.9 %input_grad.3 = (bf16[32,768]{1,0:T(8,128)(2,1)}, f32[8,768]{1,0:T(8,128)}) custom-call(bf16[32,768]{1,0:T(8,128)(2,1)} %pad_maximum_fusion.40.dq_ref, bf16[32,768]{1,0:T(8,128)(2,1)} %pad_maximum_fusion.41.dk_ref, bf16[32,768]{1,0:T(8,128)(2,1)} %pad_maximum_fusion.42.dv_ref, bf16[2,768,2304]{2,1,0:T(8,128)(2,1)} %w_ref.7, bf16[32,768]{1,0:T(8,128)(2,1)} %bitcast.552, ...), custom_call_target="tpu_custom_call" | custom-call | flops 5662 | bytes 194 | tf_op jit(solution)/shard_map/input_grad/pallas_call | solution.py:835
  319.4 2.7 collective-permute-done.37
  324.5 5.6 %collective-permute-done.41 = bf16[576,384]{1,0:T(8,128)(2,1)S(1)} collective-permute-done((bf16[576,384]{1,0:T(8,128)(2,1)S(1)}, bf16[576,384]{1,0:T(8,128)(2,1)S(1)}, u32[]{:S(2)}, u32[]{:S(2)}) %collective-permute-start.41) | collective-permute-done | bytes 442400 | tf_op jit(solution)/shard_map/ppermute | solution.py:871
  338.8 2.8 collective-permute-done.46
  352.6 4.0 %collective-permute-done.52 = f32[32,768]{1,0:T(8,128)S(1)} collective-permute-done((f32[32,768]{1,0:T(8,128)S(1)}, f32[32,768]{1,0:T(8,128)S(1)}, u32[]{:S(2)}, u32[]{:S(2)}) %collective-permute-start.52) | collective-permute-done | bytes 98336 | tf_op jit(solution)/shard_map/ppermute | solution.py:871
  361.1 3.0 collective-permute-done.56
  366.4 3.5 collective-permute-done.57
  (533 shorter events, 150.9 us)
Async XLA Ops:
  23.9 14.9 %collective-permute-start.5 = (bf16[6,84,768]{2,1,0:T(8,128)(2,1)S(1)}, bf16[6,84,768]{2,1,0:T(8,128)(2,1)S(1)}, u32[]{:S(2)}, u32[]{:S(2)}) collective-permute-start(bf16[6,84,768]{2,1,0:T(8,128)(2,1)S(1)} %slice_bitcast_fusion), channel_id=1, source_target_pairs={{0,7},{1,0},{2,1},{3,2},{4,3},{5,4},{6,5},{7,6},{8,15},{9,8},{10,9... | collective-permute-start | bytes 2322440 | tf_op jit(solution)/shard_map/ppermute | solution.py:866
  57.4 16.3 %collective-permute-start.7 = (f32[4,32,896]{2,1,0:T(8,128)S(1)}, f32[4,32,896]{2,1,0:T(8,128)S(1)}, u32[]{:S(2)}, u32[]{:S(2)}) collective-permute-start(f32[4,32,896]{2,1,0:T(8,128)S(1)} %select_maximum_fusion.3), channel_id=1, source_target_pairs={{0,2},{1,3},{2,0},{3,1},{4,6},{5,7},{6,4},{7,5},{8,10},{9,11},{10,... | collective-permute-start | bytes 1376264 | tf_op jit(solution)/shard_map/ppermute | solution.py:871
  75.2 27.5 %collective-permute-start.8 = (f32[4,32,896]{2,1,0:T(8,128)S(1)}, f32[4,32,896]{2,1,0:T(8,128)S(1)}, u32[]{:S(2)}, u32[]{:S(2)}) collective-permute-start(f32[4,32,896]{2,1,0:T(8,128)S(1)} %select_maximum_fusion.2), channel_id=1, source_target_pairs={{0,4},{1,5},{2,6},{3,7},{4,0},{5,1},{6,2},{7,3},{8,12},{9,13},{10,... | collective-permute-start | bytes 1376264 | tf_op jit(solution)/shard_map/ppermute | solution.py:871
  78.3 23.9 %collective-permute-start.9 = (bf16[32,768]{1,0:T(8,128)(2,1)S(1)}, bf16[32,768]{1,0:T(8,128)(2,1)S(1)}, u32[]{:S(2)}, u32[]{:S(2)}) collective-permute-start(bf16[32,768]{1,0:T(8,128)(2,1)S(1)} %bitcast.587), channel_id=1, source_target_pairs={{0,2},{1,3},{2,4},{3,5},{4,6},{5,7},{6,0},{7,1},{8,10},{9,11},{10,... | collective-permute-start | bytes 147464 | tf_op jit(solution)/shard_map/ppermute | solution.py:866
  78.4 24.3 %collective-permute-start.10 = (bf16[32,768]{1,0:T(8,128)(2,1)S(1)}, bf16[32,768]{1,0:T(8,128)(2,1)S(1)}, u32[]{:S(2)}, u32[]{:S(2)}) collective-permute-start(bf16[32,768]{1,0:T(8,128)(2,1)S(1)} %bitcast.588), channel_id=1, source_target_pairs={{0,4},{1,5},{2,6},{3,7},{4,0},{5,1},{6,2},{7,3},{8,12},{9,13},{10,... | collective-permute-start | bytes 147464 | tf_op jit(solution)/shard_map/ppermute | solution.py:866
  80.2 22.5 %collective-permute-start.11 = (bf16[32,768]{1,0:T(8,128)(2,1)S(1)}, bf16[32,768]{1,0:T(8,128)(2,1)S(1)}, u32[]{:S(2)}, u32[]{:S(2)}) collective-permute-start(bf16[32,768]{1,0:T(8,128)(2,1)S(1)} %bitcast.589), channel_id=1, source_target_pairs={{0,6},{1,7},{2,0},{3,1},{4,2},{5,3},{6,4},{7,5},{8,14},{9,15},{10,... | collective-permute-start | bytes 147464 | tf_op jit(solution)/shard_map/ppermute | solution.py:866
  117.0 21.6 %collective-permute-start.14 = (bf16[4,4,96,768]{3,2,1,0:T(8,128)(2,1)}, bf16[4,4,96,768]{3,2,1,0:T(8,128)(2,1)S(1)}, u32[]{:S(2)}, u32[]{:S(2)}) collective-permute-start(bf16[4,4,96,768]{3,2,1,0:T(8,128)(2,1)} %dynamic-slice_bitcast_fusion.1), channel_id=1, source_target_pairs={{0,1},{1,0},{2,3},{3,2},{4,5},{5,4},{6,7},{7,6},{8,9},{9,8},{10,11... | collective-permute-start | bytes 7077896 | tf_op jit(solution)/shard_map/ppermute | solution.py:871
  158.2 11.6 %collective-permute-start.15 = (bf16[4,5,96,768]{3,2,1,0:T(8,128)(2,1)}, bf16[4,5,96,768]{3,2,1,0:T(8,128)(2,1)}, u32[]{:S(2)}, u32[]{:S(2)}) collective-permute-start(bf16[4,5,96,768]{3,2,1,0:T(8,128)(2,1)} %dynamic-slice_bitcast_fusion), channel_id=1, source_target_pairs={{0,1},{1,0},{2,3},{3,2},{4,5},{5,4},{6,7},{7,6},{8,9},{9,8},{10,11... | collective-permute-start | bytes 8847368 | tf_op jit(solution)/shard_map/ppermute | solution.py:871
  160.1 28.2 %collective-permute-start.16 = (bf16[4,4,2,24,768]{4,3,2,1,0:T(8,128)(2,1)}, bf16[4,4,2,24,768]{4,3,2,1,0:T(8,128)(2,1)S(1)}, u32[]{:S(2)}, u32[]{:S(2)}) collective-permute-start(bf16[4,4,2,24,768]{4,3,2,1,0:T(8,128)(2,1)} %dynamic-slice_bitcast_fusion.2), channel_id=1, source_target_pairs={{0,8},{8,0},{16,24},{24,16},{1,9},{9,1},{17,25},{25,17},{2,10},{10... | collective-permute-start | bytes 3538952 | tf_op jit(solution)/shard_map/ppermute | solution.py:871
  174.7 31.7 %collective-permute-start.17 = (bf16[2,3,96,768]{3,2,1,0:T(8,128)(2,1)}, bf16[2,3,96,768]{3,2,1,0:T(8,128)(2,1)S(1)}, u32[]{:S(2)}, u32[]{:S(2)}) collective-permute-start(bf16[2,3,96,768]{3,2,1,0:T(8,128)(2,1)} %dynamic-slice_bitcast_fusion.3), channel_id=1, source_target_pairs={{0,2},{1,3},{2,0},{3,1},{4,6},{5,7},{6,4},{7,5},{8,10},{9,11},{10,... | collective-permute-start | bytes 2654216 | tf_op jit(solution)/shard_map/ppermute | solution.py:871
  189.1 16.1 %collective-permute-start.18 = (bf16[4,2,2,24,768]{4,3,2,1,0:T(8,128)(2,1)}, bf16[4,2,2,24,768]{4,3,2,1,0:T(8,128)(2,1)}, u32[]{:S(2)}, u32[]{:S(2)}) collective-permute-start(bf16[4,2,2,24,768]{4,3,2,1,0:T(8,128)(2,1)} %dynamic-slice_bitcast_fusion.5), channel_id=1, source_target_pairs={{0,8},{8,0},{16,24},{24,16},{1,9},{9,1},{17,25},{25,17},{2,10},{10... | collective-permute-start | bytes 1769480 | tf_op jit(solution)/shard_map/ppermute | solution.py:871
  190.6 15.8 %collective-permute-start.19 = (bf16[6,84,768]{2,1,0:T(8,128)(2,1)}, bf16[6,84,768]{2,1,0:T(8,128)(2,1)}, u32[]{:S(2)}, u32[]{:S(2)}) collective-permute-start(bf16[6,84,768]{2,1,0:T(8,128)(2,1)} %get-tuple-element.275), channel_id=1, source_target_pairs={{0,1},{1,2},{2,3},{3,4},{4,5},{5,6},{6,7},{7,0},{8,9},{9,10},{10,1... | collective-permute-start | bytes 2322440 | tf_op jit(solution)/shard_map/ppermute | solution.py:866
  210.8 28.6 %collective-permute-start.20 = (bf16[2,3,2,24,768]{4,3,2,1,0:T(8,128)(2,1)}, bf16[2,3,2,24,768]{4,3,2,1,0:T(8,128)(2,1)}, u32[]{:S(2)}, u32[]{:S(2)}) collective-permute-start(bf16[2,3,2,24,768]{4,3,2,1,0:T(8,128)(2,1)} %dynamic-slice_bitcast_fusion.10), channel_id=1, source_target_pairs={{0,8},{8,0},{16,24},{24,16},{1,9},{9,1},{17,25},{25,17},{2,10},{10... | collective-permute-start | bytes 1327112 | tf_op jit(solution)/shard_map/ppermute | solution.py:871
  211.5 27.9 %collective-permute-start.21 = (bf16[576,768]{1,0:T(8,128)(2,1)S(1)}, bf16[576,768]{1,0:T(8,128)(2,1)S(1)}, u32[]{:S(2)}, u32[]{:S(2)}) collective-permute-start(bf16[576,768]{1,0:T(8,128)(2,1)S(1)} %pad_maximum_fusion.4), channel_id=1, source_target_pairs={{0,16},{8,24},{16,0},{24,8},{1,17},{9,25},{17,1},{25,9},{2,18},{10... | collective-permute-start | bytes 2654216 | tf_op jit(solution)/shard_map/ppermute | solution.py:871
  215.9 32.9 %collective-permute-start.22 = (bf16[9,2,24,768]{3,2,1,0:T(8,128)(2,1)S(1)}, bf16[9,2,24,768]{3,2,1,0:T(8,128)(2,1)S(1)}, u32[]{:S(2)}, u32[]{:S(2)}) collective-permute-start(bf16[9,2,24,768]{3,2,1,0:T(8,128)(2,1)S(1)} %dynamic-slice_bitcast_fusion.4), channel_id=1, source_target_pairs={{0,8},{8,0},{16,24},{24,16},{1,9},{9,1},{17,25},{25,17},{2,10},{10... | collective-permute-start | bytes 1990664 | tf_op jit(solution)/shard_map/ppermute | solution.py:871
  242.8 25.2 %collective-permute-start.24 = (bf16[2,3,24,768]{3,2,1,0:T(8,128)(2,1)}, bf16[2,3,24,768]{3,2,1,0:T(8,128)(2,1)}, u32[]{:S(2)}, u32[]{:S(2)}) collective-permute-start(bf16[2,3,24,768]{3,2,1,0:T(8,128)(2,1)} %dynamic-slice_bitcast_fusion.13), channel_id=1, source_target_pairs={{0,16},{8,24},{16,0},{24,8},{1,17},{9,25},{17,1},{25,9},{2,18},{10... | collective-permute-start | bytes 663560 | tf_op jit(solution)/shard_map/ppermute | solution.py:871
  244.2 23.9 %collective-permute-start.25 = (bf16[288,768]{1,0:T(8,128)(2,1)}, bf16[288,768]{1,0:T(8,128)(2,1)S(1)}, u32[]{:S(2)}, u32[]{:S(2)}) collective-permute-start(bf16[288,768]{1,0:T(8,128)(2,1)} %pad_maximum_fusion.9), channel_id=1, source_target_pairs={{0,2},{1,3},{2,0},{3,1},{4,6},{5,7},{6,4},{7,5},{8,10},{9,11},{10,... | collective-permute-start | bytes 1327112 | tf_op jit(solution)/shard_map/ppermute | solution.py:871
  248.7 19.4 %collective-permute-start.23 = (bf16[4,3,96,384]{3,2,1,0:T(8,128)(2,1)S(1)}, bf16[4,3,96,384]{3,2,1,0:T(8,128)(2,1)S(1)}, u32[]{:S(2)}, u32[]{:S(2)}) collective-permute-start(bf16[4,3,96,384]{3,2,1,0:T(8,128)(2,1)S(1)} %bitcast.494), channel_id=1, source_target_pairs={{0,1},{1,0},{2,3},{3,2},{4,5},{5,4},{6,7},{7,6},{8,9},{9,8},{10,11... | collective-permute-start | bytes 2654216 | tf_op jit(solution)/shard_map/ppermute | solution.py:871
  249.0 19.0 %collective-permute-start.26 = (bf16[9,24,768]{2,1,0:T(8,128)(2,1)S(1)}, bf16[9,24,768]{2,1,0:T(8,128)(2,1)S(1)}, u32[]{:S(2)}, u32[]{:S(2)}) collective-permute-start(bf16[9,24,768]{2,1,0:T(8,128)(2,1)S(1)} %dynamic-slice_bitcast_fusion.11), channel_id=1, source_target_pairs={{0,16},{8,24},{16,0},{24,8},{1,17},{9,25},{17,1},{25,9},{2,18},{10... | collective-permute-start | bytes 995336 | tf_op jit(solution)/shard_map/ppermute | solution.py:871
  272.4 20.3 %collective-permute-start.31 = (bf16[216,768]{1,0:T(8,128)(2,1)S(1)}, bf16[216,768]{1,0:T(8,128)(2,1)S(1)}, u32[]{:S(2)}, u32[]{:S(2)}) collective-permute-start(bf16[216,768]{1,0:T(8,128)(2,1)S(1)} %pad_maximum_fusion.14), channel_id=1, source_target_pairs={{0,4},{1,5},{2,6},{3,7},{4,0},{5,1},{6,2},{7,3},{8,12},{9,13},{10,... | collective-permute-start | bytes 995336 | tf_op jit(solution)/shard_map/ppermute | solution.py:871
  274.7 18.1 %collective-permute-start.32 = (bf16[9,24,768]{2,1,0:T(8,128)(2,1)S(1)}, bf16[9,24,768]{2,1,0:T(8,128)(2,1)S(1)}, u32[]{:S(2)}, u32[]{:S(2)}) collective-permute-start(bf16[9,24,768]{2,1,0:T(8,128)(2,1)S(1)} %fusion.23), channel_id=1, source_target_pairs={{0,8},{8,0},{16,24},{24,16},{1,9},{9,1},{17,25},{25,17},{2,10},{10... | collective-permute-start | bytes 995336 | tf_op jit(solution)/shard_map/ppermute | solution.py:871
  280.6 14.8 %collective-permute-start.30 = (bf16[2,6,32,384]{3,2,1,0:T(8,128)(2,1)S(1)}, bf16[2,6,32,384]{3,2,1,0:T(8,128)(2,1)S(1)}, u32[]{:S(2)}, u32[]{:S(2)}) collective-permute-start(bf16[2,6,32,384]{3,2,1,0:T(8,128)(2,1)S(1)} %dynamic-slice_bitcast_fusion.12), channel_id=1, source_target_pairs={{0,2},{1,3},{2,0},{3,1},{4,6},{5,7},{6,4},{7,5},{8,10},{9,11},{10,... | collective-permute-start | bytes 884744 | tf_op jit(solution)/shard_map/ppermute | solution.py:871
  281.2 14.2 %collective-permute-start.29 = (bf16[4,3,2,24,384]{4,3,2,1,0:T(8,128)(2,1)S(1)}, bf16[4,3,2,24,384]{4,3,2,1,0:T(8,128)(2,1)S(1)}, u32[]{:S(2)}, u32[]{:S(2)}) collective-permute-start(bf16[4,3,2,24,384]{4,3,2,1,0:T(8,128)(2,1)S(1)} %dynamic-slice_bitcast_fusion.9), channel_id=1, source_target_pairs={{0,8},{8,0},{16,24},{24,16},{1,9},{9,1},{17,25},{25,17},{2,10},{10... | collective-permute-start | bytes 1327112 | tf_op jit(solution)/shard_map/ppermute | solution.py:871
  296.0 18.2 %collective-permute-start.35 = (bf16[4,3,2,24,384]{4,3,2,1,0:T(8,128)(2,1)S(1)}, bf16[4,3,2,24,384]{4,3,2,1,0:T(8,128)(2,1)S(1)}, u32[]{:S(2)}, u32[]{:S(2)}) collective-permute-start(bf16[4,3,2,24,384]{4,3,2,1,0:T(8,128)(2,1)S(1)} %dynamic-slice_bitcast_fusion.8), channel_id=1, source_target_pairs={{0,8},{8,0},{16,24},{24,16},{1,9},{9,1},{17,25},{25,17},{2,10},{10... | collective-permute-start | bytes 1327112 | tf_op jit(solution)/shard_map/ppermute | solution.py:871
  297.6 16.7 %collective-permute-start.36 = (bf16[216,768]{1,0:T(8,128)(2,1)S(1)}, bf16[216,768]{1,0:T(8,128)(2,1)S(1)}, u32[]{:S(2)}, u32[]{:S(2)}) collective-permute-start(bf16[216,768]{1,0:T(8,128)(2,1)S(1)} %pad_maximum_fusion.15), channel_id=1, source_target_pairs={{0,8},{8,0},{16,24},{24,16},{1,9},{9,1},{17,25},{25,17},{2,10},{10... | collective-permute-start | bytes 995336 | tf_op jit(solution)/shard_map/ppermute | solution.py:871
  301.4 18.0 %collective-permute-start.38 = (bf16[9,2,24,768]{3,2,0,1:T(8,128)(2,1)S(1)}, bf16[9,2,24,768]{3,2,0,1:T(8,128)(2,1)S(1)}, u32[]{:S(2)}, u32[]{:S(2)}) collective-permute-start(bf16[9,2,24,768]{3,2,0,1:T(8,128)(2,1)S(1)} %pad_maximum_fusion.5), channel_id=1, source_target_pairs={{0,16},{8,24},{16,0},{24,8},{1,17},{9,25},{17,1},{25,9},{2,18},{10... | collective-permute-start | bytes 1990664 | tf_op jit(solution)/shard_map/ppermute | solution.py:871
  317.0 13.2 %collective-permute-start.41 = (bf16[576,384]{1,0:T(8,128)(2,1)S(1)}, bf16[576,384]{1,0:T(8,128)(2,1)S(1)}, u32[]{:S(2)}, u32[]{:S(2)}) collective-permute-start(bf16[576,384]{1,0:T(8,128)(2,1)S(1)} %pad_maximum_fusion.10), channel_id=1, source_target_pairs={{0,16},{8,24},{16,0},{24,8},{1,17},{9,25},{17,1},{25,9},{2,18},{10... | collective-permute-start | bytes 1327112 | tf_op jit(solution)/shard_map/ppermute | solution.py:871
  318.2 18.7 %collective-permute-start.47 = (bf16[240,768]{1,0:T(8,128)(2,1)S(1)}, bf16[240,768]{1,0:T(8,128)(2,1)S(1)}, u32[]{:S(2)}, u32[]{:S(2)}) collective-permute-start(bf16[240,768]{1,0:T(8,128)(2,1)S(1)} %pad_maximum_fusion.13), channel_id=1, source_target_pairs={{0,16},{8,24},{16,0},{24,8},{1,17},{9,25},{17,1},{25,9},{2,18},{10... | collective-permute-start | bytes 1105928 | tf_op jit(solution)/shard_map/ppermute | solution.py:871
  330.9 12.0 %collective-permute-start.45 = (bf16[288,384]{1,0:T(8,128)(2,1)S(1)}, bf16[288,384]{1,0:T(8,128)(2,1)S(1)}, u32[]{:S(2)}, u32[]{:S(2)}) collective-permute-start(bf16[288,384]{1,0:T(8,128)(2,1)S(1)} %pad_maximum_fusion.17), channel_id=1, source_target_pairs={{0,2},{1,3},{2,0},{3,1},{4,6},{5,7},{6,4},{7,5},{8,10},{9,11},{10,... | collective-permute-start | bytes 663560 | tf_op jit(solution)/shard_map/ppermute | solution.py:871
  343.1 13.6 %collective-permute-start.48 = (bf16[24,2304]{1,0:T(8,128)(2,1)S(1)}, bf16[24,2304]{1,0:T(8,128)(2,1)S(1)}, u32[]{:S(2)}, u32[]{:S(2)}) collective-permute-start(bf16[24,2304]{1,0:T(8,128)(2,1)S(1)} %add_convert_fusion.1), channel_id=1, source_target_pairs={{0,8},{8,0},{16,24},{24,16},{1,9},{9,1},{17,25},{25,17},{2,10},{10... | collective-permute-start | bytes 331784 | tf_op jit(solution)/shard_map/ppermute | solution.py:871
  344.6 12.0 %collective-permute-start.49 = (bf16[24,2304]{1,0:T(8,128)(2,1)S(1)}, bf16[24,2304]{1,0:T(8,128)(2,1)S(1)}, u32[]{:S(2)}, u32[]{:S(2)}) collective-permute-start(bf16[24,2304]{1,0:T(8,128)(2,1)S(1)} %add_convert_fusion.1), channel_id=1, source_target_pairs={{0,16},{8,24},{16,0},{24,8},{1,17},{9,25},{17,1},{25,9},{2,18},{10... | collective-permute-start | bytes 331784 | tf_op jit(solution)/shard_map/ppermute | solution.py:871
  359.0 17.1 %collective-permute-start.54 = (bf16[6,84,768]{2,1,0:T(8,128)(2,1)S(1)}, bf16[6,84,768]{2,1,0:T(8,128)(2,1)S(1)}, u32[]{:S(2)}, u32[]{:S(2)}) collective-permute-start(bf16[6,84,768]{2,1,0:T(8,128)(2,1)S(1)} %copy-done.55), channel_id=1, source_target_pairs={{0,1},{1,2},{2,3},{3,4},{4,5},{5,6},{6,7},{7,0},{8,9},{9,10},{10,1... | collective-permute-start | bytes 2322440 | tf_op jit(solution)/shard_map/ppermute | solution.py:866
  (88 other events, 418.4 us)
where the time goes:
time: 382 us; the launch traced here: 378 us
  Pallas kernels  160 us (42%)
  starting transfers between devices  63.5 us (17%)
  local copies, waits for them, and re-layouts  51.7 us (14%)
  waiting for transfers between devices  38.1 us (10%)
  other arithmetic  33.6 us (9%)
  matrix products  26.8 us (7%)
  between operations  4.01 us (1%)
    ppermute x49, starting transfers between devices, swapped(): return lax.ppermute(block, axis, [(i, i ^ mask) for i in range(size)])  47.5 us
    ppermute x49, waiting for transfers between devices, swapped(): return lax.ppermute(block, axis, [(i, i ^ mask) for i in range(size)])  35 us
    pallas_call x2, Pallas kernels, attention_backward(): pl.pallas_call(functools.partial(attention_backward_kernel, windows), gri...  34.7 us
    pallas_call x2, Pallas kernels, ffn_backward(): pl.pallas_call(functools.partial(ffn_backward_kernel, stream), grid=(hidd...  32.2 us
    pallas_call x2, Pallas kernels, ffn_forward(): pl.pallas_call(functools.partial(ffn_forward_kernel, stream), grid=(hidde...  29.6 us
    dot_general x13, matrix products, dot_tn(): lax.dot_general(a, b, (((0,), (0,)), ((), ())), preferred_element_type=f32)  26.8 us
    ppermute x10, starting transfers between devices, moved(): lax.ppermute(block, axis, [(i, (i + step) % size) for i in range(size)])  16 us
    unnamed x164, local copies, waits for them, and re-layouts  15.7 us
  transfers between devices with their start and end apart: 59, of which 19 were waited for; matrix products, arithmetic and copies ran while one was open for 18% of the time, Pallas kernels for 39%

commit v1 on v0

--- a/solution.py
+++ b/solution.py
@@ -13,14 +13,14 @@
 CELLS = WIN * WIN
 PAIR = 128
 MASKED = -1000000000.0
-VMEM_LIMIT = 56 * 1024 * 1024
+MIB = 1024 * 1024
 
 bf16 = jnp.bfloat16
 f32 = jnp.float32
 
 
-def params():
-    return pltpu.CompilerParams(vmem_limit_bytes=VMEM_LIMIT)
+def params(mib):
+    return pltpu.CompilerParams(vmem_limit_bytes=min(int(mib), 56) * MIB)
 
 
 def row_block(rows):
@@ -93,7 +93,7 @@
             pltpu.VMEM((columns + 2 * WIN, width), f32),
             pltpu.VMEM((cells, width), f32),
         ],
-        compiler_params=params(),
+        compiler_params=params(14),
         cost_estimate=cost(0, 4 * cells * width),
         name="enter",
     )(own, head)
@@ -128,7 +128,7 @@
             pltpu.VMEM((columns + 2 * WIN, width), f32),
             pltpu.VMEM(cells.shape, f32),
         ],
-        compiler_params=params(),
+        compiler_params=params(14),
         cost_estimate=cost(0, 4 * cells.size),
         name="leave",
     )(cells)
@@ -171,7 +171,7 @@
             jax.ShapeDtypeStruct((rows, width), bf16),
             jax.ShapeDtypeStruct((rows, full), bf16),
         ],
-        compiler_params=params(),
+        compiler_params=params(8 + rows // 80),
         cost_estimate=cost(2 * rows * width * full, 2 * rows * (2 * width + full) + 2 * width * full),
         name="norm_qkv",
     )(x, gain, bias, weight)
@@ -207,7 +207,9 @@
     return joined(turned.T)
 
 
-def query_forward_kernel(qq_ref, k_ref, v_ref, ko_ref, vo_ref, bias_ref, out_ref, lse_ref, s_ref):
+def query_forward_kernel(
+    qq_ref, k_ref, v_ref, ko_ref, vo_ref, bias_ref, out_ref, stats_ref, s_ref, lse_ref
+):
     queries = qq_ref.shape[0]
     cells = k_ref.shape[0]
     own = ko_ref.shape[0]
@@ -228,8 +230,20 @@
         prob = jnp.exp(s_ref[at, :] - top)
         total = total + jnp.sum(prob, 0, keepdims=True)
         mixed = mixed + dot_nn(v_ref[at, :].T, prob.astype(bf16))
-    out_ref[...] = unstacked(mixed * (1.0 / total)).astype(bf16)
-    lse_ref[...] = top + jnp.log(total)
+    out_ref[...] = unstacked(mixed * (1.0 / total))
+    lse = top + jnp.log(total)
+    pair = pl.program_id(0)
+
+    @pl.when(pair == 0)
+    def _():
+        lse_ref[...] = jnp.zeros_like(lse_ref)
+
+    lse_ref[pl.ds(2 * pair, 1), :] = lse[:, :queries]
+    lse_ref[pl.ds(2 * pair + 1, 1), :] = lse[:, queries:]
+
+    @pl.when(pair == pl.num_programs(0) - 1)
+    def _():
+        stats_ref[...] = lse_ref[...].T
 
 
 def query_forward(query_qkv, own_qkv, vis_qkv, self_bias):
@@ -254,13 +268,16 @@
             part(own, 2),
             whole(self_bias.shape),
         ],
-        out_specs=[part(queries, 0), pl.BlockSpec((None, 1, 2 * queries), lambda p: (p, 0, 0))],
+        out_specs=[part(queries, 0), whole((queries, PAIR))],
         out_shape=[
-            jax.ShapeDtypeStruct((queries, width), bf16),
-            jax.ShapeDtypeStruct((pairs, 1, 2 * queries), f32),
-        ],
-        scratch_shapes=[pltpu.VMEM((cells, 2 * queries), f32)],
-        compiler_params=params(),
+            jax.ShapeDtypeStruct((queries, width), f32),
+            jax.ShapeDtypeStruct((queries, PAIR), f32),
+        ],
+        scratch_shapes=[
+            pltpu.VMEM((cells, 2 * queries), f32),
+            pltpu.VMEM((PAIR, queries), f32),
+        ],
+        compiler_params=params(10 + queries // 32),
         cost_estimate=cost(
             4 * 2 * queries * keys * width, 4 * cells * width, 2 * queries * keys * pairs
         ),
@@ -351,7 +368,7 @@
             pltpu.VMEM((windows, PAIR, 2 * CELLS), f32),
             pltpu.VMEM((PAIR, 2 * cells), f32),
         ],
-        compiler_params=params(),
+        compiler_params=params(12 + queries // 28),
         cost_estimate=cost(
             8 * cells * (CELLS + queries) * width,
             8 * cells * width,
@@ -363,6 +380,7 @@
 
 def attention_backward_kernel(
     windows,
+    first,
     q_ref,
     k_ref,
     v_ref,
@@ -382,10 +400,11 @@
     mixq_ref,
     *rest,
 ):
-    if len(rest) > 15:
+    if len(rest) > 16:
         rest = rest[3:]
     attention_backward_body(
         windows,
+        first,
         q_ref,
         k_ref,
         v_ref,
@@ -409,6 +428,7 @@
 
 def attention_backward_body(
     windows,
+    first,
     q_ref,
     k_ref,
     v_ref,
@@ -441,6 +461,7 @@
     seenk_ref,
     seenv_ref,
     far_ref,
+    stats_ref,
 ):
     cells = [slice(w * CELLS, (w + 1) * CELLS) for w in range(windows)]
     lanes = [slice(2 * w * CELLS, 2 * (w + 1) * CELLS) for w in range(windows)]
@@ -469,7 +490,11 @@
 
     scaled_q = stacked(qq_ref[...] * 0.125)
     grad_q = stacked(doq_ref[...])
-    lse_q = lseq_ref[...]
+    stats_ref[...] = lseq_ref[...].T
+    head = 2 * (first + pl.program_id(0))
+    lse_q = jnp.concatenate(
+        [stats_ref[pl.ds(head, 1), :], stats_ref[pl.ds(head + 1, 1), :]], 1
+    )
     mix_q = mixq_ref[...]
     delta_q = row_sums(grad_q.astype(f32) * jnp.concatenate([mix_q, mix_q], 0))
     bias = bias_ref[...]
@@ -514,8 +539,7 @@
     closed,
     self_bias,
     lse,
-    lse_q,
-    mix_q,
+    joint_q,
     first,
     count,
     begun=(),
@@ -541,7 +565,7 @@
 
     span = count * PAIR
     return pl.pallas_call(
-        functools.partial(attention_backward_kernel, windows),
+        functools.partial(attention_backward_kernel, windows, first),
         grid=(count,),
         in_specs=[
             part(cells, 0),
@@ -559,7 +583,7 @@
             whole(closed.shape),
             whole(self_bias.shape),
             stats(lse),
-            stats(lse_q),
+            pl.BlockSpec((queries, PAIR), lambda p: (0, pairs)),
             part(queries, 0),
         ]
         + [pl.BlockSpec(memory_space=pl.ANY)] * len(begun),
@@ -575,8 +599,9 @@
             pltpu.VMEM((cells, PAIR), f32),
             pltpu.VMEM((cells, PAIR), f32),
             pltpu.VMEM((2 * cells, PAIR), f32),
-        ],
-        compiler_params=params(),
+            pltpu.VMEM((PAIR, queries), f32),
+        ],
+        compiler_params=params(16 + queries // 25),
         cost_estimate=cost(
             20 * cells * (CELLS + 2 * queries) * span,
             14 * cells * span,
@@ -600,8 +625,8 @@
         closed,
         self_bias,
         lse,
-        lse_q,
-        mix_q,
+        joint_q,
+        joint_q,
         *begun,
     )
 
@@ -641,7 +666,7 @@
     @pl.when(step == 0)
     def _():
         for at in ats:
-            x1 = x_ref[at, :].astype(f32) + dot_nn(o_ref[at, :], wo_ref[...]) + bo_ref[row, :]
+            x1 = x_ref[at, :].astype(f32) + dot_nn(o_ref[at, :].astype(bf16), wo_ref[...]) + bo_ref[row, :]
             x1_ref[at, :] = x1
             hat, _ = normalised(x1)
             b_ref[at, :] = (hat * gain_ref[row, :] + bias_ref[row, :]).astype(bf16)
@@ -699,7 +724,7 @@
             jax.ShapeDtypeStruct((rows, width), bf16),
         ],
         scratch_shapes=[pltpu.VMEM((rows, width), f32)],
-        compiler_params=params(),
+        compiler_params=params(44),
         cost_estimate=cost(
             2 * rows * width * (2 * hidden + width),
             4 * width * hidden + 4 * rows * hidden + 12 * rows * width,
@@ -787,21 +812,21 @@
             whole(gain.shape),
         ],
         out_specs=[
-            pl.BlockSpec((rows, chunk), lambda f: (0, f)),
+            pl.BlockSpec((None, rows, chunk), lambda f: (f, 0, 0)),
             whole((rows, width)),
             whole((rows, width)),
             whole((rows, width)),
             whole((4 + hidden // chunk, width)),
         ],
         out_shape=[
-            jax.ShapeDtypeStruct((rows, hidden), bf16),
+            jax.ShapeDtypeStruct((hidden // chunk, rows, chunk), bf16),
             jax.ShapeDtypeStruct((rows, width), f32),
             jax.ShapeDtypeStruct((rows, width), bf16),
             jax.ShapeDtypeStruct((rows, width), bf16),
             jax.ShapeDtypeStruct((4 + hidden // chunk, width), f32),
         ],
         scratch_shapes=[pltpu.VMEM((rows, width), f32)],
-        compiler_params=params(),
+        compiler_params=params(44),
         cost_estimate=cost(
             2 * rows * width * (2 * hidden + width),
             4 * width * hidden + 4 * rows * hidden + 14 * rows * width,
@@ -824,8 +849,9 @@
     out_ref[...] = (
         dx1_ref[...] + norm_back(grad, hat, rstd, gain_ref[stream : stream + 1, :])
     ).astype(bf16)
-    sums_ref[0:1, :] += jnp.sum(grad * hat, 0, keepdims=True)
-    sums_ref[1:2, :] += jnp.sum(grad, 0, keepdims=True)
+    at = 4 * stream
+    sums_ref[at : at + 1, :] += jnp.sum(grad * hat, 0, keepdims=True)
+    sums_ref[at + 1 : at + 2, :] += jnp.sum(grad, 0, keepdims=True)
 
 
 def input_grad(dq, dk, dv, weight, x, dx1, gain, stream):
@@ -847,7 +873,7 @@
             jax.ShapeDtypeStruct((rows, width), bf16),
             jax.ShapeDtypeStruct((8, width), f32),
         ],
-        compiler_params=params(),
+        compiler_params=params(16),
         cost_estimate=cost(6 * rows * width * width, 14 * rows * width + 6 * width * width),
         name="input_grad",
     )(dq, dk, dv, weight, x, dx1, gain)
@@ -898,16 +924,19 @@
 class Phase:
     def __init__(self, blocks, dims, axis, mask):
         bit = bit_of(axis, mask)
-        self.mine = [[pick(term, bit, dim) for term in terms] for terms, dim in zip(blocks, dims)]
-        theirs = [
-            added([pick(term, 1 - bit, dim) for term in terms]) for terms, dim in zip(blocks, dims)
+        theirs, self.mine = [
+            [added([pick(term, half, dim) for term in terms]) for terms, dim in zip(blocks, dims)]
+            for half in (1 - bit, bit)
         ]
         self.shapes = [block.shape for block in theirs]
         self.sent, self.got = exchange(theirs, axis, mask)
 
     def terms(self):
         got = parted(self.got, self.shapes)
-        return [[added(mine + [more])] for mine, more in zip(self.mine, got)]
+        return [[mine, more] for mine, more in zip(self.mine, got)]
+
+    def sums(self):
+        return [added(terms) for terms in self.terms()]
 
 
 def mapped(change, terms):
@@ -927,6 +956,27 @@
             jnp.stack([jnp.where(first, one, two), jnp.where(first, two, one)], dim)
             for one, two, dim in zip(self.blocks, parted(self.got, self.shapes), self.dims)
         ]
+
+
+class PageGather:
+    def __init__(self, blocks):
+        self.shapes = [block.shape for block in blocks]
+        rows = [block.reshape(-1, block.shape[-1]) for block in blocks]
+        self.sent = jnp.concatenate(rows, 0)
+        self.got = [swapped(self.sent, "page", mask) for mask in (1, 2, 3)]
+
+    def whole(self):
+        def ordered(bit, one, two, axis):
+            first = bit == 0
+            return jnp.stack([jnp.where(first, one, two), jnp.where(first, two, one)], axis)
+
+        every = [parted(rows, self.shapes) for rows in [self.sent] + list(self.got)]
+        result = []
+        for mine, by_x, by_y, by_both in zip(*every):
+            near = ordered(bit_of("page", 1), mine, by_x, 1)
+            far = ordered(bit_of("page", 1), by_y, by_both, 1)
+            result.append(from_page(ordered(bit_of("page", 2), near, far, 1)))
+        return result
 
 
 def parted(rows, shapes):
@@ -973,8 +1023,9 @@
     return blocks.reshape(blocks.shape[:-4] + (-1, blocks.shape[-1]))
 
 
-def by_chip(blocks):
-    return blocks.reshape((blocks.shape[0] // 2, 2) + blocks.shape[1:])
+def by_chip(blocks, axis):
+    shape = blocks.shape
+    return blocks.reshape(shape[:axis] + (shape[axis] // 2, 2) + shape[axis + 1 :])
 
 
 def line_masks():
@@ -982,19 +1033,22 @@
     return [2 << i for i in range(size.bit_length() - 1)]
 
 
-def line_phase(blocks, mask):
-    return Phase([mapped(by_chip, terms) for terms in blocks], [1] * len(blocks), "strip", mask)
-
-
-def line_first(blocks):
+def line_phase(blocks, axes, mask):
+    split = [
+        [by_chip(term, axis) for term in terms] for terms, axis in zip(blocks, axes)
+    ]
+    return Phase(split, [axis + 1 for axis in axes], "strip", mask)
+
+
+def line_first(blocks, axes):
     masks = line_masks()
     for mask in masks[:-2]:
-        blocks = line_phase(blocks, mask).terms()
-    return line_phase(blocks, masks[-2])
-
-
-def line_last(blocks):
-    return line_phase(blocks, line_masks()[-1])
+        blocks = line_phase(blocks, axes, mask).terms()
+    return line_phase(blocks, axes, masks[-2])
+
+
+def line_last(blocks, axes):
+    return line_phase(blocks, axes, line_masks()[-1])
 
 
 def line_exchange(block):
@@ -1049,27 +1103,38 @@
     return pair.reshape(-1, pair.shape[-1])
 
 
-def packed(mix, lse):
-    rows = mix.shape[0]
-    pairs = lse.shape[0]
-    stats = lse.reshape(pairs, 2, rows).transpose(2, 0, 1).reshape(rows, 2 * pairs)
-    stats = jnp.pad(stats, ((0, 0), (0, PAIR - 2 * pairs)))
-    return jnp.concatenate([mix.astype(f32), stats], 1)
-
-
-def merged(blocks):
-    width = blocks[0].shape[-1] - PAIR
-    lead = blocks[0].shape[:-1]
-    tops = [block[..., width : width + HEADS] for block in blocks]
-    top = functools.reduce(jnp.maximum, tops)
-    shares = [jnp.exp(each - top) for each in tops]
-    total = functools.reduce(jnp.add, shares)
-    mix = 0.0
-    for block, share in zip(blocks, shares):
-        heads = block[..., :width].reshape(lead + (HEADS, width // HEADS))
-        mix = mix + heads * (share / total)[..., None]
-    stats = jnp.pad(top + jnp.log(total), [(0, 0)] * len(lead) + [(0, PAIR - HEADS)])
-    return jnp.concatenate([mix.reshape(lead + (width,)), stats], -1)
+def merge_kernel(one_ref, two_ref, out_ref):
+    width = one_ref.shape[1] - PAIR
+    one_top = one_ref[:, width:]
+    two_top = two_ref[:, width:]
+    top = jnp.maximum(one_top, two_top)
+    one_share = jnp.exp(one_top - top)
+    two_share = jnp.exp(two_top - top)
+    total = one_share + two_share
+    shape = (PAIR, width)
+    head = lax.broadcasted_iota(jnp.int32, shape, 1) // (width // HEADS)
+    spread = (lax.broadcasted_iota(jnp.int32, shape, 0) == head).astype(f32)
+
+    def over_heads(share):
+        return jnp.dot(share / total, spread, precision=lax.Precision.HIGHEST)
+
+    out_ref[:, :width] = one_ref[:, :width] * over_heads(one_share) + two_ref[
+        :, :width
+    ] * over_heads(two_share)
+    out_ref[:, width:] = top + jnp.log(total)
+
+
+def merged(one, two):
+    shape = one.shape
+    rows = one.size // shape[-1]
+    out = pl.pallas_call(
+        merge_kernel,
+        out_shape=jax.ShapeDtypeStruct((rows, shape[-1]), f32),
+        compiler_params=params(8),
+        cost_estimate=cost(6 * one.size, 12 * one.size),
+        name="merge",
+    )(one.reshape(rows, -1), two.reshape(rows, -1))
+    return out.reshape(shape)
 
 
 def region_windows(rows):
@@ -1143,22 +1208,25 @@
     vis = enter(vis_tokens[0], head_rows)
     head_cot = moved(after(vis_cotangent[0, :SHIFT], vis), "strip", -1)
     vis_norm, vis_qkv = norm_qkv(vis, norm1_gain, norm1_bias, qkv_weight, 0)
-    (vis_norm, vis_qkv), head_cot = beside((vis_norm, vis_qkv), head_cot)
-
-    part = by_core(packed(*query_forward(query_qkv, own_qkv, vis_qkv, self_bias)))
-    mine, theirs = pick(part, core, 1), pick(part, 1 - core, 1)
+
+    part = query_forward(query_qkv, own_qkv, vis_qkv, self_bias)
+    part, head_cot = beside(part, head_cot)
+    mine, theirs = [
+        jnp.concatenate([pick(by_core(each), which, 1) for each in part], -1)
+        for which in (core, 1 - core)
+    ]
     others = other_core(theirs)
     vis_cot = enter(after(vis_cotangent[0], theirs), head_cot)
     vis_cot, mine, others = beside(vis_cot, mine, others)
-    part = merged([mine, others])
+    part = merged(mine, others)
     others = swapped(part, "strip", 2)
 
     vis_windows = window_forward(after(vis_qkv, part), query_qkv, region_row, region_col, closed)
     (vis_attn, vis_lse), part, others = beside(vis_windows, part, others)
-    part = merged([part, others])
+    part = merged(part, others)
     mask = 4
     while 2 * mask < strips:
-        part = merged([part, swapped(part, "strip", mask)])
+        part = merged(part, swapped(part, "strip", mask))
         mask = 2 * mask
     others = swapped(part, "strip", mask)
     cotangents = line_gather(after(query_cotangent[0], vis_attn))
@@ -1167,7 +1235,7 @@
     made = ffn_forward(vis, after(vis_attn, part), *weights, 0)
     made, part, others, cotangents = beside(made, part, others, cotangents)
     vis_x1, vis_b, vis_hid, vis_slope, vis_result = made
-    part = merged([part, others])
+    part = merged(part, others)
     others = other_core(part)
     cotangents = line_order(cotangents)
     cot_others = other_core(cotangents)
@@ -1185,32 +1253,29 @@
     vis_dz, vis_dx1, vis_du, vis_do, vis_sums = made
     (down,) = down.terms()
     down = Phase([mapped(by_page, down)], [3], "page", 1)
-    vis_up = weight_grad(after(vis_b, down.sent), vis_dz)
-    vis_outg = weight_grad(vis_attn, vis_du)
-    up = jnp.concatenate(
-        [tiled(by_core(vis_up), features), tiled(by_core(vis_outg), features)], 2
-    )
-    up = Phase([[up]], [1], "strip", 1)
-    made = leave(after(vis_result, up.sent), columns)
-    (vis_keep, vis_send), up.got = beside(made, up.got)
+    hidden = up_weight.shape[-1] // features
+    vis_b = after(vis_b, down.sent)
+    up_a = [by_core(weight_grad(vis_b, vis_dz[i])) for i in range(hidden - 1)]
+    up_a = Phase([[jnp.stack(up_a)]], [2], "strip", 1)
+    up_b = [by_core(weight_grad(after(vis_b, up_a.sent), vis_dz[hidden - 1]))]
+    up_b = Phase([[jnp.stack(up_b + [by_core(weight_grad(vis_attn, vis_du))])]], [2], "strip", 1)
+    made = leave(after(vis_result, up_b.sent), columns)
+    (vis_keep, vis_send), up_a.got, up_b.got = beside(made, up_a.got, up_b.got)
     vis_first = moved(vis_send, "strip", 1)
-    (up,) = up.terms()
-    up_a = line_first([mapped(lambda term: term[:, :3], up)])
+    up_a = line_first(up_a.terms(), [1])
 
     every = core_order(part, others)
     query_cot = core_order(cotangents, cot_others)
-    query_mix = every[:, :features]
-    stats = every[:, features : features + HEADS]
-    query_lse = stats.T.reshape(HEADS // 2, 1, 2 * query_count)
-    query_attn = query_mix.astype(bf16)
-    made = ffn_forward(query, after(query_attn, up_a.sent), *weights, 1)
+    every, up_sent = beside(every, up_a.sent)
+    made = ffn_forward(query, every, *weights, 1)
     made, down.got = beside(made, down.got)
     query_x1, query_b, query_hid, query_slope, query_result = made
     (down,) = down.terms()
-    up_b = Phase([mapped(lambda term: by_page(term[:, 3:]), up)], [3], "page", 1)
+    down = Phase([down], [2], "page", 2)
+    up_b = Phase([mapped(by_page, terms) for terms in up_b.terms()], [3], "page", 1)
     made = ffn_backward(
         query_cot,
-        after(query_slope, up_b.sent),
+        after(query_slope, up_b.sent, down.sent),
         query_x1,
         down_weight,
         up_weight,
@@ -1218,26 +1283,29 @@
         norm2_gain,
         1,
     )
-    made, up_a.got, up_b.got, vis_first = beside(made, up_a.got, up_b.got, vis_first)
+    made, up_a.got, up_b.got = beside(made, up_a.got, up_b.got)
     query_dz, query_dx1, query_du, query_do, query_sums = made
     (up_a,) = up_a.terms()
     (up_b,) = up_b.terms()
     up_a = Phase([mapped(by_page, up_a)], [3], "page", 1)
-    low = Phase([down, up_b], [2, 2], "page", 2)
+    up_b = Phase([up_b], [2], "page", 2)
 
     def query_grads(left, right):
         return weight_grad(own_columns(left), right)
 
     up_rows = features // strips
+    query_dz = after(query_dz, up_a.sent, up_b.sent)
     one = jnp.concatenate(
         [
-            tiled(query_grads(query_b, after(query_dz, up_a.sent, low.sent)), features),
-            query_grads(query_attn, query_du)[None],
+            jnp.stack([query_grads(query_b, query_dz[i]) for i in range(hidden)]),
+            query_grads(every[:, :features].astype(bf16), query_du)[None],
             query_grads(query_hid, query_cot).reshape(-1, up_rows, features),
         ],
         0,
     )
+    one, down.got = beside(one, down.got)
     one = Phase([[by_page(one)]], [2], "page", 1)
+    down = line_first(down.terms(), [0])
 
     pairs = HEADS // 2
     half = pairs // 2
@@ -1254,8 +1322,7 @@
             closed,
             self_bias,
             vis_lse,
-            query_lse,
-            query_mix,
+            every,
             first,
             half,
             begun,
@@ -1271,54 +1338,48 @@
             2,
         )
 
-    back_one = backward(after(vis_qkv, one.sent), 0)
-    back_one, up_a.got, low.got = beside(back_one, up_a.got, low.got)
+    back_one = backward(after(vis_qkv, one.sent, down.sent), 0)
+    back_one, up_a.got, up_b.got, down.got, vis_first = beside(
+        back_one, up_a.got, up_b.got, down.got, vis_first
+    )
+    first = Phase([[head_grads(vis_norm, back_one[:3], 0)]], [1], "strip", 1)
+    first.sent, one.got = beside(first.sent, one.got)
     (up_a,) = up_a.terms()
-    low = low.terms()
-    up_a = Phase([up_a], [2], "page", 2)
-    low = line_first(low)
-    first = Phase(
-        [[head_grads(after(vis_norm, up_a.sent, low.sent), back_one[:3], 0)]], [1], "strip", 1
-    )
-    first.sent, one.got = beside(first.sent, one.got)
     (one,) = one.terms()
-    one = Phase([one], [1], "page", 2)
-
-    back_two = backward(after(vis_qkv, first.sent, one.sent), half, back_one[:3])
-    back_two, first.got, up_a.got, low.got, one.got = beside(
-        back_two, first.got, up_a.got, low.got, one.got
-    )
-    (up_a,) = up_a.terms()
-    low = low.terms()
-    line = line_last([up_a] + low)
-    (one,) = one.terms()
-    one_gather = Gather([one[0]], [1], "page", 1)
+    mixed_y = Phase([after(up_a, first.sent), one], [2, 1], "page", 2)
+    up_b = line_first(up_b.terms(), [1])
+    down = line_last(down.terms(), [0])
+    down.sent, up_b.sent, mixed_y.sent, first.got = beside(
+        down.sent, up_b.sent, mixed_y.sent, first.got
+    )
+    (first,) = first.terms()
+    first = Phase([mapped(by_page, first)], [3], "page", 1)
+
+    back_two = backward(
+        after(vis_qkv, first.sent, mixed_y.sent, up_b.sent, down.sent), half, back_one[:3]
+    )
+    back_two, first.got, mixed_y.got, up_b.got, down.got = beside(
+        back_two, first.got, mixed_y.got, up_b.got, down.got
+    )
     part = jnp.stack(
         [by_core(each) for pair in zip(back_one[3:6], back_two[3:6]) for each in pair], 2
     )
     part = Phase([[part]], [1], "strip", 1)
-    second = Phase(
-        [
-            [
-                head_grads(
-                    after(vis_norm, part.sent, line.sent, one_gather.sent), back_two[:3], half
-                )
-            ]
-        ],
-        [1],
-        "strip",
-        1,
-    )
+    grads = head_grads(after(vis_norm, part.sent), back_two[:3], half)
+    second = Phase([[grads]], [1], "strip", 1)
     second.sent, part.got = beside(second.sent, part.got)
-    (part,) = part.terms()
-    part = line_first([part])
-    (first,) = first.terms()
-    first = Phase([mapped(by_page, after(first, part.sent))], [3], "page", 1)
-    first.sent, second.got = beside(first.sent, second.got)
+    part = line_first(part.terms(), [0])
+    up_a, one = mixed_y.terms()
+    (up_b,) = up_b.terms()
+    line = line_last([after(up_a, part.sent), up_b], [1, 1])
+    line.sent, second.got = beside(line.sent, second.got)
     (second,) = second.terms()
+    second = Phase([mapped(by_page, second)], [3], "page", 1)
+    (down,) = down.sums()
+    early = Gather([after(added(one), second.sent), down[0]], [1, 1], "page", 1)
 
     made = input_grad(
-        after(back_two[0], second, part.sent, first.sent),
+        after(back_two[0], part.sent, line.sent, second.sent, early.sent),
         back_two[1],
         back_two[2],
         qkv_weight,
@@ -1327,17 +1388,11 @@
         norm1_gain,
         0,
     )
-    made, first.got, part.got, line.got, one_gather.got = beside(
-        made, first.got, part.got, line.got, one_gather.got
-    )
+    made, part.got = beside(made, part.got)
     vis_input, vis_head = made
-    (part,) = part.terms()
-    part = line_last([part])
-    second = Phase([mapped(by_page, after(second, part.sent))], [3], "page", 1)
-    one_gather = Gather(one_gather.pairs(), [1], "page", 2)
-    all_gather = Gather([terms[0][0] for terms in line.terms()], [1, 1, 1], "page", 1)
-    made = leave(after(vis_input, part.sent, second.sent, all_gather.sent), columns)
-    made, part.got = beside(made, part.got)
+    part = line_last(part.terms(), [0])
+    made = leave(after(vis_input, part.sent), columns)
+    made, part.got, second.got, line.got = beside(made, part.got, second.got, line.got)
     grad_keep, grad_send = made
     (part,) = part.terms()
     own_self = [jnp.zeros_like(back_one[6])] * 2 + [back_one[6], back_two[6], back_one[7], back_two[7]]
@@ -1348,8 +1403,11 @@
         lined = Gather([lined], [1], "strip", mask).pairs()[0]
         lined = lined.reshape((-1,) + own_dqkv.shape)
     lined = Gather([lined], [0], "strip", masks[-1])
+    qkv = Phase(
+        [after(terms, lined.sent) for terms in first.terms() + second.terms()], [2, 2], "page", 2
+    )
     made = input_grad(
-        untiled(after(own_dqkv, lined.sent)[0:2]),
+        untiled(after(own_dqkv, lined.sent, qkv.sent)[0:2]),
         untiled(own_dqkv[2:4]),
         untiled(own_dqkv[4:6]),
         qkv_weight,
@@ -1358,83 +1416,82 @@
         norm1_gain,
         1,
     )
-    made, lined.got, second.got, all_gather.got = beside(
-        made, lined.got, second.got, all_gather.got
-    )
+    made, lined.got, early.got = beside(made, lined.got, early.got)
     own_input, own_head = made
     lined = lined.pairs()[0].reshape((-1,) + own_dqkv.shape)
     lined = Gather([lined], [1], "strip", masks[0])
-    (first,) = first.terms()
-    (second,) = second.terms()
-    qkv = Phase([first, second], [2, 2], "page", 2)
-    up_a, down, up_b = all_gather.pairs()
-    up_gather = Gather([up_a, up_b], [1, 1], "page", 2)
-
-    once = jnp.where(strip == 0, 1.0, 0.0)
-    small = jnp.concatenate([vis_sums, vis_head, once * query_sums, own_head], 0)
-    lined.got, small, one_gather.got = beside(lined.got, small, one_gather.got)
+    one, down = after(early.pairs(), lined.sent)
+    down = Gather([down], [1], "page", 2)
+
+    small = jnp.concatenate([vis_sums, vis_head + own_head], 0)
+    small_others = other_core(small)
+    lined.got, small_others, qkv.got = beside(lined.got, small_others, qkv.got)
+    small = small + small_others
     lined = lined.pairs()[0].reshape((-1,) + own_dqkv.shape)
     lined_others = other_core(lined)
-    small_others = other_core(small)
-    lined_others, small_others, qkv.got = beside(lined_others, small_others, qkv.got)
+    grad_first = moved(after(grad_send, lined), "strip", 1)
+    for mask in masks[:-2]:
+        small = small + swapped(small, "strip", mask)
+    small_others = swapped(small, "strip", masks[-2])
+    qkv = line_first(after(qkv.terms(), lined), [0, 0])
+    up_part, low_part = line.sums()
+    up_gather = Gather([after(up_part, lined)[:, 0], low_part[:, 0]], [1, 1], "page", 1)
+    lined_others, small_others, down.got = beside(lined_others, small_others, down.got)
+    one_first = Gather([after(one, down.got)[:5]], [1], "page", 2)
     small = small + small_others
     query_dqkv = jnp.stack(
         [jnp.where(core == 0, lined, lined_others), jnp.where(core == 0, lined_others, lined)], 1
     )
     query_dqkv = [query_dqkv[:, :, i].reshape(query_count, -1) for i in range(6)]
-    qkv = line_first(qkv.terms())
     three = query_grads(query_norm, jnp.concatenate(query_dqkv, 1))
-    three = page_exchange(three)
-    for mask in masks[:-2]:
-        small = small + swapped(small, "strip", mask)
-    small_others = swapped(small, "strip", masks[-2])
-    three, qkv.got, small_others, up_gather.got = beside(
-        three, qkv.got, small_others, up_gather.got
-    )
-    three = page_gather(added(three))
-    qkv = line_last(qkv.terms())
+    three = Phase([[by_page(tiled(three, half * PAIR))]], [2], "page", 1)
+    small_others = swapped(small, "strip", masks[-1])
+    three.got, qkv.got, small_others, up_gather.got, one_first.got, grad_first = beside(
+        three.got, qkv.got, small_others, up_gather.got, one_first.got, grad_first
+    )
+    three = Phase(three.terms(), [1], "page", 2)
+    qkv = line_last(after(qkv.terms(), three.sent), [0, 0])
+    small = jnp.concatenate([small + small_others, query_sums], 0)
+    small_others = swapped(small, "page", 2)
+    last = Gather([after(one, three.sent)[5:]] + up_gather.pairs(), [1, 1, 1], "page", 2)
+    three.got, qkv.got, small_others = beside(three.got, qkv.got, small_others)
+    late = PageGather([each[0] for each in qkv.sums()] + three.sums())
     small = small + small_others
-    small_others = swapped(small, "strip", masks[-1])
-    down_gather = Gather([down], [1], "page", 2)
-    three, qkv.got, small_others, down_gather.got = beside(
-        three, qkv.got, small_others, down_gather.got
-    )
-    qkv = [terms[0][0] for terms in qkv.terms()]
-    late = Gather(qkv, [1, 1], "page", 1)
+    small_others = swapped(after(small, late.sent), "page", 1)
     small = small + small_others
-    small_others = swapped(small, "page", 1)
-    grad_first = moved(after(grad_send, late.sent), "strip", 1)
-    three = page_order(three)
-    late.got, small_others = beside(late.got, small_others)
-    late = Gather(late.pairs(), [1, 1], "page", 2)
-    small = small + small_others
-    small_others = swapped(small, "page", 2)
-    small = small + small_others
-
-    up_a, up_b = [from_page(each) for each in up_gather.pairs()]
-    (one,) = [from_page(each) for each in one_gather.pairs()]
-    (down,) = [from_page(each) for each in down_gather.pairs()]
-    hidden = up_weight.shape[-1] // features
+
+    one_last, up_a, up_b = [from_page(each) for each in last.pairs()]
+    (down,) = [from_page(each) for each in down.pairs()]
+    one = jnp.concatenate([from_page(each) for each in one_first.pairs()] + [one_last], 0)
     up = jnp.concatenate([up_a, up_b], 0)
     up_grad = jnp.stack([untiled(up[:hidden]), untiled(one[:hidden])]).astype(f32)
     out_grad = jnp.stack([up[hidden], one[hidden]]).astype(f32)
     down_grad = jnp.stack([down, one[hidden + 1 :]]).astype(f32).reshape(2, -1, features)
-    first, second = [from_page(each) for each in late.pairs()]
+    vis_final = jnp.concatenate([vis_first, vis_keep], 0)[None]
+    grad_final = jnp.concatenate([grad_first, grad_keep], 0)[None]
+    late.got, up_grad, out_grad, down_grad, vis_final, grad_final = beside(
+        late.got, up_grad, out_grad, down_grad, vis_final, grad_final
+    )
+    first, second, three = late.whole()
     vis_qkv_grad = jnp.concatenate(
         [each[i] for i in range(3) for each in (first, second)], 1
     )
-    qkv_grad = jnp.stack([vis_qkv_grad.astype(f32), three])
+    qkv_grad = jnp.stack([vis_qkv_grad, untiled(three)]).astype(f32)
 
     count = vis_sums.shape[0]
-    small = small.reshape(2, count + 8, features)
-    gain_two, bias_two, obias, dbias = [own_columns(small[:, i]) for i in range(4)]
-    gain_one, bias_one = [own_columns(small[:, count + i]) for i in range(2)]
-    ubias = own_columns(small[:, 4:count].reshape(2, -1))
+    gain_two, bias_two, obias, dbias = [
+        own_columns(jnp.stack([small[i], small[count + 8 + i]])) for i in range(4)
+    ]
+    gain_one, bias_one = [
+        own_columns(jnp.stack([small[count + i], small[count + 4 + i]])) for i in range(2)
+    ]
+    ubias = jnp.stack([small[4:count].reshape(-1), small[count + 12 :].reshape(-1)])
+    ubias = own_columns(ubias)
 
     return (
-        jnp.concatenate([vis_first, vis_keep], 0)[None],
+        vis_final,
         own_rows(query_result)[None],
-        jnp.concatenate([grad_first, grad_keep], 0)[None],
+        grad_final,
         own_input[None],
         gain_one,
         bias_one,

time: 382 us -> 362 us (0.948)
  the two profiles are of different devices: /device:TPU:0 before, /device:TPU:1 now
where the time goes in v1:
time: 362 us; the launch traced here: 359 us
  Pallas kernels  129 us (36%)
  waiting for transfers between devices  64.4 us (18%)
  starting transfers between devices  57.9 us (16%)
  other arithmetic  39.9 us (11%)
  local copies, waits for them, and re-layouts  36.7 us (10%)
  matrix products  26.5 us (7%)
  between operations  4.48 us (1%)
    ppermute x49, waiting for transfers between devices, swapped(): return lax.ppermute(block, axis, [(i, i ^ mask) for i in range(size)])  59.3 us
    ppermute x49, starting transfers between devices, swapped(): return lax.ppermute(block, axis, [(i, i ^ mask) for i in range(size)])  44.7 us
    pallas_call x2, Pallas kernels, attention_backward(): pl.pallas_call(functools.partial(attention_backward_kernel, windows, firs...  32 us
    dot_general x19, matrix products, dot_tn(): lax.dot_general(a, b, (((0,), (0,)), ((), ())), preferred_element_type=f32)  26.5 us
    pallas_call x2, Pallas kernels, ffn_backward(): pl.pallas_call(functools.partial(ffn_backward_kernel, stream), grid=(hidd...  26.4 us
    pallas_call x2, Pallas kernels, ffn_forward(): pl.pallas_call(functools.partial(ffn_forward_kernel, stream), grid=(hidde...  25.6 us
    unnamed x237, local copies, waits for them, and re-layouts  21.5 us
    convert_element_type x40, other arithmetic, added(): return total.astype(kind)  19.9 us
  transfers between devices with their start and end apart: 59, of which 16 were waited for; matrix products, arithmetic and copies ran while one was open for 18% of the time, Pallas kernels for 34%

profile of v1, /device:TPU:1, one launch (start us, length us, event | category | flops | bytes accessed | tf_op | source)
XLA Modules:
  0.0 358.6 jit_solution(2200030292581231900)
XLA Ops:
  0.7 4.2 %collective-permute-start = (bf16[32,768]{1,0:T(8,128)(2,1)}, bf16[32,768]{1,0:T(8,128)(2,1)S(1)}, u32[]{:S(2)}, u32[]{:S(2)}) collective-permute-start(bf16[32,768]{1,0:T(8,128)(2,1)} %bitcast.580), channel_id=1, source_target_pairs={{0,6},{1,7},{2,0},{3,1},{4,2},{5,3},{6,4},{7,5},{8,14},{9,15},{10,... | collective-permute-start | bytes 147464 | tf_op jit(solution)/shard_map/ppermute | solution.py:892
  14.9 3.1 copy-done.2
  24.1 5.2 %norm_qkv.3 = (bf16[1008,768]{1,0:T(8,128)(2,1)S(1)}, bf16[1008,2304]{1,0:T(8,128)(2,1)S(1)}) custom-call(bf16[1008,768]{1,0:T(8,128)(2,1)S(1)} %enter.2.x_ref, f32[2,768]{1,0:T(2,128)S(1)} %copy-done.50, f32[2,768]{1,0:T(2,128)S(1)} %copy-done.58, bf16[2,768,2304]{2,1,0:T(8,128)(2,1)S(1)} %bitcast.558), custom_call_target="tpu_custom_call" | custom-call | flops 178362 | bytes 564 | tf_op jit(solution)/shard_map/norm_qkv/pallas_call | solution.py:160
  30.4 9.1 %query_forward.1 = (f32[256,768]{1,0:T(8,128)S(1)}, f32[256,128]{1,0:T(8,128)S(1)}) custom-call(bf16[256,2304]{1,0:T(8,128)(2,1)S(1)} %get-tuple-element.232.qq_ref.kq_ref.vq_ref, bf16[1008,2304]{1,0:T(8,128)(2,1)S(1)} %get-tuple-element.336.k_ref.v_ref.q_ref, bf16[1008,2304]{1,0:T(8,128)(2,1)S(1)} %get-tuple-element.336.k_ref.v_ref.q_ref, ...), custom_call_target="tpu_custom_call" | custom-call | flops 81788 | bytes 154 | tf_op jit(solution)/shard_map/query_forward/pallas_call | solution.py:260
  41.4 3.1 collective-permute-start.6
  53.8 11.7 %window_forward.1 = (bf16[1008,768]{1,0:T(8,128)(2,1)S(1)}, f32[6,1,2016]{2,1,0:T(1,128)S(1)}) custom-call(bf16[1008,2304]{1,0:T(8,128)(2,1)S(1)} %copy-done.1, bf16[1008,2304]{1,0:T(8,128)(2,1)S(1)} %copy-done.1, bf16[1008,2304]{1,0:T(8,128)(2,1)S(1)} %copy-done.1, bf16[256,2304]{1,0:T(8,128)(2,1)S(1)} %copy-done.4, bf16[256,2304]{1,0:T(8,128)(2,1)S(1)} %copy-done.4, ...), custom_call_target="tpu_custom_call" | custom-call | flops 123863 | bytes 309 | tf_op jit(solution)/shard_map/window_forward/pallas_call | solution.py:344
  72.7 18.0 %ffn_forward.2 = (f32[1008,768]{1,0:T(8,128)}, bf16[1008,768]{1,0:T(8,128)(2,1)S(1)}, bf16[1008,3072]{1,0:T(8,128)(2,1)}, bf16[1008,3072]{1,0:T(8,128)(2,1)}, bf16[1008,768]{1,0:T(8,128)(2,1)S(1)}) custom-call(bf16[1008,768]{1,0:T(8,128)(2,1)S(1)} %copy-done.7, bf16[1008,768]{1,0:T(8,128)(2,1)S(1)} %get-tuple-element.248.o_ref, ...), custom_call_target="tpu_custom_call" | custom-call | flops 535088 | bytes 1555 | tf_op jit(solution)/shard_map/ffn_forward/pallas_call | solution.py:697
  90.8 3.9 %collective-permute-done.10 = bf16[32,768]{1,0:T(8,128)(2,1)S(1)} collective-permute-done((bf16[32,768]{1,0:T(8,128)(2,1)S(1)}, bf16[32,768]{1,0:T(8,128)(2,1)S(1)}, u32[]{:S(2)}, u32[]{:S(2)}) %collective-permute-start.10) | collective-permute-done | bytes 49184 | tf_op jit(solution)/shard_map/ppermute | solution.py:892
  97.0 8.6 %convolution_convert_fusion = bf16[3072,768]{1,0:T(8,128)(2,1)S(1)} fusion(bf16[1008,3072]{1,0:T(8,128)(2,1)} %get-tuple-element.262, bf16[1008,768]{1,0:T(8,128)(2,1)S(1)} %copy-done.16), kind=kOutput, calls=%fused_computation.1 | convolution fusion | flops 4758700032 | bytes 12460032 | tf_op jit(solution)/shard_map/dot_general | solution.py:42
  105.7 2.7 constant_dynamic-slice_fusion.34
  110.9 19.0 %ffn_backward.2 = (bf16[4,1008,768]{2,1,0:T(8,128)(2,1)}, f32[1008,768]{1,0:T(8,128)S(1)}, bf16[1008,768]{1,0:T(8,128)(2,1)S(1)}, bf16[1008,768]{1,0:T(8,128)(2,1)S(1)}, f32[8,768]{1,0:T(8,128)S(1)}) custom-call(bf16[1008,768]{1,0:T(8,128)(2,1)S(1)} %copy-done.17, bf16[1008,3072]{1,0:T(8,128)(2,1)} %get-tuple-element.269.slope_ref, ...), custom_call_target="tpu_custom_call" | custom-call | flops 535088 | bytes 1633 | tf_op jit(solution)/shard_map/ffn_backward/pallas_call | solution.py:802
  131.6 3.2 fusion.24
  134.8 3.0 fusion.12
  155.4 2.7 add_convert_fusion
  158.2 3.2 add_convert_fusion.2
  162.4 7.6 %ffn_forward.3 = (f32[256,768]{1,0:T(8,128)S(1)}, bf16[256,768]{1,0:T(8,128)(2,1)S(1)}, bf16[256,3072]{1,0:T(8,128)(2,1)S(1)}, bf16[256,3072]{1,0:T(8,128)(2,1)S(1)}, bf16[256,768]{1,0:T(8,128)(2,1)S(1)}) custom-call(bf16[256,768]{1,0:T(8,128)(2,1)S(1)} %bitcast.570, f32[256,896]{1,0:T(8,128)S(1)} %bitcast.561, bf16[2,768,768]{2,1,0:T(8,128)(2,1)S(1)} %copy-done.5, ...), custom_call_target="tpu_custom_call" | custom-call | flops 135895 | bytes 747 | tf_op jit(solution)/shard_map/ffn_forward/pallas_call | solution.py:697
  170.0 6.5 %collective-permute-done.17 = bf16[4,4,2,24,768]{4,3,1,0,2:T(8,128)(2,1)} collective-permute-done((bf16[4,4,2,24,768]{4,3,1,0,2:T(8,128)(2,1)}, bf16[4,4,2,24,768]{4,3,1,0,2:T(8,128)(2,1)}, u32[]{:S(2)}, u32[]{:S(2)}) %collective-permute-start.17) | collective-permute-done | bytes 1179680 | tf_op jit(solution)/shard_map/ppermute | solution.py:897
  179.9 2.7 fusion.28
  182.6 7.5 %ffn_backward.3 = (bf16[4,256,768]{2,1,0:T(8,128)(2,1)S(1)}, f32[256,768]{1,0:T(8,128)S(1)}, bf16[256,768]{1,0:T(8,128)(2,1)S(1)}, bf16[256,768]{1,0:T(8,128)(2,1)S(1)}, f32[8,768]{1,0:T(8,128)S(1)}) custom-call(bf16[256,768]{1,0:T(8,128)(2,1)S(1)} %bitcast.571, bf16[256,3072]{1,0:T(8,128)(2,1)S(1)} %get-tuple-element.298.slope_ref, ...), custom_call_target="tpu_custom_call" | custom-call | flops 135895 | bytes 766 | tf_op jit(solution)/shard_map/ffn_backward/pallas_call | solution.py:802
  200.7 3.4 collective-permute-done.20
  205.8 15.9 %attention_backward.2 = (bf16[1008,768]{1,0:T(8,128)(2,1)S(1)}, bf16[1008,768]{1,0:T(8,128)(2,1)S(1)}, bf16[1008,768]{1,0:T(8,128)(2,1)S(1)}, bf16[256,384]{1,0:...) custom-call(bf16[1008,2304]{1,0:T(8,128)(2,1)S(1)} %bitcast.556, ...), custom_call_target="tpu_custom_call" | custom-call | flops 253919 | bytes 270 | tf_op jit(solution)/shard_map/attention_backward/pallas_call | solution.py:567
  226.9 4.4 %collective-permute-start.26 = (bf16[4,3,96,384]{3,2,1,0:T(8,128)(2,1)S(1)}, bf16[4,3,96,384]{3,2,1,0:T(8,128)(2,1)S(1)}, u32[]{:S(2)}, u32[]{:S(2)}) collective-permute-start(bf16[4,3,96,384]{3,2,1,0:T(8,128)(2,1)S(1)} %bitcast.634), channel_id=1, source_target_pairs={{0,1},{1,0},{2,3},{3,2},{4,5},{5,4},{6,7},{7,6},{8,9},{9,8},{10,11... | collective-permute-start | bytes 2654216 | tf_op jit(solution)/shard_map/ppermute | solution.py:897
  238.2 16.1 %attention_backward.3 = (bf16[1008,768]{1,0:T(8,128)(2,1)S(1)}, bf16[1008,768]{1,0:T(8,128)(2,1)S(1)}, bf16[1008,768]{1,0:T(8,128)(2,1)S(1)}, bf16[256,384]{1,0:...) custom-call(bf16[1008,2304]{1,0:T(8,128)(2,1)S(1)} %bitcast.556, ...), custom_call_target="tpu_custom_call", output_to_operand_aliasing={{0}: (17, {}), {1}: (18, {}), {2}: (19, {})} | custom-call | flops 253919 | bytes 270 | tf_op jit(solution)/shard_map/attention_backward/pallas_call | solution.py:567
  265.5 5.7 %input_grad.2 = (bf16[1008,768]{1,0:T(8,128)(2,1)S(1)}, f32[8,768]{1,0:T(8,128)S(1)}) custom-call(bf16[1008,768]{1,0:T(8,128)(2,1)S(1)} %get-tuple-element.364.dq_ref, bf16[1008,768]{1,0:T(8,128)(2,1)S(1)} %get-tuple-element.354.dk_ref, bf16[1008,768]{1,0:T(8,128)(2,1)S(1)} %get-tuple-element.355.dv_ref, bf16[2,768,2304]{2,1,0:T(8,128)(2,1)S(1)} %bitcast.560, ...), custom_call_target="tpu_custom_call" | custom-call | flops 178362 | bytes 718 | tf_op jit(solution)/shard_map/input_grad/pallas_call | solution.py:861
  271.2 3.5 collective-permute-done.33
  276.5 8.2 %collective-permute-done.34 = bf16[1,6,32,384]{3,2,1,0:T(8,128)(2,1)S(1)} collective-permute-done((bf16[1,6,32,384]{3,2,1,0:T(8,128)(2,1)S(1)}, bf16[1,6,32,384]{3,2,1,0:T(8,128)(2,1)S(1)}, u32[]{:S(2)}, u32[]{:S(2)}) %collective-permute-start.34) | collective-permute-done | bytes 147488 | tf_op jit(solution)/shard_map/ppermute | solution.py:897
  287.9 5.8 %collective-permute-done.37 = bf16[1,6,32,384]{3,2,1,0:T(8,128)(2,1)S(1)} collective-permute-done((bf16[1,6,32,384]{3,2,1,0:T(8,128)(2,1)S(1)}, bf16[1,6,32,384]{3,2,1,0:T(8,128)(2,1)S(1)}, u32[]{:S(2)}, u32[]{:S(2)}) %collective-permute-start.37) | collective-permute-done | bytes 147488 | tf_op jit(solution)/shard_map/ppermute | solution.py:897
  295.2 7.9 %collective-permute-done.39 = bf16[2,6,32,384]{3,2,1,0:T(8,128)(2,1)S(1)} collective-permute-done((bf16[2,6,32,384]{3,2,1,0:T(8,128)(2,1)S(1)}, bf16[2,6,32,384]{3,2,1,0:T(8,128)(2,1)S(1)}, u32[]{:S(2)}, u32[]{:S(2)}) %collective-permute-start.39) | collective-permute-done | bytes 294944 | tf_op jit(solution)/shard_map/ppermute | solution.py:897
  306.4 10.9 %collective-permute-done.43 = f32[16,768]{1,0:T(8,128)S(1)} collective-permute-done((f32[16,768]{1,0:T(8,128)S(1)}, f32[16,768]{1,0:T(8,128)S(1)}, u32[]{:S(2)}, u32[]{:S(2)}) %collective-permute-start.43) | collective-permute-done | bytes 49184 | tf_op jit(solution)/shard_map/ppermute | solution.py:897
  320.3 3.9 %collective-permute-start.47 = (f32[16,768]{1,0:T(8,128)S(1)}, f32[16,768]{1,0:T(8,128)S(1)}, u32[]{:S(2)}, u32[]{:S(2)}) collective-permute-start(f32[16,768]{1,0:T(8,128)S(1)} %add.698), channel_id=1, source_target_pairs={{0,4},{1,5},{2,6},{3,7},{4,0},{5,1},{6,2},{7,3},{8,12},{9,13},{10,... | collective-permute-start | bytes 147464 | tf_op jit(solution)/shard_map/ppermute | solution.py:897
  327.8 3.8 %collective-permute-start.52 = (bf16[144,384]{1,0:T(8,128)(2,1)S(1)}, bf16[144,384]{1,0:T(8,128)(2,1)S(1)}, u32[]{:S(2)}, u32[]{:S(2)}) collective-permute-start(bf16[144,384]{1,0:T(8,128)(2,1)S(1)} %pad_maximum_fusion.31), channel_id=1, source_target_pairs={{0,4},{1,5},{2,6},{3,7},{4,0},{5,1},{6,2},{7,3},{8,12},{9,13},{10,... | collective-permute-start | bytes 331784 | tf_op jit(solution)/shard_map/ppermute | solution.py:897
  344.2 7.7 %collective-permute-done.57 = bf16[432,768]{1,0:T(8,128)(2,1)S(1)} collective-permute-done((bf16[432,768]{1,0:T(8,128)(2,1)S(1)}, bf16[432,768]{1,0:T(8,128)(2,1)S(1)}, u32[]{:S(2)}, u32[]{:S(2)}) %collective-permute-start.57) | collective-permute-done | bytes 663584 | tf_op jit(solution)/shard_map/ppermute | solution.py:897
  (577 shorter events, 132.0 us)
Async XLA Ops:
  23.2 16.3 %collective-permute-start.5 = (bf16[6,84,768]{2,1,0:T(8,128)(2,1)S(1)}, bf16[6,84,768]{2,1,0:T(8,128)(2,1)S(1)}, u32[]{:S(2)}, u32[]{:S(2)}) collective-permute-start(bf16[6,84,768]{2,1,0:T(8,128)(2,1)S(1)} %copy-done.72), channel_id=1, source_target_pairs={{0,7},{1,0},{2,1},{3,2},{4,3},{5,4},{6,5},{7,6},{8,15},{9,8},{10,9... | collective-permute-start | bytes 2322440 | tf_op jit(solution)/shard_map/ppermute | solution.py:892
  48.6 17.5 %collective-permute-start.7 = (f32[4,32,896]{2,1,0:T(8,128)}, f32[4,32,896]{2,1,0:T(8,128)}, u32[]{:S(2)}, u32[]{:S(2)}) collective-permute-start(f32[4,32,896]{2,1,0:T(8,128)} %bitcast.21), channel_id=1, source_target_pairs={{0,2},{1,3},{2,0},{3,1},{4,6},{5,7},{6,4},{7,5},{8,10},{9,11},{10,... | collective-permute-start | bytes 1376264 | tf_op jit(solution)/shard_map/ppermute | solution.py:897
  68.6 26.1 %collective-permute-start.8 = (f32[4,32,896]{2,1,0:T(8,128)S(1)}, f32[4,32,896]{2,1,0:T(8,128)S(1)}, u32[]{:S(2)}, u32[]{:S(2)}) collective-permute-start(f32[4,32,896]{2,1,0:T(8,128)S(1)} %bitcast.576), channel_id=1, source_target_pairs={{0,4},{1,5},{2,6},{3,7},{4,0},{5,1},{6,2},{7,3},{8,12},{9,13},{10,... | collective-permute-start | bytes 1376264 | tf_op jit(solution)/shard_map/ppermute | solution.py:897
  68.7 26.0 %collective-permute-start.10 = (bf16[32,768]{1,0:T(8,128)(2,1)S(1)}, bf16[32,768]{1,0:T(8,128)(2,1)S(1)}, u32[]{:S(2)}, u32[]{:S(2)}) collective-permute-start(bf16[32,768]{1,0:T(8,128)(2,1)S(1)} %bitcast.729), channel_id=1, source_target_pairs={{0,4},{1,5},{2,6},{3,7},{4,0},{5,1},{6,2},{7,3},{8,12},{9,13},{10,... | collective-permute-start | bytes 147464 | tf_op jit(solution)/shard_map/ppermute | solution.py:892
  71.1 23.7 %collective-permute-start.11 = (bf16[32,768]{1,0:T(8,128)(2,1)S(1)}, bf16[32,768]{1,0:T(8,128)(2,1)S(1)}, u32[]{:S(2)}, u32[]{:S(2)}) collective-permute-start(bf16[32,768]{1,0:T(8,128)(2,1)S(1)} %bitcast.730), channel_id=1, source_target_pairs={{0,6},{1,7},{2,0},{3,1},{4,2},{5,3},{6,4},{7,5},{8,14},{9,15},{10,... | collective-permute-start | bytes 147464 | tf_op jit(solution)/shard_map/ppermute | solution.py:892
  72.3 22.4 %collective-permute-start.9 = (bf16[32,768]{1,0:T(8,128)(2,1)S(1)}, bf16[32,768]{1,0:T(8,128)(2,1)S(1)}, u32[]{:S(2)}, u32[]{:S(2)}) collective-permute-start(bf16[32,768]{1,0:T(8,128)(2,1)S(1)} %bitcast.731), channel_id=1, source_target_pairs={{0,2},{1,3},{2,4},{3,5},{4,6},{5,7},{6,0},{7,1},{8,10},{9,11},{10,... | collective-permute-start | bytes 147464 | tf_op jit(solution)/shard_map/ppermute | solution.py:892
  108.4 23.2 %collective-permute-start.14 = (bf16[4,4,96,768]{3,2,1,0:T(8,128)(2,1)}, bf16[4,4,96,768]{3,2,1,0:T(8,128)(2,1)}, u32[]{:S(2)}, u32[]{:S(2)}) collective-permute-start(bf16[4,4,96,768]{3,2,1,0:T(8,128)(2,1)} %get-tuple-element.440), channel_id=1, source_target_pairs={{0,1},{1,0},{2,3},{3,2},{4,5},{5,4},{6,7},{7,6},{8,9},{9,8},{10,11... | collective-permute-start | bytes 7077896 | tf_op jit(solution)/shard_map/ppermute | solution.py:897
  143.6 14.5 %collective-permute-start.15 = (bf16[3,4,96,768]{3,2,1,0:T(8,128)(2,1)}, bf16[3,4,96,768]{3,2,1,0:T(8,128)(2,1)}, u32[]{:S(2)}, u32[]{:S(2)}) collective-permute-start(bf16[3,4,96,768]{3,2,1,0:T(8,128)(2,1)} %get-tuple-element.444), channel_id=1, source_target_pairs={{0,1},{1,0},{2,3},{3,2},{4,5},{5,4},{6,7},{7,6},{8,9},{9,8},{10,11... | collective-permute-start | bytes 5308424 | tf_op jit(solution)/shard_map/ppermute | solution.py:897
  148.7 27.8 %collective-permute-start.17 = (bf16[4,4,2,24,768]{4,3,1,0,2:T(8,128)(2,1)}, bf16[4,4,2,24,768]{4,3,1,0,2:T(8,128)(2,1)}, u32[]{:S(2)}, u32[]{:S(2)}) collective-permute-start(bf16[4,4,2,24,768]{4,3,1,0,2:T(8,128)(2,1)} %fusion.24), channel_id=1, source_target_pairs={{0,8},{8,0},{16,24},{24,16},{1,9},{9,1},{17,25},{25,17},{2,10},{10... | collective-permute-start | bytes 3538952 | tf_op jit(solution)/shard_map/ppermute | solution.py:897
  161.4 34.7 %collective-permute-start.18 = (bf16[3,2,96,768]{3,2,1,0:T(8,128)(2,1)}, bf16[3,2,96,768]{3,2,1,0:T(8,128)(2,1)}, u32[]{:S(2)}, u32[]{:S(2)}) collective-permute-start(bf16[3,2,96,768]{3,2,1,0:T(8,128)(2,1)} %get-tuple-element.442), channel_id=1, source_target_pairs={{0,2},{1,3},{2,0},{3,1},{4,6},{5,7},{6,4},{7,5},{8,10},{9,11},{10,... | collective-permute-start | bytes 2654216 | tf_op jit(solution)/shard_map/ppermute | solution.py:897
  178.7 17.4 %collective-permute-start.19 = (bf16[2,4,2,24,768]{4,3,1,0,2:T(8,128)(2,1)}, bf16[2,4,2,24,768]{4,3,1,0,2:T(8,128)(2,1)}, u32[]{:S(2)}, u32[]{:S(2)}) collective-permute-start(bf16[2,4,2,24,768]{4,3,1,0,2:T(8,128)(2,1)} %fusion.50), channel_id=1, source_target_pairs={{0,8},{8,0},{16,24},{24,16},{1,9},{9,1},{17,25},{25,17},{2,10},{10... | collective-permute-start | bytes 1769480 | tf_op jit(solution)/shard_map/ppermute | solution.py:897
  190.2 13.9 %collective-permute-start.20 = (bf16[4,4,24,768]{3,2,1,0:T(8,128)(2,1)}, bf16[4,4,24,768]{3,2,1,0:T(8,128)(2,1)S(1)}, u32[]{:S(2)}, u32[]{:S(2)}) collective-permute-start(bf16[4,4,24,768]{3,2,1,0:T(8,128)(2,1)} %get-tuple-element.446), channel_id=1, source_target_pairs={{0,16},{8,24},{16,0},{24,8},{1,17},{9,25},{17,1},{25,9},{2,18},{10... | collective-permute-start | bytes 1769480 | tf_op jit(solution)/shard_map/ppermute | solution.py:897
  191.5 31.5 %collective-permute-start.24 = (bf16[6,84,768]{2,1,0:T(8,128)(2,1)S(1)}, bf16[6,84,768]{2,1,0:T(8,128)(2,1)S(1)}, u32[]{:S(2)}, u32[]{:S(2)}) collective-permute-start(bf16[6,84,768]{2,1,0:T(8,128)(2,1)S(1)} %get-tuple-element.325), channel_id=1, source_target_pairs={{0,1},{1,2},{2,3},{3,4},{4,5},{5,6},{6,7},{7,0},{8,9},{9,10},{10,1... | collective-permute-start | bytes 2322440 | tf_op jit(solution)/shard_map/ppermute | solution.py:892
  197.3 25.7 %collective-permute-start.22 = (bf16[2,4,24,768]{3,2,1,0:T(8,128)(2,1)S(1)}, bf16[2,4,24,768]{3,2,1,0:T(8,128)(2,1)S(1)}, u32[]{:S(2)}, u32[]{:S(2)}) collective-permute-start(bf16[2,4,24,768]{3,2,1,0:T(8,128)(2,1)S(1)} %get-tuple-element.466), channel_id=1, source_target_pairs={{0,16},{8,24},{16,0},{24,8},{1,17},{9,25},{17,1},{25,9},{2,18},{10... | collective-permute-start | bytes 884744 | tf_op jit(solution)/shard_map/ppermute | solution.py:897
  198.8 24.3 %collective-permute-start.21 = (bf16[3,2,2,24,768]{4,3,2,1,0:T(8,128)(2,1)S(1)}, bf16[3,2,2,24,768]{4,3,2,1,0:T(8,128)(2,1)S(1)}, u32[]{:S(2)}, u32[]{:S(2)}) collective-permute-start(bf16[3,2,2,24,768]{4,3,2,1,0:T(8,128)(2,1)S(1)} %fusion.54), channel_id=1, source_target_pairs={{0,8},{8,0},{16,24},{24,16},{1,9},{9,1},{17,25},{25,17},{2,10},{10... | collective-permute-start | bytes 1327112 | tf_op jit(solution)/shard_map/ppermute | solution.py:897
  204.3 18.7 %collective-permute-start.23 = (bf16[2,4,24,768]{3,2,1,0:T(8,128)(2,1)S(1)}, bf16[2,4,24,768]{3,2,1,0:T(8,128)(2,1)S(1)}, u32[]{:S(2)}, u32[]{:S(2)}) collective-permute-start(bf16[2,4,24,768]{3,2,1,0:T(8,128)(2,1)S(1)} %get-tuple-element.468), channel_id=1, source_target_pairs={{0,2},{1,3},{2,0},{3,1},{4,6},{5,7},{6,4},{7,5},{8,10},{9,11},{10,... | collective-permute-start | bytes 884744 | tf_op jit(solution)/shard_map/ppermute | solution.py:897
  205.4 29.8 %collective-permute-start.25 = (bf16[9,2,24,768]{3,2,0,1:T(8,128)(2,1)S(1)}, bf16[9,2,24,768]{3,2,0,1:T(8,128)(2,1)S(1)}, u32[]{:S(2)}, u32[]{:S(2)}) collective-permute-start(bf16[9,2,24,768]{3,2,0,1:T(8,128)(2,1)S(1)} %copy_bitcast_fusion.2), channel_id=1, source_target_pairs={{0,8},{8,0},{16,24},{24,16},{1,9},{9,1},{17,25},{25,17},{2,10},{10... | collective-permute-start | bytes 1990664 | tf_op jit(solution)/shard_map/ppermute | solution.py:897
  231.3 23.0 %collective-permute-start.29 = (bf16[2,2,24,768]{3,2,0,1:T(8,128)(2,1)S(1)}, bf16[2,2,24,768]{3,2,0,1:T(8,128)(2,1)S(1)}, u32[]{:S(2)}, u32[]{:S(2)}) collective-permute-start(bf16[2,2,24,768]{3,2,0,1:T(8,128)(2,1)S(1)} %fusion.88), channel_id=1, source_target_pairs={{0,2},{1,3},{2,0},{3,1},{4,6},{5,7},{6,4},{7,5},{8,10},{9,11},{10,... | collective-permute-start | bytes 442376 | tf_op jit(solution)/shard_map/ppermute | solution.py:897
  232.0 22.4 %collective-permute-start.30 = (bf16[1,4,24,768]{3,2,1,0:T(8,128)(2,1)S(1)}, bf16[1,4,24,768]{3,2,1,0:T(8,128)(2,1)S(1)}, u32[]{:S(2)}, u32[]{:S(2)}) collective-permute-start(bf16[1,4,24,768]{3,2,1,0:T(8,128)(2,1)S(1)} %fusion.74), channel_id=1, source_target_pairs={{0,4},{1,5},{2,6},{3,7},{4,0},{5,1},{6,2},{7,3},{8,12},{9,13},{10,... | collective-permute-start | bytes 442376 | tf_op jit(solution)/shard_map/ppermute | solution.py:897
  235.4 19.0 %collective-permute-start.28 = (bf16[360,768]{1,0:T(8,128)(2,1)S(1)}, bf16[360,768]{1,0:T(8,128)(2,1)S(1)}, u32[]{:S(2)}, u32[]{:S(2)}) collective-permute-start(bf16[360,768]{1,0:T(8,128)(2,1)S(1)} %pad_maximum_fusion.9), channel_id=1, source_target_pairs={{0,16},{8,24},{16,0},{24,8},{1,17},{9,25},{17,1},{25,9},{2,18},{10... | collective-permute-start | bytes 1658888 | tf_op jit(solution)/shard_map/ppermute | solution.py:897
  236.8 17.6 %collective-permute-start.27 = (bf16[4,3,2,24,384]{4,3,2,1,0:T(8,128)(2,1)S(1)}, bf16[4,3,2,24,384]{4,3,2,1,0:T(8,128)(2,1)S(1)}, u32[]{:S(2)}, u32[]{:S(2)}) collective-permute-start(bf16[4,3,2,24,384]{4,3,2,1,0:T(8,128)(2,1)S(1)} %fusion.57), channel_id=1, source_target_pairs={{0,8},{8,0},{16,24},{24,16},{1,9},{9,1},{17,25},{25,17},{2,10},{10... | collective-permute-start | bytes 1327112 | tf_op jit(solution)/shard_map/ppermute | solution.py:897
  262.5 14.0 %collective-permute-start.36 = (bf16[120,768]{1,0:T(8,128)(2,1)S(1)}, bf16[120,768]{1,0:T(8,128)(2,1)S(1)}, u32[]{:S(2)}, u32[]{:S(2)}) collective-permute-start(bf16[120,768]{1,0:T(8,128)(2,1)S(1)} %pad_maximum_fusion.24), channel_id=1, source_target_pairs={{0,4},{1,5},{2,6},{3,7},{4,0},{5,1},{6,2},{7,3},{8,12},{9,13},{10,... | collective-permute-start | bytes 552968 | tf_op jit(solution)/shard_map/ppermute | solution.py:897
  265.1 19.6 %collective-permute-start.35 = (bf16[4,3,2,24,384]{4,3,2,1,0:T(8,128)(2,1)S(1)}, bf16[4,3,2,24,384]{4,3,2,1,0:T(8,128)(2,1)S(1)}, u32[]{:S(2)}, u32[]{:S(2)}) collective-permute-start(bf16[4,3,2,24,384]{4,3,2,1,0:T(8,128)(2,1)S(1)} %fusion.58), channel_id=1, source_target_pairs={{0,8},{8,0},{16,24},{24,16},{1,9},{9,1},{17,25},{25,17},{2,10},{10... | collective-permute-start | bytes 1327112 | tf_op jit(solution)/shard_map/ppermute | solution.py:897
  285.3 17.8 %collective-permute-start.41 = (bf16[576,384]{1,0:T(8,128)(2,1)S(1)}, bf16[576,384]{1,0:T(8,128)(2,1)S(1)}, u32[]{:S(2)}, u32[]{:S(2)}) collective-permute-start(bf16[576,384]{1,0:T(8,128)(2,1)S(1)} %pad_maximum_fusion.13), channel_id=1, source_target_pairs={{0,16},{8,24},{16,0},{24,8},{1,17},{9,25},{17,1},{25,9},{2,18},{10... | collective-permute-start | bytes 1327112 | tf_op jit(solution)/shard_map/ppermute | solution.py:897
  303.4 14.0 %collective-permute-start.42 = (bf16[4,6,32,384]{3,2,1,0:T(8,128)(2,1)S(1)}, bf16[4,6,32,384]{3,2,1,0:T(8,128)(2,1)S(1)}, u32[]{:S(2)}, u32[]{:S(2)}) collective-permute-start(bf16[4,6,32,384]{3,2,1,0:T(8,128)(2,1)S(1)} %bitcast.605), channel_id=1, source_target_pairs={{0,1},{1,0},{2,3},{3,2},{4,5},{5,4},{6,7},{7,6},{8,9},{9,8},{10,11... | collective-permute-start | bytes 1769480 | tf_op jit(solution)/shard_map/ppermute | solution.py:897
  304.2 21.5 %collective-permute-start.50 = (bf16[6,84,768]{2,1,0:T(8,128)(2,1)S(1)}, bf16[6,84,768]{2,1,0:T(8,128)(2,1)S(1)}, u32[]{:S(2)}, u32[]{:S(2)}) collective-permute-start(bf16[6,84,768]{2,1,0:T(8,128)(2,1)S(1)} %get-tuple-element.409), channel_id=1, source_target_pairs={{0,1},{1,2},{2,3},{3,4},{4,5},{5,6},{6,7},{7,0},{8,9},{9,10},{10,1... | collective-permute-start | bytes 2322440 | tf_op jit(solution)/shard_map/ppermute | solution.py:892
  305.2 15.1 %collective-permute-start.48 = (bf16[120,768]{1,0:T(8,128)(2,1)S(1)}, bf16[120,768]{1,0:T(8,128)(2,1)S(1)}, u32[]{:S(2)}, u32[]{:S(2)}) collective-permute-start(bf16[120,768]{1,0:T(8,128)(2,1)S(1)} %pad_maximum_fusion.25), channel_id=1, source_target_pairs={{0,8},{8,0},{16,24},{24,16},{1,9},{9,1},{17,25},{25,17},{2,10},{10... | collective-permute-start | bytes 552968 | tf_op jit(solution)/shard_map/ppermute | solution.py:897
  305.8 18.5 %collective-permute-start.46 = (bf16[288,384]{1,0:T(8,128)(2,1)S(1)}, bf16[288,384]{1,0:T(8,128)(2,1)S(1)}, u32[]{:S(2)}, u32[]{:S(2)}) collective-permute-start(bf16[288,384]{1,0:T(8,128)(2,1)S(1)} %pad_maximum_fusion.17), channel_id=1, source_target_pairs={{0,2},{1,3},{2,0},{3,1},{4,6},{5,7},{6,4},{7,5},{8,10},{9,11},{10,... | collective-permute-start | bytes 663560 | tf_op jit(solution)/shard_map/ppermute | solution.py:897
  331.9 19.9 %collective-permute-start.57 = (bf16[432,768]{1,0:T(8,128)(2,1)S(1)}, bf16[432,768]{1,0:T(8,128)(2,1)S(1)}, u32[]{:S(2)}, u32[]{:S(2)}) collective-permute-start(bf16[432,768]{1,0:T(8,128)(2,1)S(1)} %pad_maximum_fusion.5), channel_id=1, source_target_pairs={{0,16},{8,24},{16,0},{24,8},{1,17},{9,25},{17,1},{25,9},{2,18},{10... | collective-permute-start | bytes 1990664 | tf_op jit(solution)/shard_map/ppermute | solution.py:897
  336.8 19.4 %collective-permute-start.54 = (bf16[288,384]{1,0:T(8,128)(2,1)S(1)}, bf16[288,384]{1,0:T(8,128)(2,1)S(1)}, u32[]{:S(2)}, u32[]{:S(2)}) collective-permute-start(bf16[288,384]{1,0:T(8,128)(2,1)S(1)} %pad_maximum_fusion.18), channel_id=1, source_target_pairs={{0,8},{8,0},{16,24},{24,16},{1,9},{9,1},{17,25},{25,17},{2,10},{10... | collective-permute-start | bytes 663560 | tf_op jit(solution)/shard_map/ppermute | solution.py:897
  338.0 18.2 %collective-permute-start.55 = (bf16[288,384]{1,0:T(8,128)(2,1)S(1)}, bf16[288,384]{1,0:T(8,128)(2,1)S(1)}, u32[]{:S(2)}, u32[]{:S(2)}) collective-permute-start(bf16[288,384]{1,0:T(8,128)(2,1)S(1)} %pad_maximum_fusion.18), channel_id=1, source_target_pairs={{0,16},{8,24},{16,0},{24,8},{1,17},{9,25},{17,1},{25,9},{2,18},{10... | collective-permute-start | bytes 663560 | tf_op jit(solution)/shard_map/ppermute | solution.py:897
  338.0 18.2 %collective-permute-start.56 = (bf16[288,384]{1,0:T(8,128)(2,1)S(1)}, bf16[288,384]{1,0:T(8,128)(2,1)S(1)}, u32[]{:S(2)}, u32[]{:S(2)}) collective-permute-start(bf16[288,384]{1,0:T(8,128)(2,1)S(1)} %pad_maximum_fusion.18), channel_id=1, source_target_pairs={{0,24},{8,16},{16,8},{24,0},{1,25},{9,17},{17,9},{25,1},{2,26},{10... | collective-permute-start | bytes 663560 | tf_op jit(solution)/shard_map/ppermute | solution.py:897
  (119 other events, 819.3 us)

commit v2 on v1

--- a/solution.py
+++ b/solution.py
@@ -53,6 +53,11 @@
 
 def whole(shape):
     return pl.BlockSpec(shape, lambda *_: (0,) * len(shape))
+
+
+def once(shape, place=None):
+    place = place or (lambda *_: (0,) * len(shape))
+    return pl.BlockSpec(shape, place, pipeline_mode=pl.Buffered(1))
 
 
 def normalised(values):
@@ -698,9 +703,9 @@
         functools.partial(ffn_forward_kernel, stream),
         grid=(hidden // chunk,),
         in_specs=[
-            whole((rows, width)),
-            whole((rows, width)),
-            pl.BlockSpec((None, width, width), lambda f: (stream, 0, 0)),
+            once((rows, width)),
+            once((rows, width)),
+            once((None, width, width), lambda f: (stream, 0, 0)),
             whole(out_b.shape),
             whole(gain.shape),
             whole(bias.shape),
@@ -724,7 +729,7 @@
             jax.ShapeDtypeStruct((rows, width), bf16),
         ],
         scratch_shapes=[pltpu.VMEM((rows, width), f32)],
-        compiler_params=params(44),
+        compiler_params=params(34 if stream == 0 else 56),
         cost_estimate=cost(
             2 * rows * width * (2 * hidden + width),
             4 * width * hidden + 4 * rows * hidden + 12 * rows * width,
@@ -803,12 +808,12 @@
         functools.partial(ffn_backward_kernel, stream),
         grid=(hidden // chunk,),
         in_specs=[
-            whole((rows, width)),
+            once((rows, width)),
             pl.BlockSpec((rows, chunk), lambda f: (0, f)),
-            whole((rows, width)),
+            once((rows, width)),
             pl.BlockSpec((None, chunk, width), lambda f: (stream, f, 0)),
             pl.BlockSpec((None, width, chunk), lambda f: (stream, 0, f)),
-            pl.BlockSpec((None, width, width), lambda f: (stream, 0, 0)),
+            once((None, width, width), lambda f: (stream, 0, 0)),
             whole(gain.shape),
         ],
         out_specs=[
@@ -826,7 +831,7 @@
             jax.ShapeDtypeStruct((4 + hidden // chunk, width), f32),
         ],
         scratch_shapes=[pltpu.VMEM((rows, width), f32)],
-        compiler_params=params(44),
+        compiler_params=params(34 if stream == 0 else 56),
         cost_estimate=cost(
             2 * rows * width * (2 * hidden + width),
             4 * width * hidden + 4 * rows * hidden + 14 * rows * width,
@@ -1376,10 +1381,12 @@
     (second,) = second.terms()
     second = Phase([mapped(by_page, second)], [3], "page", 1)
     (down,) = down.sums()
-    early = Gather([after(added(one), second.sent), down[0]], [1, 1], "page", 1)
+    one = after(added(one), second.sent)
+    early = Gather([one[:5], down[0]], [1, 1], "page", 1)
+    early_y = Gather([one[5:]], [1], "page", 2)
 
     made = input_grad(
-        after(back_two[0], part.sent, line.sent, second.sent, early.sent),
+        after(back_two[0], part.sent, line.sent, second.sent, early.sent, early_y.sent),
         back_two[1],
         back_two[2],
         qkv_weight,
@@ -1416,11 +1423,12 @@
         norm1_gain,
         1,
     )
-    made, lined.got, early.got = beside(made, lined.got, early.got)
+    made, lined.got, early.got, early_y.got = beside(made, lined.got, early.got, early_y.got)
     own_input, own_head = made
     lined = lined.pairs()[0].reshape((-1,) + own_dqkv.shape)
     lined = Gather([lined], [1], "strip", masks[0])
     one, down = after(early.pairs(), lined.sent)
+    (one_b,) = after(early_y.pairs(), lined.sent)
     down = Gather([down], [1], "page", 2)
 
     small = jnp.concatenate([vis_sums, vis_head + own_head], 0)
@@ -1429,15 +1437,15 @@
     small = small + small_others
     lined = lined.pairs()[0].reshape((-1,) + own_dqkv.shape)
     lined_others = other_core(lined)
-    grad_first = moved(after(grad_send, lined), "strip", 1)
     for mask in masks[:-2]:
         small = small + swapped(small, "strip", mask)
     small_others = swapped(small, "strip", masks[-2])
     qkv = line_first(after(qkv.terms(), lined), [0, 0])
     up_part, low_part = line.sums()
     up_gather = Gather([after(up_part, lined)[:, 0], low_part[:, 0]], [1, 1], "page", 1)
+    grad_near = moved(after(grad_send[: SHIFT // 2], lined), "strip", 1)
     lined_others, small_others, down.got = beside(lined_others, small_others, down.got)
-    one_first = Gather([after(one, down.got)[:5]], [1], "page", 2)
+    one_first = Gather([after(one, down.got)], [1], "page", 2)
     small = small + small_others
     query_dqkv = jnp.stack(
         [jnp.where(core == 0, lined, lined_others), jnp.where(core == 0, lined_others, lined)], 1
@@ -1446,21 +1454,21 @@
     three = query_grads(query_norm, jnp.concatenate(query_dqkv, 1))
     three = Phase([[by_page(tiled(three, half * PAIR))]], [2], "page", 1)
     small_others = swapped(small, "strip", masks[-1])
-    three.got, qkv.got, small_others, up_gather.got, one_first.got, grad_first = beside(
-        three.got, qkv.got, small_others, up_gather.got, one_first.got, grad_first
+    three.got, qkv.got, small_others, up_gather.got, one_first.got, grad_near = beside(
+        three.got, qkv.got, small_others, up_gather.got, one_first.got, grad_near
     )
     three = Phase(three.terms(), [1], "page", 2)
     qkv = line_last(after(qkv.terms(), three.sent), [0, 0])
     small = jnp.concatenate([small + small_others, query_sums], 0)
-    small_others = swapped(small, "page", 2)
-    last = Gather([after(one, three.sent)[5:]] + up_gather.pairs(), [1, 1, 1], "page", 2)
-    three.got, qkv.got, small_others = beside(three.got, qkv.got, small_others)
-    late = PageGather([each[0] for each in qkv.sums()] + three.sums())
-    small = small + small_others
-    small_others = swapped(after(small, late.sent), "page", 1)
-    small = small + small_others
-
-    one_last, up_a, up_b = [from_page(each) for each in last.pairs()]
+    last = Gather(after(up_gather.pairs(), three.sent), [1, 1], "page", 2)
+    one_last = Gather([after(one_b, three.sent)], [2], "page", 1)
+    three.got, qkv.got, small = beside(three.got, qkv.got, small)
+    grad_far = moved(after(grad_send[SHIFT // 2 :], three.got), "strip", 1)
+    small = tiled(small.astype(bf16), half * PAIR)
+    late = PageGather([each[0] for each in qkv.sums()] + three.sums() + [small])
+
+    up_a, up_b = [from_page(each) for each in last.pairs()]
+    (one_last,) = [from_page(each) for each in one_last.pairs()]
     (down,) = [from_page(each) for each in down.pairs()]
     one = jnp.concatenate([from_page(each) for each in one_first.pairs()] + [one_last], 0)
     up = jnp.concatenate([up_a, up_b], 0)
@@ -1468,11 +1476,14 @@
     out_grad = jnp.stack([up[hidden], one[hidden]]).astype(f32)
     down_grad = jnp.stack([down, one[hidden + 1 :]]).astype(f32).reshape(2, -1, features)
     vis_final = jnp.concatenate([vis_first, vis_keep], 0)[None]
-    grad_final = jnp.concatenate([grad_first, grad_keep], 0)[None]
+    grad_final = jnp.concatenate([grad_near, grad_far, grad_keep], 0)[None]
     late.got, up_grad, out_grad, down_grad, vis_final, grad_final = beside(
         late.got, up_grad, out_grad, down_grad, vis_final, grad_final
     )
-    first, second, three = late.whole()
+    first, second, three, small = late.whole()
+    tiles, rows, span = small.shape
+    pages = lax.axis_size("page")
+    small = untiled(small.reshape(tiles, pages, rows // pages, span).astype(f32).sum(1))
     vis_qkv_grad = jnp.concatenate(
         [each[i] for i in range(3) for each in (first, second)], 1
     )

time: 362 us -> 350 us (0.967)
  the two profiles are of different devices: /device:TPU:1 before, /device:TPU:0 now
where the time goes in v2:
time: 350 us; the launch traced here: 344 us
  Pallas kernels  131 us (37%)
  starting transfers between devices  57.8 us (17%)
  waiting for transfers between devices  51.9 us (15%)
  local copies, waits for them, and re-layouts  38.2 us (11%)
  other arithmetic  38 us (11%)
  matrix products  22.9 us (7%)
  between operations  4.44 us (1%)
    ppermute x49, waiting for transfers between devices, swapped(): return lax.ppermute(block, axis, [(i, i ^ mask) for i in range(size)])  43.6 us
    ppermute x49, starting transfers between devices, swapped(): return lax.ppermute(block, axis, [(i, i ^ mask) for i in range(size)])  38.4 us
    pallas_call x2, Pallas kernels, attention_backward(): pl.pallas_call(functools.partial(attention_backward_kernel, windows, firs...  32 us
    pallas_call x2, Pallas kernels, ffn_forward(): pl.pallas_call(functools.partial(ffn_forward_kernel, stream), grid=(hidde...  26.9 us
    pallas_call x2, Pallas kernels, ffn_backward(): pl.pallas_call(functools.partial(ffn_backward_kernel, stream), grid=(hidd...  26.8 us
    dot_general x19, matrix products, dot_tn(): lax.dot_general(a, b, (((0,), (0,)), ((), ())), preferred_element_type=f32)  22.9 us
    unnamed x238, local copies, waits for them, and re-layouts  21.3 us
    convert_element_type x41, other arithmetic, added(): return total.astype(kind)  20.6 us
  transfers between devices with their start and end apart: 60, of which 15 were waited for; matrix products, arithmetic and copies ran while one was open for 18% of the time, Pallas kernels for 36%

profile of v2, /device:TPU:0, one launch (start us, length us, event | category | flops | bytes accessed | tf_op | source)
XLA Modules:
  0.0 344.0 jit_solution(4208085402194910362)
XLA Ops:
  0.7 5.1 %collective-permute-start = (bf16[32,768]{1,0:T(8,128)(2,1)}, bf16[32,768]{1,0:T(8,128)(2,1)S(1)}, u32[]{:S(2)}, u32[]{:S(2)}) collective-permute-start(bf16[32,768]{1,0:T(8,128)(2,1)} %bitcast.622), channel_id=1, source_target_pairs={{0,6},{1,7},{2,0},{3,1},{4,2},{5,3},{6,4},{7,5},{8,14},{9,15},{10,... | collective-permute-start | bytes 147464 | tf_op jit(solution)/shard_map/ppermute | solution.py:897
  15.2 3.1 copy-done.2
  22.9 4.0 %collective-permute-start.5 = (bf16[6,84,768]{2,1,0:T(8,128)(2,1)S(1)}, bf16[6,84,768]{2,1,0:T(8,128)(2,1)S(1)}, u32[]{:S(2)}, u32[]{:S(2)}) collective-permute-start(bf16[6,84,768]{2,1,0:T(8,128)(2,1)S(1)} %copy-done.71), channel_id=1, source_target_pairs={{0,7},{1,0},{2,1},{3,2},{4,3},{5,4},{6,5},{7,6},{8,15},{9,8},{10,9... | collective-permute-start | bytes 2322440 | tf_op jit(solution)/shard_map/ppermute | solution.py:897
  27.1 5.2 %norm_qkv.3 = (bf16[1008,768]{1,0:T(8,128)(2,1)S(1)}, bf16[1008,2304]{1,0:T(8,128)(2,1)S(1)}) custom-call(bf16[1008,768]{1,0:T(8,128)(2,1)S(1)} %enter.2.x_ref, f32[2,768]{1,0:T(2,128)S(1)} %copy-done.49, f32[2,768]{1,0:T(2,128)S(1)} %copy-done.54, bf16[2,768,2304]{2,1,0:T(8,128)(2,1)S(1)} %bitcast.602), custom_call_target="tpu_custom_call" | custom-call | flops 178362 | bytes 564 | tf_op jit(solution)/shard_map/norm_qkv/pallas_call | solution.py:165
  33.5 9.1 %query_forward.1 = (f32[256,768]{1,0:T(8,128)S(1)}, f32[256,128]{1,0:T(8,128)S(1)}) custom-call(bf16[256,2304]{1,0:T(8,128)(2,1)S(1)} %get-tuple-element.236.qq_ref.kq_ref.vq_ref, bf16[1008,2304]{1,0:T(8,128)(2,1)S(1)} %get-tuple-element.340.k_ref.v_ref.q_ref, bf16[1008,2304]{1,0:T(8,128)(2,1)S(1)} %get-tuple-element.340.k_ref.v_ref.q_ref, ...), custom_call_target="tpu_custom_call" | custom-call | flops 81788 | bytes 154 | tf_op jit(solution)/shard_map/query_forward/pallas_call | solution.py:265
  53.8 11.7 %window_forward.1 = (bf16[1008,768]{1,0:T(8,128)(2,1)S(1)}, f32[6,1,2016]{2,1,0:T(1,128)S(1)}) custom-call(bf16[1008,2304]{1,0:T(8,128)(2,1)S(1)} %copy-done.1, bf16[1008,2304]{1,0:T(8,128)(2,1)S(1)} %copy-done.1, bf16[1008,2304]{1,0:T(8,128)(2,1)S(1)} %copy-done.1, bf16[256,2304]{1,0:T(8,128)(2,1)S(1)} %copy-done.4, bf16[256,2304]{1,0:T(8,128)(2,1)S(1)} %copy-done.4, ...), custom_call_target="tpu_custom_call" | custom-call | flops 123863 | bytes 309 | tf_op jit(solution)/shard_map/window_forward/pallas_call | solution.py:349
  66.1 2.5 merge.4
  73.8 16.9 %ffn_forward.2 = (f32[1008,768]{1,0:T(8,128)S(1)}, bf16[1008,768]{1,0:T(8,128)(2,1)S(1)}, bf16[1008,3072]{1,0:T(8,128)(2,1)S(1)}, bf16[1008,3072]{1,0:T(8,128)(2,1)}, bf16[1008,768]{1,0:T(8,128)(2,1)S(1)}) custom-call(bf16[1008,768]{1,0:T(8,128)(2,1)S(1)} %copy-done.8, bf16[1008,768]{1,0:T(8,128)(2,1)S(1)} %get-tuple-element.252.o_ref, ...), custom_call_target="tpu_custom_call" | custom-call | flops 535088 | bytes 1555 | tf_op jit(solution)/shard_map/ffn_forward/pallas_call | solution.py:702
  90.8 5.1 %collective-permute-done.10 = bf16[32,768]{1,0:T(8,128)(2,1)S(1)} collective-permute-done((bf16[32,768]{1,0:T(8,128)(2,1)S(1)}, bf16[32,768]{1,0:T(8,128)(2,1)S(1)}, u32[]{:S(2)}, u32[]{:S(2)}) %collective-permute-start.10) | collective-permute-done | bytes 49184 | tf_op jit(solution)/shard_map/ppermute | solution.py:897
  97.5 5.5 %convolution_convert_fusion = bf16[3072,768]{1,0:T(8,128)(2,1)S(1)} fusion(bf16[1008,3072]{1,0:T(8,128)(2,1)S(1)} %get-tuple-element.266, bf16[1008,768]{1,0:T(8,128)(2,1)S(1)} %copy-done.17), kind=kOutput, calls=%fused_computation.1 | convolution fusion | flops 4758700032 | bytes 12460032 | tf_op jit(solution)/shard_map/dot_general | solution.py:42
  103.1 2.5 constant_dynamic-slice_fusion.44
  109.6 16.6 %ffn_backward.2 = (bf16[4,1008,768]{2,1,0:T(8,128)(2,1)S(1)}, f32[1008,768]{1,0:T(8,128)S(1)}, bf16[1008,768]{1,0:T(8,128)(2,1)S(1)}, bf16[1008,768]{1,0:T(8,128)(2,1)S(1)}, f32[8,768]{1,0:T(8,128)S(1)}) custom-call(bf16[1008,768]{1,0:T(8,128)(2,1)S(1)} %copy-done.18, bf16[1008,3072]{1,0:T(8,128)(2,1)} %get-tuple-element.273.slope_ref, ...), custom_call_target="tpu_custom_call" | custom-call | flops 535088 | bytes 1633 | tf_op jit(solution)/shard_map/ffn_backward/pallas_call | solution.py:807
  127.9 3.3 fusion.24
  149.7 3.0 add_convert_fusion
  152.7 3.2 add_convert_fusion.2
  157.1 9.9 %ffn_forward.3 = (f32[256,768]{1,0:T(8,128)}, bf16[256,768]{1,0:T(8,128)(2,1)}, bf16[256,3072]{1,0:T(8,128)(2,1)}, bf16[256,3072]{1,0:T(8,128)(2,1)}, bf16[256,768]{1,0:T(8,128)(2,1)}) custom-call(bf16[256,768]{1,0:T(8,128)(2,1)} %bitcast.614, f32[256,896]{1,0:T(8,128)} %bitcast.605, bf16[2,768,768]{2,1,0:T(8,128)(2,1)} %wo_ref.7, f32[2,768]{1,0:T(2,128)} %bo_ref.3, ...), custom_call_target="tpu_custom_call" | custom-call | flops 135895 | bytes 747 | tf_op jit(solution)/shard_map/ffn_forward/pallas_call | solution.py:702
  167.0 5.1 %collective-permute-done.17 = bf16[4,4,2,24,768]{4,3,1,0,2:T(8,128)(2,1)} collective-permute-done((bf16[4,4,2,24,768]{4,3,1,0,2:T(8,128)(2,1)}, bf16[4,4,2,24,768]{4,3,1,0,2:T(8,128)(2,1)}, u32[]{:S(2)}, u32[]{:S(2)}) %collective-permute-start.17) | collective-permute-done | bytes 1179680 | tf_op jit(solution)/shard_map/ppermute | solution.py:902
  175.9 2.7 fusion.28
  178.6 10.2 %ffn_backward.3 = (bf16[4,256,768]{2,1,0:T(8,128)(2,1)}, f32[256,768]{1,0:T(8,128)}, bf16[256,768]{1,0:T(8,128)(2,1)}, bf16[256,768]{1,0:T(8,128)(2,1)}, f32[8,768]{1,0:T(8,128)}) custom-call(bf16[256,768]{1,0:T(8,128)(2,1)} %bitcast.645, bf16[256,3072]{1,0:T(8,128)(2,1)} %get-tuple-element.302.slope_ref, f32[256,768]{1,0:T(8,128)} %get-tuple-element.303.x1_ref, ...), custom_call_target="tpu_custom_call" | custom-call | flops 135895 | bytes 766 | tf_op jit(solution)/shard_map/ffn_backward/pallas_call | solution.py:807
  200.2 5.2 %collective-permute-done.20 = bf16[4,4,24,768]{3,2,1,0:T(8,128)(2,1)S(1)} collective-permute-done((bf16[4,4,24,768]{3,2,1,0:T(8,128)(2,1)}, bf16[4,4,24,768]{3,2,1,0:T(8,128)(2,1)S(1)}, u32[]{:S(2)}, u32[]{:S(2)}) %collective-permute-start.20) | collective-permute-done | bytes 589856 | tf_op jit(solution)/shard_map/ppermute | solution.py:902
  208.6 15.9 %attention_backward.2 = (bf16[1008,768]{1,0:T(8,128)(2,1)S(1)}, bf16[1008,768]{1,0:T(8,128)(2,1)S(1)}, bf16[1008,768]{1,0:T(8,128)(2,1)S(1)}, bf16[256,384]{1,0:...) custom-call(bf16[1008,2304]{1,0:T(8,128)(2,1)S(1)} %bitcast.600, ...), custom_call_target="tpu_custom_call" | custom-call | flops 253919 | bytes 270 | tf_op jit(solution)/shard_map/attention_backward/pallas_call | solution.py:572
  236.8 16.1 %attention_backward.3 = (bf16[1008,768]{1,0:T(8,128)(2,1)S(1)}, bf16[1008,768]{1,0:T(8,128)(2,1)S(1)}, bf16[1008,768]{1,0:T(8,128)(2,1)S(1)}, bf16[256,384]{1,0:...) custom-call(bf16[1008,2304]{1,0:T(8,128)(2,1)S(1)} %bitcast.600, ...), custom_call_target="tpu_custom_call", output_to_operand_aliasing={{0}: (17, {}), {1}: (18, {}), {2}: (19, {})} | custom-call | flops 253919 | bytes 270 | tf_op jit(solution)/shard_map/attention_backward/pallas_call | solution.py:572
  260.2 2.8 collective-permute-start.36
  263.9 5.7 %input_grad.2 = (bf16[1008,768]{1,0:T(8,128)(2,1)S(1)}, f32[8,768]{1,0:T(8,128)S(1)}) custom-call(bf16[1008,768]{1,0:T(8,128)(2,1)S(1)} %get-tuple-element.368.dq_ref, bf16[1008,768]{1,0:T(8,128)(2,1)S(1)} %get-tuple-element.358.dk_ref, bf16[1008,768]{1,0:T(8,128)(2,1)S(1)} %get-tuple-element.359.dv_ref, bf16[2,768,2304]{2,1,0:T(8,128)(2,1)S(1)} %bitcast.604, ...), custom_call_target="tpu_custom_call" | custom-call | flops 178362 | bytes 718 | tf_op jit(solution)/shard_map/input_grad/pallas_call | solution.py:866
  269.6 3.4 %collective-permute-done.33 = bf16[2,6,32,384]{3,2,1,0:T(8,128)(2,1)S(1)} collective-permute-done((bf16[2,6,32,384]{3,2,1,0:T(8,128)(2,1)S(1)}, bf16[2,6,32,384]{3,2,1,0:T(8,128)(2,1)S(1)}, u32[]{:S(2)}, u32[]{:S(2)}) %collective-permute-start.33) | collective-permute-done | bytes 294944 | tf_op jit(solution)/shard_map/ppermute | solution.py:902
  275.9 6.8 %collective-permute-done.34 = bf16[1,6,32,384]{3,2,1,0:T(8,128)(2,1)S(1)} collective-permute-done((bf16[1,6,32,384]{3,2,1,0:T(8,128)(2,1)S(1)}, bf16[1,6,32,384]{3,2,1,0:T(8,128)(2,1)S(1)}, u32[]{:S(2)}, u32[]{:S(2)}) %collective-permute-start.34) | collective-permute-done | bytes 147488 | tf_op jit(solution)/shard_map/ppermute | solution.py:902
  286.0 5.7 %collective-permute-done.37 = bf16[1,6,32,384]{3,2,1,0:T(8,128)(2,1)S(1)} collective-permute-done((bf16[1,6,32,384]{3,2,1,0:T(8,128)(2,1)S(1)}, bf16[1,6,32,384]{3,2,1,0:T(8,128)(2,1)S(1)}, u32[]{:S(2)}, u32[]{:S(2)}) %collective-permute-start.37) | collective-permute-done | bytes 147488 | tf_op jit(solution)/shard_map/ppermute | solution.py:902
  293.1 8.3 %collective-permute-done.40 = bf16[2,6,32,384]{3,2,1,0:T(8,128)(2,1)S(1)} collective-permute-done((bf16[2,6,32,384]{3,2,1,0:T(8,128)(2,1)S(1)}, bf16[2,6,32,384]{3,2,1,0:T(8,128)(2,1)S(1)}, u32[]{:S(2)}, u32[]{:S(2)}) %collective-permute-start.40) | collective-permute-done | bytes 294944 | tf_op jit(solution)/shard_map/ppermute | solution.py:902
  309.9 2.7 collective-permute-start.48
  312.7 3.5 %collective-permute-done.47 = bf16[288,384]{1,0:T(8,128)(2,1)S(1)} collective-permute-done((bf16[288,384]{1,0:T(8,128)(2,1)S(1)}, bf16[288,384]{1,0:T(8,128)(2,1)S(1)}, u32[]{:S(2)}, u32[]{:S(2)}) %collective-permute-start.47) | collective-permute-done | bytes 221216 | tf_op jit(solution)/shard_map/ppermute | solution.py:902
  327.8 2.8 collective-permute-start.59
  334.9 3.0 collective-permute-done.59
  (579 shorter events, 132.8 us)
Async XLA Ops:
  0.7 12.7 %collective-permute-start = (bf16[32,768]{1,0:T(8,128)(2,1)}, bf16[32,768]{1,0:T(8,128)(2,1)S(1)}, u32[]{:S(2)}, u32[]{:S(2)}) collective-permute-start(bf16[32,768]{1,0:T(8,128)(2,1)} %bitcast.622), channel_id=1, source_target_pairs={{0,6},{1,7},{2,0},{3,1},{4,2},{5,3},{6,4},{7,5},{8,14},{9,15},{10,... | collective-permute-start | bytes 147464 | tf_op jit(solution)/shard_map/ppermute | solution.py:897
  22.9 19.8 %collective-permute-start.5 = (bf16[6,84,768]{2,1,0:T(8,128)(2,1)S(1)}, bf16[6,84,768]{2,1,0:T(8,128)(2,1)S(1)}, u32[]{:S(2)}, u32[]{:S(2)}) collective-permute-start(bf16[6,84,768]{2,1,0:T(8,128)(2,1)S(1)} %copy-done.71), channel_id=1, source_target_pairs={{0,7},{1,0},{2,1},{3,2},{4,3},{5,4},{6,5},{7,6},{8,15},{9,8},{10,9... | collective-permute-start | bytes 2322440 | tf_op jit(solution)/shard_map/ppermute | solution.py:897
  48.6 17.5 %collective-permute-start.7 = (f32[4,32,896]{2,1,0:T(8,128)}, f32[4,32,896]{2,1,0:T(8,128)}, u32[]{:S(2)}, u32[]{:S(2)}) collective-permute-start(f32[4,32,896]{2,1,0:T(8,128)} %bitcast.21), channel_id=1, source_target_pairs={{0,2},{1,3},{2,0},{3,1},{4,6},{5,7},{6,4},{7,5},{8,10},{9,11},{10,... | collective-permute-start | bytes 1376264 | tf_op jit(solution)/shard_map/ppermute | solution.py:902
  68.6 27.3 %collective-permute-start.8 = (f32[4,32,896]{2,1,0:T(8,128)S(1)}, f32[4,32,896]{2,1,0:T(8,128)S(1)}, u32[]{:S(2)}, u32[]{:S(2)}) collective-permute-start(f32[4,32,896]{2,1,0:T(8,128)S(1)} %bitcast.618), channel_id=1, source_target_pairs={{0,4},{1,5},{2,6},{3,7},{4,0},{5,1},{6,2},{7,3},{8,12},{9,13},{10,... | collective-permute-start | bytes 1376264 | tf_op jit(solution)/shard_map/ppermute | solution.py:902
  69.6 26.2 %collective-permute-start.10 = (bf16[32,768]{1,0:T(8,128)(2,1)S(1)}, bf16[32,768]{1,0:T(8,128)(2,1)S(1)}, u32[]{:S(2)}, u32[]{:S(2)}) collective-permute-start(bf16[32,768]{1,0:T(8,128)(2,1)S(1)} %bitcast.773), channel_id=1, source_target_pairs={{0,4},{1,5},{2,6},{3,7},{4,0},{5,1},{6,2},{7,3},{8,12},{9,13},{10,... | collective-permute-start | bytes 147464 | tf_op jit(solution)/shard_map/ppermute | solution.py:897
  71.6 24.3 %collective-permute-start.11 = (bf16[32,768]{1,0:T(8,128)(2,1)S(1)}, bf16[32,768]{1,0:T(8,128)(2,1)S(1)}, u32[]{:S(2)}, u32[]{:S(2)}) collective-permute-start(bf16[32,768]{1,0:T(8,128)(2,1)S(1)} %bitcast.774), channel_id=1, source_target_pairs={{0,6},{1,7},{2,0},{3,1},{4,2},{5,3},{6,4},{7,5},{8,14},{9,15},{10,... | collective-permute-start | bytes 147464 | tf_op jit(solution)/shard_map/ppermute | solution.py:897
  73.1 22.7 %collective-permute-start.9 = (bf16[32,768]{1,0:T(8,128)(2,1)S(1)}, bf16[32,768]{1,0:T(8,128)(2,1)S(1)}, u32[]{:S(2)}, u32[]{:S(2)}) collective-permute-start(bf16[32,768]{1,0:T(8,128)(2,1)S(1)} %bitcast.775), channel_id=1, source_target_pairs={{0,2},{1,3},{2,4},{3,5},{4,6},{5,7},{6,0},{7,1},{8,10},{9,11},{10,... | collective-permute-start | bytes 147464 | tf_op jit(solution)/shard_map/ppermute | solution.py:897
  105.6 22.3 %collective-permute-start.14 = (bf16[4,4,96,768]{3,2,1,0:T(8,128)(2,1)}, bf16[4,4,96,768]{3,2,1,0:T(8,128)(2,1)}, u32[]{:S(2)}, u32[]{:S(2)}) collective-permute-start(bf16[4,4,96,768]{3,2,1,0:T(8,128)(2,1)} %get-tuple-element.448), channel_id=1, source_target_pairs={{0,1},{1,0},{2,3},{3,2},{4,5},{5,4},{6,7},{7,6},{8,9},{9,8},{10,11... | collective-permute-start | bytes 7077896 | tf_op jit(solution)/shard_map/ppermute | solution.py:902
  138.4 14.2 %collective-permute-start.15 = (bf16[3,4,96,768]{3,2,1,0:T(8,128)(2,1)}, bf16[3,4,96,768]{3,2,1,0:T(8,128)(2,1)}, u32[]{:S(2)}, u32[]{:S(2)}) collective-permute-start(bf16[3,4,96,768]{3,2,1,0:T(8,128)(2,1)} %get-tuple-element.452), channel_id=1, source_target_pairs={{0,1},{1,0},{2,3},{3,2},{4,5},{5,4},{6,7},{7,6},{8,9},{9,8},{10,11... | collective-permute-start | bytes 5308424 | tf_op jit(solution)/shard_map/ppermute | solution.py:902
  143.5 28.7 %collective-permute-start.17 = (bf16[4,4,2,24,768]{4,3,1,0,2:T(8,128)(2,1)}, bf16[4,4,2,24,768]{4,3,1,0,2:T(8,128)(2,1)}, u32[]{:S(2)}, u32[]{:S(2)}) collective-permute-start(bf16[4,4,2,24,768]{4,3,1,0,2:T(8,128)(2,1)} %fusion.24), channel_id=1, source_target_pairs={{0,8},{8,0},{16,24},{24,16},{1,9},{9,1},{17,25},{25,17},{2,10},{10... | collective-permute-start | bytes 3538952 | tf_op jit(solution)/shard_map/ppermute | solution.py:902
  155.8 39.0 %collective-permute-start.18 = (bf16[3,2,96,768]{3,2,1,0:T(8,128)(2,1)}, bf16[3,2,96,768]{3,2,1,0:T(8,128)(2,1)}, u32[]{:S(2)}, u32[]{:S(2)}) collective-permute-start(bf16[3,2,96,768]{3,2,1,0:T(8,128)(2,1)} %get-tuple-element.450), channel_id=1, source_target_pairs={{0,2},{1,3},{2,0},{3,1},{4,6},{5,7},{6,4},{7,5},{8,10},{9,11},{10,... | collective-permute-start | bytes 2654216 | tf_op jit(solution)/shard_map/ppermute | solution.py:902
  174.4 20.5 %collective-permute-start.19 = (bf16[2,4,2,24,768]{4,3,1,0,2:T(8,128)(2,1)}, bf16[2,4,2,24,768]{4,3,1,0,2:T(8,128)(2,1)}, u32[]{:S(2)}, u32[]{:S(2)}) collective-permute-start(bf16[2,4,2,24,768]{4,3,1,0,2:T(8,128)(2,1)} %fusion.50), channel_id=1, source_target_pairs={{0,8},{8,0},{16,24},{24,16},{1,9},{9,1},{17,25},{25,17},{2,10},{10... | collective-permute-start | bytes 1769480 | tf_op jit(solution)/shard_map/ppermute | solution.py:902
  188.9 16.5 %collective-permute-start.20 = (bf16[4,4,24,768]{3,2,1,0:T(8,128)(2,1)}, bf16[4,4,24,768]{3,2,1,0:T(8,128)(2,1)S(1)}, u32[]{:S(2)}, u32[]{:S(2)}) collective-permute-start(bf16[4,4,24,768]{3,2,1,0:T(8,128)(2,1)} %get-tuple-element.454), channel_id=1, source_target_pairs={{0,16},{8,24},{16,0},{24,8},{1,17},{9,25},{17,1},{25,9},{2,18},{10... | collective-permute-start | bytes 1769480 | tf_op jit(solution)/shard_map/ppermute | solution.py:902
  190.4 35.3 %collective-permute-start.24 = (bf16[6,84,768]{2,1,0:T(8,128)(2,1)}, bf16[6,84,768]{2,1,0:T(8,128)(2,1)S(1)}, u32[]{:S(2)}, u32[]{:S(2)}) collective-permute-start(bf16[6,84,768]{2,1,0:T(8,128)(2,1)} %copy-done.60), channel_id=1, source_target_pairs={{0,1},{1,2},{2,3},{3,4},{4,5},{5,6},{6,7},{7,0},{8,9},{9,10},{10,1... | collective-permute-start | bytes 2322440 | tf_op jit(solution)/shard_map/ppermute | solution.py:897
  196.2 29.6 %collective-permute-start.22 = (bf16[2,4,24,768]{3,2,1,0:T(8,128)(2,1)S(1)}, bf16[2,4,24,768]{3,2,1,0:T(8,128)(2,1)S(1)}, u32[]{:S(2)}, u32[]{:S(2)}) collective-permute-start(bf16[2,4,24,768]{3,2,1,0:T(8,128)(2,1)S(1)} %get-tuple-element.474), channel_id=1, source_target_pairs={{0,16},{8,24},{16,0},{24,8},{1,17},{9,25},{17,1},{25,9},{2,18},{10... | collective-permute-start | bytes 884744 | tf_op jit(solution)/shard_map/ppermute | solution.py:902
  198.0 27.8 %collective-permute-start.21 = (bf16[3,2,2,24,768]{4,3,2,1,0:T(8,128)(2,1)S(1)}, bf16[3,2,2,24,768]{4,3,2,1,0:T(8,128)(2,1)S(1)}, u32[]{:S(2)}, u32[]{:S(2)}) collective-permute-start(bf16[3,2,2,24,768]{4,3,2,1,0:T(8,128)(2,1)S(1)} %fusion.54), channel_id=1, source_target_pairs={{0,8},{8,0},{16,24},{24,16},{1,9},{9,1},{17,25},{25,17},{2,10},{10... | collective-permute-start | bytes 1327112 | tf_op jit(solution)/shard_map/ppermute | solution.py:902
  205.6 20.2 %collective-permute-start.23 = (bf16[2,4,24,768]{3,2,1,0:T(8,128)(2,1)S(1)}, bf16[2,4,24,768]{3,2,1,0:T(8,128)(2,1)S(1)}, u32[]{:S(2)}, u32[]{:S(2)}) collective-permute-start(bf16[2,4,24,768]{3,2,1,0:T(8,128)(2,1)S(1)} %fusion.68), channel_id=1, source_target_pairs={{0,2},{1,3},{2,0},{3,1},{4,6},{5,7},{6,4},{7,5},{8,10},{9,11},{10,... | collective-permute-start | bytes 884744 | tf_op jit(solution)/shard_map/ppermute | solution.py:902
  206.9 26.4 %collective-permute-start.25 = (bf16[9,2,24,768]{3,2,0,1:T(8,128)(2,1)S(1)}, bf16[9,2,24,768]{3,2,0,1:T(8,128)(2,1)S(1)}, u32[]{:S(2)}, u32[]{:S(2)}) collective-permute-start(bf16[9,2,24,768]{3,2,0,1:T(8,128)(2,1)S(1)} %copy_bitcast_fusion.2), channel_id=1, source_target_pairs={{0,8},{8,0},{16,24},{24,16},{1,9},{9,1},{17,25},{25,17},{2,10},{10... | collective-permute-start | bytes 1990664 | tf_op jit(solution)/shard_map/ppermute | solution.py:902
  229.8 23.3 %collective-permute-start.29 = (bf16[2,2,24,768]{3,2,1,0:T(8,128)(2,1)S(1)}, bf16[2,2,24,768]{3,2,1,0:T(8,128)(2,1)S(1)}, u32[]{:S(2)}, u32[]{:S(2)}) collective-permute-start(bf16[2,2,24,768]{3,2,1,0:T(8,128)(2,1)S(1)} %fusion.88), channel_id=1, source_target_pairs={{0,2},{1,3},{2,0},{3,1},{4,6},{5,7},{6,4},{7,5},{8,10},{9,11},{10,... | collective-permute-start | bytes 442376 | tf_op jit(solution)/shard_map/ppermute | solution.py:902
  230.7 22.4 %collective-permute-start.30 = (bf16[1,4,24,768]{3,2,1,0:T(8,128)(2,1)S(1)}, bf16[1,4,24,768]{3,2,1,0:T(8,128)(2,1)S(1)}, u32[]{:S(2)}, u32[]{:S(2)}) collective-permute-start(bf16[1,4,24,768]{3,2,1,0:T(8,128)(2,1)S(1)} %fusion.74), channel_id=1, source_target_pairs={{0,4},{1,5},{2,6},{3,7},{4,0},{5,1},{6,2},{7,3},{8,12},{9,13},{10,... | collective-permute-start | bytes 442376 | tf_op jit(solution)/shard_map/ppermute | solution.py:902
  233.5 19.6 %collective-permute-start.28 = (bf16[360,768]{1,0:T(8,128)(2,1)S(1)}, bf16[360,768]{1,0:T(8,128)(2,1)S(1)}, u32[]{:S(2)}, u32[]{:S(2)}) collective-permute-start(bf16[360,768]{1,0:T(8,128)(2,1)S(1)} %pad_maximum_fusion.7), channel_id=1, source_target_pairs={{0,16},{8,24},{16,0},{24,8},{1,17},{9,25},{17,1},{25,9},{2,18},{10... | collective-permute-start | bytes 1658888 | tf_op jit(solution)/shard_map/ppermute | solution.py:902
  235.2 17.9 %collective-permute-start.27 = (bf16[4,3,2,24,384]{4,3,2,1,0:T(8,128)(2,1)S(1)}, bf16[4,3,2,24,384]{4,3,2,1,0:T(8,128)(2,1)S(1)}, u32[]{:S(2)}, u32[]{:S(2)}) collective-permute-start(bf16[4,3,2,24,384]{4,3,2,1,0:T(8,128)(2,1)S(1)} %fusion.57), channel_id=1, source_target_pairs={{0,8},{8,0},{16,24},{24,16},{1,9},{9,1},{17,25},{25,17},{2,10},{10... | collective-permute-start | bytes 1327112 | tf_op jit(solution)/shard_map/ppermute | solution.py:902
  259.6 13.4 %collective-permute-start.33 = (bf16[2,6,32,384]{3,2,1,0:T(8,128)(2,1)S(1)}, bf16[2,6,32,384]{3,2,1,0:T(8,128)(2,1)S(1)}, u32[]{:S(2)}, u32[]{:S(2)}) collective-permute-start(bf16[2,6,32,384]{3,2,1,0:T(8,128)(2,1)S(1)} %get-tuple-element.470), channel_id=1, source_target_pairs={{0,2},{1,3},{2,0},{3,1},{4,6},{5,7},{6,4},{7,5},{8,10},{9,11},{10,... | collective-permute-start | bytes 884744 | tf_op jit(solution)/shard_map/ppermute | solution.py:902
  260.2 15.6 %collective-permute-start.36 = (bf16[120,768]{1,0:T(8,128)(2,1)S(1)}, bf16[120,768]{1,0:T(8,128)(2,1)S(1)}, u32[]{:S(2)}, u32[]{:S(2)}) collective-permute-start(bf16[120,768]{1,0:T(8,128)(2,1)S(1)} %pad_maximum_fusion.24), channel_id=1, source_target_pairs={{0,4},{1,5},{2,6},{3,7},{4,0},{5,1},{6,2},{7,3},{8,12},{9,13},{10,... | collective-permute-start | bytes 552968 | tf_op jit(solution)/shard_map/ppermute | solution.py:902
  263.2 19.5 %collective-permute-start.35 = (bf16[4,3,2,24,384]{4,3,2,1,0:T(8,128)(2,1)S(1)}, bf16[4,3,2,24,384]{4,3,2,1,0:T(8,128)(2,1)S(1)}, u32[]{:S(2)}, u32[]{:S(2)}) collective-permute-start(bf16[4,3,2,24,384]{4,3,2,1,0:T(8,128)(2,1)S(1)} %fusion.58), channel_id=1, source_target_pairs={{0,8},{8,0},{16,24},{24,16},{1,9},{9,1},{17,25},{25,17},{2,10},{10... | collective-permute-start | bytes 1327112 | tf_op jit(solution)/shard_map/ppermute | solution.py:902
  283.3 18.2 %collective-permute-start.42 = (bf16[576,384]{1,0:T(8,128)(2,1)S(1)}, bf16[576,384]{1,0:T(8,128)(2,1)S(1)}, u32[]{:S(2)}, u32[]{:S(2)}) collective-permute-start(bf16[576,384]{1,0:T(8,128)(2,1)S(1)} %pad_maximum_fusion.10), channel_id=1, source_target_pairs={{0,16},{8,24},{16,0},{24,8},{1,17},{9,25},{17,1},{25,9},{2,18},{10... | collective-permute-start | bytes 1327112 | tf_op jit(solution)/shard_map/ppermute | solution.py:902
  301.8 14.4 %collective-permute-start.51 = (bf16[3,84,768]{2,1,0:T(8,128)(2,1)S(1)}, bf16[3,84,768]{2,1,0:T(8,128)(2,1)S(1)}, u32[]{:S(2)}, u32[]{:S(2)}) collective-permute-start(bf16[3,84,768]{2,1,0:T(8,128)(2,1)S(1)} %get-tuple-element.413), channel_id=1, source_target_pairs={{0,1},{1,2},{2,3},{3,4},{4,5},{5,6},{6,7},{7,0},{8,9},{9,10},{10,1... | collective-permute-start | bytes 1161224 | tf_op jit(solution)/shard_map/ppermute | solution.py:897
  303.4 12.7 %collective-permute-start.47 = (bf16[288,384]{1,0:T(8,128)(2,1)S(1)}, bf16[288,384]{1,0:T(8,128)(2,1)S(1)}, u32[]{:S(2)}, u32[]{:S(2)}) collective-permute-start(bf16[288,384]{1,0:T(8,128)(2,1)S(1)} %pad_maximum_fusion.19), channel_id=1, source_target_pairs={{0,2},{1,3},{2,0},{3,1},{4,6},{5,7},{6,4},{7,5},{8,10},{9,11},{10,... | collective-permute-start | bytes 663560 | tf_op jit(solution)/shard_map/ppermute | solution.py:902
  319.6 12.6 %collective-permute-start.57 = (bf16[240,768]{1,0:T(8,128)(2,1)S(1)}, bf16[240,768]{1,0:T(8,128)(2,1)S(1)}, u32[]{:S(2)}, u32[]{:S(2)}) collective-permute-start(bf16[240,768]{1,0:T(8,128)(2,1)S(1)} %pad_maximum_fusion.14), channel_id=1, source_target_pairs={{0,16},{8,24},{16,0},{24,8},{1,17},{9,25},{17,1},{25,9},{2,18},{10... | collective-permute-start | bytes 1105928 | tf_op jit(solution)/shard_map/ppermute | solution.py:902
  324.2 15.0 %collective-permute-start.54 = (bf16[336,384]{1,0:T(8,128)(2,1)S(1)}, bf16[336,384]{1,0:T(8,128)(2,1)S(1)}, u32[]{:S(2)}, u32[]{:S(2)}) collective-permute-start(bf16[336,384]{1,0:T(8,128)(2,1)S(1)} %pad_maximum_fusion.18), channel_id=1, source_target_pairs={{0,8},{8,0},{16,24},{24,16},{1,9},{9,1},{17,25},{25,17},{2,10},{10... | collective-permute-start | bytes 774152 | tf_op jit(solution)/shard_map/ppermute | solution.py:902
  325.7 13.5 %collective-permute-start.55 = (bf16[336,384]{1,0:T(8,128)(2,1)S(1)}, bf16[336,384]{1,0:T(8,128)(2,1)S(1)}, u32[]{:S(2)}, u32[]{:S(2)}) collective-permute-start(bf16[336,384]{1,0:T(8,128)(2,1)S(1)} %pad_maximum_fusion.18), channel_id=1, source_target_pairs={{0,16},{8,24},{16,0},{24,8},{1,17},{9,25},{17,1},{25,9},{2,18},{10... | collective-permute-start | bytes 774152 | tf_op jit(solution)/shard_map/ppermute | solution.py:902
  326.5 13.0 %collective-permute-start.56 = (bf16[336,384]{1,0:T(8,128)(2,1)S(1)}, bf16[336,384]{1,0:T(8,128)(2,1)S(1)}, u32[]{:S(2)}, u32[]{:S(2)}) collective-permute-start(bf16[336,384]{1,0:T(8,128)(2,1)S(1)} %pad_maximum_fusion.18), channel_id=1, source_target_pairs={{0,24},{8,16},{16,8},{24,0},{1,25},{9,17},{17,9},{25,1},{2,26},{10... | collective-permute-start | bytes 774152 | tf_op jit(solution)/shard_map/ppermute | solution.py:902
  (120 other events, 853.8 us)

commit v3 on v2

--- a/solution.py
+++ b/solution.py
@@ -1234,27 +1234,25 @@
         part = merged(part, swapped(part, "strip", mask))
         mask = 2 * mask
     others = swapped(part, "strip", mask)
-    cotangents = line_gather(after(query_cotangent[0], vis_attn))
 
     weights = (out_weight, out_bias, norm2_gain, norm2_bias, up_weight, up_bias, down_weight, down_bias)
     made = ffn_forward(vis, after(vis_attn, part), *weights, 0)
-    made, part, others, cotangents = beside(made, part, others, cotangents)
+    made, part, others = beside(made, part, others)
     vis_x1, vis_b, vis_hid, vis_slope, vis_result = made
     part = merged(part, others)
     others = other_core(part)
+    vis_down = weight_grad(after(vis_hid, part), vis_cot)
+    vis_down, part, others = beside(vis_down, part, others)
+    cotangents = line_gather(after(query_cotangent[0], part))
+    down = by_core(vis_down)
+    down = Phase([[down.reshape(chips, 2, -1, features // strips, features)]], [1], "strip", 1)
+
+    made = ffn_backward(
+        after(vis_cot, down.sent), vis_slope, vis_x1, down_weight, up_weight, out_weight, norm2_gain, 0
+    )
+    made, down.got, cotangents = beside(made, down.got, cotangents)
     cotangents = line_order(cotangents)
     cot_others = other_core(cotangents)
-    vis_down = weight_grad(after(vis_hid, part, cotangents), vis_cot)
-    vis_down, part, others, cotangents, cot_others = beside(
-        vis_down, part, others, cotangents, cot_others
-    )
-    down = by_core(vis_down)
-    down = Phase([[down.reshape(chips, 2, -1, features // strips, features)]], [1], "strip", 1)
-
-    made = ffn_backward(
-        after(vis_cot, down.sent), vis_slope, vis_x1, down_weight, up_weight, out_weight, norm2_gain, 0
-    )
-    made, down.got = beside(made, down.got)
     vis_dz, vis_dx1, vis_du, vis_do, vis_sums = made
     (down,) = down.terms()
     down = Phase([mapped(by_page, down)], [3], "page", 1)
@@ -1270,10 +1268,10 @@
     up_a = line_first(up_a.terms(), [1])
 
     every = core_order(part, others)
-    query_cot = core_order(cotangents, cot_others)
     every, up_sent = beside(every, up_a.sent)
     made = ffn_forward(query, every, *weights, 1)
-    made, down.got = beside(made, down.got)
+    made, down.got, cot_others = beside(made, down.got, cot_others)
+    query_cot = core_order(cotangents, cot_others)
     query_x1, query_b, query_hid, query_slope, query_result = made
     (down,) = down.terms()
     down = Phase([down], [2], "page", 2)

time: 350 us -> 343 us (0.980)
  local copies, waits for them, and re-layouts: 38.2 us -> 31.3 us
  waiting for transfers between devices: 51.9 us -> 56.2 us
    ppermute x49, waiting for transfers between devices: 43.6 us -> 53 us  [swapped(): return lax.ppermute(block, axis, [(i, i ^ mask) for i in range(size)])]
    ppermute x11, waiting for transfers between devices: 8.32 us -> 3.2 us  [moved(): lax.ppermute(block, axis, [(i, (i + step) % size) for i in range(size)])]
    unnamed x238 -> x224, local copies, waits for them, and re-layouts: 21.3 us -> 17.3 us
  transfers between devices with their start and end apart: 60 -> 60, of which waited for: 15 -> 15; matrix products, arithmetic and copies ran while one was open for 18% -> 18% of each run, Pallas kernels for 36% -> 37%
where the time goes in v3:
time: 343 us; the launch traced here: 338 us
  Pallas kernels  131 us (38%)
  waiting for transfers between devices  56.2 us (16%)
  starting transfers between devices  55.6 us (16%)
  other arithmetic  36.3 us (11%)
  local copies, waits for them, and re-layouts  31.3 us (9%)
  matrix products  23 us (7%)
  between operations  4.47 us (1%)
    ppermute x49, waiting for transfers between devices, swapped(): return lax.ppermute(block, axis, [(i, i ^ mask) for i in range(size)])  53 us
    ppermute x49, starting transfers between devices, swapped(): return lax.ppermute(block, axis, [(i, i ^ mask) for i in range(size)])  36.5 us
    pallas_call x2, Pallas kernels, attention_backward(): pl.pallas_call(functools.partial(attention_backward_kernel, windows, firs...  32.1 us
    pallas_call x2, Pallas kernels, ffn_forward(): pl.pallas_call(functools.partial(ffn_forward_kernel, stream), grid=(hidde...  27 us
    pallas_call x2, Pallas kernels, ffn_backward(): pl.pallas_call(functools.partial(ffn_backward_kernel, stream), grid=(hidd...  26.7 us
    dot_general x19, matrix products, dot_tn(): lax.dot_general(a, b, (((0,), (0,)), ((), ())), preferred_element_type=f32)  23 us
    ppermute x11, starting transfers between devices, moved(): lax.ppermute(block, axis, [(i, (i + step) % size) for i in range(size)])  19.1 us
    convert_element_type x41, other arithmetic, added(): return total.astype(kind)  18.9 us
  transfers between devices with their start and end apart: 60, of which 15 were waited for; matrix products, arithmetic and copies ran while one was open for 18% of the time, Pallas kernels for 37%

profile of v3, /device:TPU:0, one launch (start us, length us, event | category | flops | bytes accessed | tf_op | source)
XLA Modules:
  0.0 337.5 jit_solution(8085565193067441107)
XLA Ops:
  0.7 5.1 %collective-permute-start = (bf16[32,768]{1,0:T(8,128)(2,1)}, bf16[32,768]{1,0:T(8,128)(2,1)S(1)}, u32[]{:S(2)}, u32[]{:S(2)}) collective-permute-start(bf16[32,768]{1,0:T(8,128)(2,1)} %bitcast.622), channel_id=1, source_target_pairs={{0,6},{1,7},{2,0},{3,1},{4,2},{5,3},{6,4},{7,5},{8,14},{9,15},{10,... | collective-permute-start | bytes 147464 | tf_op jit(solution)/shard_map/ppermute | solution.py:897
  15.2 3.1 copy-done.2
  22.9 4.0 %collective-permute-start.5 = (bf16[6,84,768]{2,1,0:T(8,128)(2,1)S(1)}, bf16[6,84,768]{2,1,0:T(8,128)(2,1)S(1)}, u32[]{:S(2)}, u32[]{:S(2)}) collective-permute-start(bf16[6,84,768]{2,1,0:T(8,128)(2,1)S(1)} %copy-done.67), channel_id=1, source_target_pairs={{0,7},{1,0},{2,1},{3,2},{4,3},{5,4},{6,5},{7,6},{8,15},{9,8},{10,9... | collective-permute-start | bytes 2322440 | tf_op jit(solution)/shard_map/ppermute | solution.py:897
  27.1 5.1 %norm_qkv.3 = (bf16[1008,768]{1,0:T(8,128)(2,1)S(1)}, bf16[1008,2304]{1,0:T(8,128)(2,1)S(1)}) custom-call(bf16[1008,768]{1,0:T(8,128)(2,1)S(1)} %enter.2.x_ref, f32[2,768]{1,0:T(2,128)S(1)} %copy-done.46, f32[2,768]{1,0:T(2,128)S(1)} %copy-done.51, bf16[2,768,2304]{2,1,0:T(8,128)(2,1)S(1)} %bitcast.602), custom_call_target="tpu_custom_call" | custom-call | flops 178362 | bytes 564 | tf_op jit(solution)/shard_map/norm_qkv/pallas_call | solution.py:165
  32.4 9.1 %query_forward.1 = (f32[256,768]{1,0:T(8,128)S(1)}, f32[256,128]{1,0:T(8,128)S(1)}) custom-call(bf16[256,2304]{1,0:T(8,128)(2,1)S(1)} %get-tuple-element.235.qq_ref.kq_ref.vq_ref, bf16[1008,2304]{1,0:T(8,128)(2,1)S(1)} %get-tuple-element.338.k_ref.v_ref.q_ref, bf16[1008,2304]{1,0:T(8,128)(2,1)S(1)} %get-tuple-element.338.k_ref.v_ref.q_ref, ...), custom_call_target="tpu_custom_call" | custom-call | flops 81788 | bytes 154 | tf_op jit(solution)/shard_map/query_forward/pallas_call | solution.py:265
  49.2 2.3 copy-done.1
  52.6 11.6 %window_forward.1 = (bf16[1008,768]{1,0:T(8,128)(2,1)S(1)}, f32[6,1,2016]{2,1,0:T(1,128)S(1)}) custom-call(bf16[1008,2304]{1,0:T(8,128)(2,1)S(1)} %copy-done.1, bf16[1008,2304]{1,0:T(8,128)(2,1)S(1)} %copy-done.1, bf16[1008,2304]{1,0:T(8,128)(2,1)S(1)} %copy-done.1, bf16[256,2304]{1,0:T(8,128)(2,1)S(1)} %copy-done.4, bf16[256,2304]{1,0:T(8,128)(2,1)S(1)} %copy-done.4, ...), custom_call_target="tpu_custom_call" | custom-call | flops 123863 | bytes 309 | tf_op jit(solution)/shard_map/window_forward/pallas_call | solution.py:349
  64.9 2.5 merge.4
  68.5 17.1 %ffn_forward.2 = (f32[1008,768]{1,0:T(8,128)S(1)}, bf16[1008,768]{1,0:T(8,128)(2,1)S(1)}, bf16[1008,3072]{1,0:T(8,128)(2,1)S(1)}, bf16[1008,3072]{1,0:T(8,128)(2,1)}, bf16[1008,768]{1,0:T(8,128)(2,1)S(1)}) custom-call(bf16[1008,768]{1,0:T(8,128)(2,1)S(1)} %copy-done.8, bf16[1008,768]{1,0:T(8,128)(2,1)S(1)} %get-tuple-element.251.o_ref, ...), custom_call_target="tpu_custom_call" | custom-call | flops 535088 | bytes 1555 | tf_op jit(solution)/shard_map/ffn_forward/pallas_call | solution.py:702
  85.6 5.5 %collective-permute-done.8 = f32[4,32,896]{2,1,0:T(8,128)S(1)} collective-permute-done((f32[4,32,896]{2,1,0:T(8,128)S(1)}, f32[4,32,896]{2,1,0:T(8,128)S(1)}, u32[]{:S(2)}, u32[]{:S(2)}) %collective-permute-start.8) | collective-permute-done | bytes 458784 | tf_op jit(solution)/shard_map/ppermute | solution.py:902
  92.0 5.5 %convolution_convert_fusion = bf16[3072,768]{1,0:T(8,128)(2,1)S(1)} fusion(bf16[1008,3072]{1,0:T(8,128)(2,1)S(1)} %get-tuple-element.260, bf16[1008,768]{1,0:T(8,128)(2,1)S(1)} %copy-done.17), kind=kOutput, calls=%fused_computation.1 | convolution fusion | flops 4758700032 | bytes 12460032 | tf_op jit(solution)/shard_map/dot_general | solution.py:42
  97.6 2.5 constant_dynamic-slice_fusion.45
  109.9 16.5 %ffn_backward.2 = (bf16[4,1008,768]{2,1,0:T(8,128)(2,1)S(1)}, f32[1008,768]{1,0:T(8,128)S(1)}, bf16[1008,768]{1,0:T(8,128)(2,1)S(1)}, bf16[1008,768]{1,0:T(8,128)(2,1)S(1)}, f32[8,768]{1,0:T(8,128)S(1)}) custom-call(bf16[1008,768]{1,0:T(8,128)(2,1)S(1)} %copy-done.18, bf16[1008,3072]{1,0:T(8,128)(2,1)} %get-tuple-element.267.slope_ref, ...), custom_call_target="tpu_custom_call" | custom-call | flops 535088 | bytes 1633 | tf_op jit(solution)/shard_map/ffn_backward/pallas_call | solution.py:807
  128.1 3.2 fusion.24
  142.4 2.7 add_convert_fusion
  148.2 9.9 %ffn_forward.3 = (f32[256,768]{1,0:T(8,128)}, bf16[256,768]{1,0:T(8,128)(2,1)}, bf16[256,3072]{1,0:T(8,128)(2,1)}, bf16[256,3072]{1,0:T(8,128)(2,1)}, bf16[256,768]{1,0:T(8,128)(2,1)}) custom-call(bf16[256,768]{1,0:T(8,128)(2,1)} %bitcast.614, f32[256,896]{1,0:T(8,128)} %bitcast.605, bf16[2,768,768]{2,1,0:T(8,128)(2,1)} %wo_ref.7, f32[2,768]{1,0:T(2,128)} %bo_ref.3, ...), custom_call_target="tpu_custom_call" | custom-call | flops 135895 | bytes 747 | tf_op jit(solution)/shard_map/ffn_forward/pallas_call | solution.py:702
  158.1 7.4 %collective-permute-done.16 = bf16[4,4,2,24,768]{4,3,1,0,2:T(8,128)(2,1)} collective-permute-done((bf16[4,4,2,24,768]{4,3,1,0,2:T(8,128)(2,1)}, bf16[4,4,2,24,768]{4,3,1,0,2:T(8,128)(2,1)}, u32[]{:S(2)}, u32[]{:S(2)}) %collective-permute-start.16) | collective-permute-done | bytes 1179680 | tf_op jit(solution)/shard_map/ppermute | solution.py:902
  168.2 2.7 fusion.28
  171.8 10.2 %ffn_backward.3 = (bf16[4,256,768]{2,1,0:T(8,128)(2,1)}, f32[256,768]{1,0:T(8,128)}, bf16[256,768]{1,0:T(8,128)(2,1)}, bf16[256,768]{1,0:T(8,128)(2,1)}, f32[8,768]{1,0:T(8,128)}) custom-call(bf16[256,768]{1,0:T(8,128)(2,1)} %bitcast.645, bf16[256,3072]{1,0:T(8,128)(2,1)} %get-tuple-element.300.slope_ref, f32[256,768]{1,0:T(8,128)} %get-tuple-element.301.x1_ref, ...), custom_call_target="tpu_custom_call" | custom-call | flops 135895 | bytes 766 | tf_op jit(solution)/shard_map/ffn_backward/pallas_call | solution.py:807
  193.3 5.4 %collective-permute-done.20 = bf16[4,4,24,768]{3,2,1,0:T(8,128)(2,1)S(1)} collective-permute-done((bf16[4,4,24,768]{3,2,1,0:T(8,128)(2,1)}, bf16[4,4,24,768]{3,2,1,0:T(8,128)(2,1)S(1)}, u32[]{:S(2)}, u32[]{:S(2)}) %collective-permute-start.20) | collective-permute-done | bytes 589856 | tf_op jit(solution)/shard_map/ppermute | solution.py:902
  201.2 16.0 %attention_backward.2 = (bf16[1008,768]{1,0:T(8,128)(2,1)S(1)}, bf16[1008,768]{1,0:T(8,128)(2,1)S(1)}, bf16[1008,768]{1,0:T(8,128)(2,1)S(1)}, bf16[256,384]{1,0:...) custom-call(bf16[1008,2304]{1,0:T(8,128)(2,1)S(1)} %bitcast.600, ...), custom_call_target="tpu_custom_call" | custom-call | flops 253919 | bytes 270 | tf_op jit(solution)/shard_map/attention_backward/pallas_call | solution.py:572
  231.3 16.1 %attention_backward.3 = (bf16[1008,768]{1,0:T(8,128)(2,1)S(1)}, bf16[1008,768]{1,0:T(8,128)(2,1)S(1)}, bf16[1008,768]{1,0:T(8,128)(2,1)S(1)}, bf16[256,384]{1,0:...) custom-call(bf16[1008,2304]{1,0:T(8,128)(2,1)S(1)} %bitcast.600, ...), custom_call_target="tpu_custom_call", output_to_operand_aliasing={{0}: (17, {}), {1}: (18, {}), {2}: (19, {})} | custom-call | flops 253919 | bytes 270 | tf_op jit(solution)/shard_map/attention_backward/pallas_call | solution.py:572
  256.6 5.7 %input_grad.2 = (bf16[1008,768]{1,0:T(8,128)(2,1)S(1)}, f32[8,768]{1,0:T(8,128)S(1)}) custom-call(bf16[1008,768]{1,0:T(8,128)(2,1)S(1)} %get-tuple-element.366.dq_ref, bf16[1008,768]{1,0:T(8,128)(2,1)S(1)} %get-tuple-element.356.dk_ref, bf16[1008,768]{1,0:T(8,128)(2,1)S(1)} %get-tuple-element.357.dv_ref, bf16[2,768,2304]{2,1,0:T(8,128)(2,1)S(1)} %bitcast.604, ...), custom_call_target="tpu_custom_call" | custom-call | flops 178362 | bytes 718 | tf_op jit(solution)/shard_map/input_grad/pallas_call | solution.py:866
  262.4 5.1 %collective-permute-done.33 = bf16[2,6,32,384]{3,2,1,0:T(8,128)(2,1)S(1)} collective-permute-done((bf16[2,6,32,384]{3,2,1,0:T(8,128)(2,1)S(1)}, bf16[2,6,32,384]{3,2,1,0:T(8,128)(2,1)S(1)}, u32[]{:S(2)}, u32[]{:S(2)}) %collective-permute-start.33) | collective-permute-done | bytes 294944 | tf_op jit(solution)/shard_map/ppermute | solution.py:902
  269.7 6.4 %collective-permute-done.34 = bf16[1,6,32,384]{3,2,1,0:T(8,128)(2,1)S(1)} collective-permute-done((bf16[1,6,32,384]{3,2,1,0:T(8,128)(2,1)S(1)}, bf16[1,6,32,384]{3,2,1,0:T(8,128)(2,1)S(1)}, u32[]{:S(2)}, u32[]{:S(2)}) %collective-permute-start.34) | collective-permute-done | bytes 147488 | tf_op jit(solution)/shard_map/ppermute | solution.py:902
  279.5 5.7 %collective-permute-done.37 = bf16[1,6,32,384]{3,2,1,0:T(8,128)(2,1)S(1)} collective-permute-done((bf16[1,6,32,384]{3,2,1,0:T(8,128)(2,1)S(1)}, bf16[1,6,32,384]{3,2,1,0:T(8,128)(2,1)S(1)}, u32[]{:S(2)}, u32[]{:S(2)}) %collective-permute-start.37) | collective-permute-done | bytes 147488 | tf_op jit(solution)/shard_map/ppermute | solution.py:902
  286.6 8.3 %collective-permute-done.40 = bf16[2,6,32,384]{3,2,1,0:T(8,128)(2,1)S(1)} collective-permute-done((bf16[2,6,32,384]{3,2,1,0:T(8,128)(2,1)S(1)}, bf16[2,6,32,384]{3,2,1,0:T(8,128)(2,1)S(1)}, u32[]{:S(2)}, u32[]{:S(2)}) %collective-permute-start.40) | collective-permute-done | bytes 294944 | tf_op jit(solution)/shard_map/ppermute | solution.py:902
  303.4 2.6 collective-permute-start.48
  306.1 3.5 %collective-permute-done.47 = bf16[288,384]{1,0:T(8,128)(2,1)S(1)} collective-permute-done((bf16[288,384]{1,0:T(8,128)(2,1)S(1)}, bf16[288,384]{1,0:T(8,128)(2,1)S(1)}, u32[]{:S(2)}, u32[]{:S(2)}) %collective-permute-start.47) | collective-permute-done | bytes 221216 | tf_op jit(solution)/shard_map/ppermute | solution.py:902
  315.1 2.3 collective-permute-done.53
  321.2 2.9 collective-permute-start.59
  328.4 2.9 collective-permute-done.59
  (565 shorter events, 123.8 us)
Async XLA Ops:
  0.7 12.7 %collective-permute-start = (bf16[32,768]{1,0:T(8,128)(2,1)}, bf16[32,768]{1,0:T(8,128)(2,1)S(1)}, u32[]{:S(2)}, u32[]{:S(2)}) collective-permute-start(bf16[32,768]{1,0:T(8,128)(2,1)} %bitcast.622), channel_id=1, source_target_pairs={{0,6},{1,7},{2,0},{3,1},{4,2},{5,3},{6,4},{7,5},{8,14},{9,15},{10,... | collective-permute-start | bytes 147464 | tf_op jit(solution)/shard_map/ppermute | solution.py:897
  22.9 18.6 %collective-permute-start.5 = (bf16[6,84,768]{2,1,0:T(8,128)(2,1)S(1)}, bf16[6,84,768]{2,1,0:T(8,128)(2,1)S(1)}, u32[]{:S(2)}, u32[]{:S(2)}) collective-permute-start(bf16[6,84,768]{2,1,0:T(8,128)(2,1)S(1)} %copy-done.67), channel_id=1, source_target_pairs={{0,7},{1,0},{2,1},{3,2},{4,3},{5,4},{6,5},{7,6},{8,15},{9,8},{10,9... | collective-permute-start | bytes 2322440 | tf_op jit(solution)/shard_map/ppermute | solution.py:897
  47.4 17.4 %collective-permute-start.7 = (f32[4,32,896]{2,1,0:T(8,128)}, f32[4,32,896]{2,1,0:T(8,128)}, u32[]{:S(2)}, u32[]{:S(2)}) collective-permute-start(f32[4,32,896]{2,1,0:T(8,128)} %bitcast.21), channel_id=1, source_target_pairs={{0,2},{1,3},{2,0},{3,1},{4,6},{5,7},{6,4},{7,5},{8,10},{9,11},{10,... | collective-permute-start | bytes 1376264 | tf_op jit(solution)/shard_map/ppermute | solution.py:902
  67.4 23.7 %collective-permute-start.8 = (f32[4,32,896]{2,1,0:T(8,128)S(1)}, f32[4,32,896]{2,1,0:T(8,128)S(1)}, u32[]{:S(2)}, u32[]{:S(2)}) collective-permute-start(f32[4,32,896]{2,1,0:T(8,128)S(1)} %bitcast.618), channel_id=1, source_target_pairs={{0,4},{1,5},{2,6},{3,7},{4,0},{5,1},{6,2},{7,3},{8,12},{9,13},{10,... | collective-permute-start | bytes 1376264 | tf_op jit(solution)/shard_map/ppermute | solution.py:902
  100.1 28.0 %collective-permute-start.10 = (bf16[4,4,96,768]{3,2,1,0:T(8,128)(2,1)}, bf16[4,4,96,768]{3,2,1,0:T(8,128)(2,1)}, u32[]{:S(2)}, u32[]{:S(2)}) collective-permute-start(bf16[4,4,96,768]{3,2,1,0:T(8,128)(2,1)} %get-tuple-element.446), channel_id=1, source_target_pairs={{0,1},{1,0},{2,3},{3,2},{4,5},{5,4},{6,7},{7,6},{8,9},{9,8},{10,11... | collective-permute-start | bytes 7077896 | tf_op jit(solution)/shard_map/ppermute | solution.py:902
  101.9 26.2 %collective-permute-start.11 = (bf16[32,768]{1,0:T(8,128)(2,1)}, bf16[32,768]{1,0:T(8,128)(2,1)S(1)}, u32[]{:S(2)}, u32[]{:S(2)}) collective-permute-start(bf16[32,768]{1,0:T(8,128)(2,1)} %bitcast.776), channel_id=1, source_target_pairs={{0,2},{1,3},{2,4},{3,5},{4,6},{5,7},{6,0},{7,1},{8,10},{9,11},{10,... | collective-permute-start | bytes 147464 | tf_op jit(solution)/shard_map/ppermute | solution.py:897
  101.9 26.2 %collective-permute-start.12 = (bf16[32,768]{1,0:T(8,128)(2,1)}, bf16[32,768]{1,0:T(8,128)(2,1)S(1)}, u32[]{:S(2)}, u32[]{:S(2)}) collective-permute-start(bf16[32,768]{1,0:T(8,128)(2,1)} %bitcast.777), channel_id=1, source_target_pairs={{0,4},{1,5},{2,6},{3,7},{4,0},{5,1},{6,2},{7,3},{8,12},{9,13},{10,... | collective-permute-start | bytes 147464 | tf_op jit(solution)/shard_map/ppermute | solution.py:897
  103.6 24.5 %collective-permute-start.13 = (bf16[32,768]{1,0:T(8,128)(2,1)}, bf16[32,768]{1,0:T(8,128)(2,1)S(1)}, u32[]{:S(2)}, u32[]{:S(2)}) collective-permute-start(bf16[32,768]{1,0:T(8,128)(2,1)} %bitcast.778), channel_id=1, source_target_pairs={{0,6},{1,7},{2,0},{3,1},{4,2},{5,3},{6,4},{7,5},{8,14},{9,15},{10,... | collective-permute-start | bytes 147464 | tf_op jit(solution)/shard_map/ppermute | solution.py:897
  136.9 28.7 %collective-permute-start.16 = (bf16[4,4,2,24,768]{4,3,1,0,2:T(8,128)(2,1)}, bf16[4,4,2,24,768]{4,3,1,0,2:T(8,128)(2,1)}, u32[]{:S(2)}, u32[]{:S(2)}) collective-permute-start(bf16[4,4,2,24,768]{4,3,1,0,2:T(8,128)(2,1)} %fusion.24), channel_id=1, source_target_pairs={{0,8},{8,0},{16,24},{24,16},{1,9},{9,1},{17,25},{25,17},{2,10},{10... | collective-permute-start | bytes 3538952 | tf_op jit(solution)/shard_map/ppermute | solution.py:902
  141.9 16.2 %collective-permute-start.17 = (bf16[4,32,768]{2,1,0:T(8,128)(2,1)S(1)}, bf16[4,32,768]{2,1,0:T(8,128)(2,1)S(1)}, u32[]{:S(2)}, u32[]{:S(2)}) collective-permute-start(bf16[4,32,768]{2,1,0:T(8,128)(2,1)S(1)} %constant_dynamic-slice_fusion.39), channel_id=1, source_target_pairs={{0,1},{1,0},{2,3},{3,2},{4,5},{5,4},{6,7},{7,6},{8,9},{9,8},{10,11... | collective-permute-start | bytes 589832 | tf_op jit(solution)/shard_map/ppermute | solution.py:902
  147.7 40.3 %collective-permute-start.18 = (bf16[3,2,96,768]{3,2,1,0:T(8,128)(2,1)}, bf16[3,2,96,768]{3,2,1,0:T(8,128)(2,1)}, u32[]{:S(2)}, u32[]{:S(2)}) collective-permute-start(bf16[3,2,96,768]{3,2,1,0:T(8,128)(2,1)} %get-tuple-element.448), channel_id=1, source_target_pairs={{0,2},{1,3},{2,0},{3,1},{4,6},{5,7},{6,4},{7,5},{8,10},{9,11},{10,... | collective-permute-start | bytes 2654216 | tf_op jit(solution)/shard_map/ppermute | solution.py:902
  166.8 21.2 %collective-permute-start.19 = (bf16[2,4,2,24,768]{4,3,1,0,2:T(8,128)(2,1)}, bf16[2,4,2,24,768]{4,3,1,0,2:T(8,128)(2,1)}, u32[]{:S(2)}, u32[]{:S(2)}) collective-permute-start(bf16[2,4,2,24,768]{4,3,1,0,2:T(8,128)(2,1)} %fusion.50), channel_id=1, source_target_pairs={{0,8},{8,0},{16,24},{24,16},{1,9},{9,1},{17,25},{25,17},{2,10},{10... | collective-permute-start | bytes 1769480 | tf_op jit(solution)/shard_map/ppermute | solution.py:902
  182.1 16.5 %collective-permute-start.20 = (bf16[4,4,24,768]{3,2,1,0:T(8,128)(2,1)}, bf16[4,4,24,768]{3,2,1,0:T(8,128)(2,1)S(1)}, u32[]{:S(2)}, u32[]{:S(2)}) collective-permute-start(bf16[4,4,24,768]{3,2,1,0:T(8,128)(2,1)} %get-tuple-element.452), channel_id=1, source_target_pairs={{0,16},{8,24},{16,0},{24,8},{1,17},{9,25},{17,1},{25,9},{2,18},{10... | collective-permute-start | bytes 1769480 | tf_op jit(solution)/shard_map/ppermute | solution.py:902
  183.7 34.8 %collective-permute-start.24 = (bf16[6,84,768]{2,1,0:T(8,128)(2,1)}, bf16[6,84,768]{2,1,0:T(8,128)(2,1)S(1)}, u32[]{:S(2)}, u32[]{:S(2)}) collective-permute-start(bf16[6,84,768]{2,1,0:T(8,128)(2,1)} %copy-done.57), channel_id=1, source_target_pairs={{0,1},{1,2},{2,3},{3,4},{4,5},{5,6},{6,7},{7,0},{8,9},{9,10},{10,1... | collective-permute-start | bytes 2322440 | tf_op jit(solution)/shard_map/ppermute | solution.py:897
  189.3 29.2 %collective-permute-start.22 = (bf16[2,4,24,768]{3,2,1,0:T(8,128)(2,1)S(1)}, bf16[2,4,24,768]{3,2,1,0:T(8,128)(2,1)S(1)}, u32[]{:S(2)}, u32[]{:S(2)}) collective-permute-start(bf16[2,4,24,768]{3,2,1,0:T(8,128)(2,1)S(1)} %get-tuple-element.472), channel_id=1, source_target_pairs={{0,16},{8,24},{16,0},{24,8},{1,17},{9,25},{17,1},{25,9},{2,18},{10... | collective-permute-start | bytes 884744 | tf_op jit(solution)/shard_map/ppermute | solution.py:902
  191.1 27.5 %collective-permute-start.21 = (bf16[3,2,2,24,768]{4,3,2,1,0:T(8,128)(2,1)S(1)}, bf16[3,2,2,24,768]{4,3,2,1,0:T(8,128)(2,1)S(1)}, u32[]{:S(2)}, u32[]{:S(2)}) collective-permute-start(bf16[3,2,2,24,768]{4,3,2,1,0:T(8,128)(2,1)S(1)} %fusion.54), channel_id=1, source_target_pairs={{0,8},{8,0},{16,24},{24,16},{1,9},{9,1},{17,25},{25,17},{2,10},{10... | collective-permute-start | bytes 1327112 | tf_op jit(solution)/shard_map/ppermute | solution.py:902
  198.8 19.7 %collective-permute-start.23 = (bf16[2,4,24,768]{3,2,1,0:T(8,128)(2,1)S(1)}, bf16[2,4,24,768]{3,2,1,0:T(8,128)(2,1)S(1)}, u32[]{:S(2)}, u32[]{:S(2)}) collective-permute-start(bf16[2,4,24,768]{3,2,1,0:T(8,128)(2,1)S(1)} %fusion.68), channel_id=1, source_target_pairs={{0,2},{1,3},{2,0},{3,1},{4,6},{5,7},{6,4},{7,5},{8,10},{9,11},{10,... | collective-permute-start | bytes 884744 | tf_op jit(solution)/shard_map/ppermute | solution.py:902
  199.5 28.2 %collective-permute-start.25 = (bf16[9,2,24,768]{3,2,0,1:T(8,128)(2,1)S(1)}, bf16[9,2,24,768]{3,2,0,1:T(8,128)(2,1)S(1)}, u32[]{:S(2)}, u32[]{:S(2)}) collective-permute-start(bf16[9,2,24,768]{3,2,0,1:T(8,128)(2,1)S(1)} %copy_bitcast_fusion.2), channel_id=1, source_target_pairs={{0,8},{8,0},{16,24},{24,16},{1,9},{9,1},{17,25},{25,17},{2,10},{10... | collective-permute-start | bytes 1990664 | tf_op jit(solution)/shard_map/ppermute | solution.py:902
  222.5 25.0 %collective-permute-start.29 = (bf16[2,2,24,768]{3,2,1,0:T(8,128)(2,1)S(1)}, bf16[2,2,24,768]{3,2,1,0:T(8,128)(2,1)S(1)}, u32[]{:S(2)}, u32[]{:S(2)}) collective-permute-start(bf16[2,2,24,768]{3,2,1,0:T(8,128)(2,1)S(1)} %fusion.88), channel_id=1, source_target_pairs={{0,2},{1,3},{2,0},{3,1},{4,6},{5,7},{6,4},{7,5},{8,10},{9,11},{10,... | collective-permute-start | bytes 442376 | tf_op jit(solution)/shard_map/ppermute | solution.py:902
  224.1 23.4 %collective-permute-start.30 = (bf16[1,4,24,768]{3,2,1,0:T(8,128)(2,1)S(1)}, bf16[1,4,24,768]{3,2,1,0:T(8,128)(2,1)S(1)}, u32[]{:S(2)}, u32[]{:S(2)}) collective-permute-start(bf16[1,4,24,768]{3,2,1,0:T(8,128)(2,1)S(1)} %fusion.74), channel_id=1, source_target_pairs={{0,4},{1,5},{2,6},{3,7},{4,0},{5,1},{6,2},{7,3},{8,12},{9,13},{10,... | collective-permute-start | bytes 442376 | tf_op jit(solution)/shard_map/ppermute | solution.py:902
  228.0 19.5 %collective-permute-start.28 = (bf16[360,768]{1,0:T(8,128)(2,1)S(1)}, bf16[360,768]{1,0:T(8,128)(2,1)S(1)}, u32[]{:S(2)}, u32[]{:S(2)}) collective-permute-start(bf16[360,768]{1,0:T(8,128)(2,1)S(1)} %pad_maximum_fusion.7), channel_id=1, source_target_pairs={{0,16},{8,24},{16,0},{24,8},{1,17},{9,25},{17,1},{25,9},{2,18},{10... | collective-permute-start | bytes 1658888 | tf_op jit(solution)/shard_map/ppermute | solution.py:902
  229.7 17.9 %collective-permute-start.27 = (bf16[4,3,2,24,384]{4,3,2,1,0:T(8,128)(2,1)S(1)}, bf16[4,3,2,24,384]{4,3,2,1,0:T(8,128)(2,1)S(1)}, u32[]{:S(2)}, u32[]{:S(2)}) collective-permute-start(bf16[4,3,2,24,384]{4,3,2,1,0:T(8,128)(2,1)S(1)} %fusion.57), channel_id=1, source_target_pairs={{0,8},{8,0},{16,24},{24,16},{1,9},{9,1},{17,25},{25,17},{2,10},{10... | collective-permute-start | bytes 1327112 | tf_op jit(solution)/shard_map/ppermute | solution.py:902
  254.1 13.4 %collective-permute-start.33 = (bf16[2,6,32,384]{3,2,1,0:T(8,128)(2,1)S(1)}, bf16[2,6,32,384]{3,2,1,0:T(8,128)(2,1)S(1)}, u32[]{:S(2)}, u32[]{:S(2)}) collective-permute-start(bf16[2,6,32,384]{3,2,1,0:T(8,128)(2,1)S(1)} %get-tuple-element.468), channel_id=1, source_target_pairs={{0,2},{1,3},{2,0},{3,1},{4,6},{5,7},{6,4},{7,5},{8,10},{9,11},{10,... | collective-permute-start | bytes 884744 | tf_op jit(solution)/shard_map/ppermute | solution.py:902
  254.3 15.4 %collective-permute-start.36 = (bf16[120,768]{1,0:T(8,128)(2,1)S(1)}, bf16[120,768]{1,0:T(8,128)(2,1)S(1)}, u32[]{:S(2)}, u32[]{:S(2)}) collective-permute-start(bf16[120,768]{1,0:T(8,128)(2,1)S(1)} %pad_maximum_fusion.24), channel_id=1, source_target_pairs={{0,4},{1,5},{2,6},{3,7},{4,0},{5,1},{6,2},{7,3},{8,12},{9,13},{10,... | collective-permute-start | bytes 552968 | tf_op jit(solution)/shard_map/ppermute | solution.py:902
  255.9 20.2 %collective-permute-start.35 = (bf16[4,3,2,24,384]{4,3,2,1,0:T(8,128)(2,1)S(1)}, bf16[4,3,2,24,384]{4,3,2,1,0:T(8,128)(2,1)S(1)}, u32[]{:S(2)}, u32[]{:S(2)}) collective-permute-start(bf16[4,3,2,24,384]{4,3,2,1,0:T(8,128)(2,1)S(1)} %fusion.58), channel_id=1, source_target_pairs={{0,8},{8,0},{16,24},{24,16},{1,9},{9,1},{17,25},{25,17},{2,10},{10... | collective-permute-start | bytes 1327112 | tf_op jit(solution)/shard_map/ppermute | solution.py:902
  276.7 18.2 %collective-permute-start.42 = (bf16[576,384]{1,0:T(8,128)(2,1)S(1)}, bf16[576,384]{1,0:T(8,128)(2,1)S(1)}, u32[]{:S(2)}, u32[]{:S(2)}) collective-permute-start(bf16[576,384]{1,0:T(8,128)(2,1)S(1)} %pad_maximum_fusion.10), channel_id=1, source_target_pairs={{0,16},{8,24},{16,0},{24,8},{1,17},{9,25},{17,1},{25,9},{2,18},{10... | collective-permute-start | bytes 1327112 | tf_op jit(solution)/shard_map/ppermute | solution.py:902
  295.2 14.4 %collective-permute-start.51 = (bf16[3,84,768]{2,1,0:T(8,128)(2,1)S(1)}, bf16[3,84,768]{2,1,0:T(8,128)(2,1)S(1)}, u32[]{:S(2)}, u32[]{:S(2)}) collective-permute-start(bf16[3,84,768]{2,1,0:T(8,128)(2,1)S(1)} %get-tuple-element.411), channel_id=1, source_target_pairs={{0,1},{1,2},{2,3},{3,4},{4,5},{5,6},{6,7},{7,0},{8,9},{9,10},{10,1... | collective-permute-start | bytes 1161224 | tf_op jit(solution)/shard_map/ppermute | solution.py:897
  296.9 12.7 %collective-permute-start.47 = (bf16[288,384]{1,0:T(8,128)(2,1)S(1)}, bf16[288,384]{1,0:T(8,128)(2,1)S(1)}, u32[]{:S(2)}, u32[]{:S(2)}) collective-permute-start(bf16[288,384]{1,0:T(8,128)(2,1)S(1)} %pad_maximum_fusion.19), channel_id=1, source_target_pairs={{0,2},{1,3},{2,0},{3,1},{4,6},{5,7},{6,4},{7,5},{8,10},{9,11},{10,... | collective-permute-start | bytes 663560 | tf_op jit(solution)/shard_map/ppermute | solution.py:902
  313.1 12.7 %collective-permute-start.57 = (bf16[240,768]{1,0:T(8,128)(2,1)S(1)}, bf16[240,768]{1,0:T(8,128)(2,1)S(1)}, u32[]{:S(2)}, u32[]{:S(2)}) collective-permute-start(bf16[240,768]{1,0:T(8,128)(2,1)S(1)} %pad_maximum_fusion.14), channel_id=1, source_target_pairs={{0,16},{8,24},{16,0},{24,8},{1,17},{9,25},{17,1},{25,9},{2,18},{10... | collective-permute-start | bytes 1105928 | tf_op jit(solution)/shard_map/ppermute | solution.py:902
  317.6 15.1 %collective-permute-start.54 = (bf16[336,384]{1,0:T(8,128)(2,1)S(1)}, bf16[336,384]{1,0:T(8,128)(2,1)S(1)}, u32[]{:S(2)}, u32[]{:S(2)}) collective-permute-start(bf16[336,384]{1,0:T(8,128)(2,1)S(1)} %pad_maximum_fusion.18), channel_id=1, source_target_pairs={{0,8},{8,0},{16,24},{24,16},{1,9},{9,1},{17,25},{25,17},{2,10},{10... | collective-permute-start | bytes 774152 | tf_op jit(solution)/shard_map/ppermute | solution.py:902
  319.2 13.5 %collective-permute-start.55 = (bf16[336,384]{1,0:T(8,128)(2,1)S(1)}, bf16[336,384]{1,0:T(8,128)(2,1)S(1)}, u32[]{:S(2)}, u32[]{:S(2)}) collective-permute-start(bf16[336,384]{1,0:T(8,128)(2,1)S(1)} %pad_maximum_fusion.18), channel_id=1, source_target_pairs={{0,16},{8,24},{16,0},{24,8},{1,17},{9,25},{17,1},{25,9},{2,18},{10... | collective-permute-start | bytes 774152 | tf_op jit(solution)/shard_map/ppermute | solution.py:902
  319.9 13.0 %collective-permute-start.56 = (bf16[336,384]{1,0:T(8,128)(2,1)S(1)}, bf16[336,384]{1,0:T(8,128)(2,1)S(1)}, u32[]{:S(2)}, u32[]{:S(2)}) collective-permute-start(bf16[336,384]{1,0:T(8,128)(2,1)S(1)} %pad_maximum_fusion.18), channel_id=1, source_target_pairs={{0,24},{8,16},{16,8},{24,0},{1,25},{9,17},{17,9},{25,1},{2,26},{10... | collective-permute-start | bytes 774152 | tf_op jit(solution)/shard_map/ppermute | solution.py:902
  (113 other events, 813.5 us)

commit v4 on v3

--- a/solution.py
+++ b/solution.py
@@ -373,7 +373,7 @@
             pltpu.VMEM((windows, PAIR, 2 * CELLS), f32),
             pltpu.VMEM((PAIR, 2 * cells), f32),
         ],
-        compiler_params=params(12 + queries // 28),
+        compiler_params=params(56),
         cost_estimate=cost(
             8 * cells * (CELLS + queries) * width,
             8 * cells * width,
@@ -1237,12 +1237,11 @@
 
     weights = (out_weight, out_bias, norm2_gain, norm2_bias, up_weight, up_bias, down_weight, down_bias)
     made = ffn_forward(vis, after(vis_attn, part), *weights, 0)
-    made, part, others = beside(made, part, others)
     vis_x1, vis_b, vis_hid, vis_slope, vis_result = made
+    vis_down = weight_grad(vis_hid, vis_cot)
+    vis_down, part, others = beside(vis_down, part, others)
     part = merged(part, others)
     others = other_core(part)
-    vis_down = weight_grad(after(vis_hid, part), vis_cot)
-    vis_down, part, others = beside(vis_down, part, others)
     cotangents = line_gather(after(query_cotangent[0], part))
     down = by_core(vis_down)
     down = Phase([[down.reshape(chips, 2, -1, features // strips, features)]], [1], "strip", 1)
@@ -1250,7 +1249,7 @@
     made = ffn_backward(
         after(vis_cot, down.sent), vis_slope, vis_x1, down_weight, up_weight, out_weight, norm2_gain, 0
     )
-    made, down.got, cotangents = beside(made, down.got, cotangents)
+    made, down.got, cotangents, others = beside(made, down.got, cotangents, others)
     cotangents = line_order(cotangents)
     cot_others = other_core(cotangents)
     vis_dz, vis_dx1, vis_du, vis_do, vis_sums = made

time: 343 us -> 339 us (0.988)
  waiting for transfers between devices: 56.2 us -> 46.2 us
  local copies, waits for them, and re-layouts: 31.3 us -> 35.8 us
    ppermute x49, waiting for transfers between devices: 53 us -> 36.5 us  [swapped(): return lax.ppermute(block, axis, [(i, i ^ mask) for i in range(size)])]
    ppermute x11, waiting for transfers between devices: 3.2 us -> 9.73 us  [moved(): lax.ppermute(block, axis, [(i, (i + step) % size) for i in range(size)])]
    ppermute x11, starting transfers between devices: 19.1 us -> 15 us  [moved(): lax.ppermute(block, axis, [(i, (i + step) % size) for i in range(size)])]
    unnamed x224 -> x210, local copies, waits for them, and re-layouts: 17.3 us -> 17.9 us
  transfers between devices with their start and end apart: 60 -> 60, of which waited for: 15 -> 15; matrix products, arithmetic and copies ran while one was open for 18% -> 19% of each run, Pallas kernels for 37% -> 38%
where the time goes in v4:
time: 339 us; the launch traced here: 335 us
  Pallas kernels  133 us (39%)
  starting transfers between devices  54.4 us (16%)
  waiting for transfers between devices  46.2 us (14%)
  other arithmetic  37.9 us (11%)
  local copies, waits for them, and re-layouts  35.8 us (11%)
  matrix products  23.8 us (7%)
  between operations  4.38 us (1%)
    ppermute x49, starting transfers between devices, swapped(): return lax.ppermute(block, axis, [(i, i ^ mask) for i in range(size)])  39.4 us
    ppermute x49, waiting for transfers between devices, swapped(): return lax.ppermute(block, axis, [(i, i ^ mask) for i in range(size)])  36.5 us
    pallas_call x2, Pallas kernels, attention_backward(): pl.pallas_call(functools.partial(attention_backward_kernel, windows, firs...  32.3 us
    pallas_call x2, Pallas kernels, ffn_backward(): pl.pallas_call(functools.partial(ffn_backward_kernel, stream), grid=(hidd...  27.4 us
    pallas_call x2, Pallas kernels, ffn_forward(): pl.pallas_call(functools.partial(ffn_forward_kernel, stream), grid=(hidde...  27.1 us
    dot_general x19, matrix products, dot_tn(): lax.dot_general(a, b, (((0,), (0,)), ((), ())), preferred_element_type=f32)  23.8 us
    convert_element_type x41, other arithmetic, added(): return total.astype(kind)  19.1 us
    unnamed x210, local copies, waits for them, and re-layouts  17.9 us
  transfers between devices with their start and end apart: 60, of which 15 were waited for; matrix products, arithmetic and copies ran while one was open for 19% of the time, Pallas kernels for 38%

profile of v4, /device:TPU:0, one launch (start us, length us, event | category | flops | bytes accessed | tf_op | source)
XLA Modules:
  0.0 335.3 jit_solution(7177992363245061166)
XLA Ops:
  0.7 5.1 %collective-permute-start = (bf16[32,768]{1,0:T(8,128)(2,1)}, bf16[32,768]{1,0:T(8,128)(2,1)S(1)}, u32[]{:S(2)}, u32[]{:S(2)}) collective-permute-start(bf16[32,768]{1,0:T(8,128)(2,1)} %bitcast.623), channel_id=1, source_target_pairs={{0,6},{1,7},{2,0},{3,1},{4,2},{5,3},{6,4},{7,5},{8,14},{9,15},{10,... | collective-permute-start | bytes 147464 | tf_op jit(solution)/shard_map/ppermute | solution.py:897
  6.8 2.1 slice_bitcast_fusion.1
  16.7 3.1 copy-done.1
  19.9 2.0 norm_qkv.2
  22.0 2.4 enter.2.x_ref
  24.5 2.1 collective-permute-start.5
  26.8 5.1 %norm_qkv.3 = (bf16[1008,768]{1,0:T(8,128)(2,1)S(1)}, bf16[1008,2304]{1,0:T(8,128)(2,1)S(1)}) custom-call(bf16[1008,768]{1,0:T(8,128)(2,1)S(1)} %enter.2.x_ref, f32[2,768]{1,0:T(2,128)S(1)} %copy-done.36, f32[2,768]{1,0:T(2,128)S(1)} %copy-done.40, bf16[2,768,2304]{2,1,0:T(8,128)(2,1)S(1)} %bitcast.602), custom_call_target="tpu_custom_call" | custom-call | flops 178362 | bytes 564 | tf_op jit(solution)/shard_map/norm_qkv/pallas_call | solution.py:165
  33.1 9.1 %query_forward.1 = (f32[256,768]{1,0:T(8,128)S(1)}, f32[256,128]{1,0:T(8,128)S(1)}) custom-call(bf16[256,2304]{1,0:T(8,128)(2,1)S(1)} %get-tuple-element.228.qq_ref.kq_ref.vq_ref, bf16[1008,2304]{1,0:T(8,128)(2,1)S(1)} %get-tuple-element.324.k_ref.v_ref.q_ref, bf16[1008,2304]{1,0:T(8,128)(2,1)S(1)} %get-tuple-element.324.k_ref.v_ref.q_ref, ...), custom_call_target="tpu_custom_call" | custom-call | flops 81788 | bytes 154 | tf_op jit(solution)/shard_map/query_forward/pallas_call | solution.py:265
  51.3 13.4 %window_forward.1 = (bf16[1008,768]{1,0:T(8,128)(2,1)}, f32[6,1,2016]{2,1,0:T(1,128)}) custom-call(bf16[1008,2304]{1,0:T(8,128)(2,1)} %copy-done, bf16[1008,2304]{1,0:T(8,128)(2,1)} %copy-done, bf16[1008,2304]{1,0:T(8,128)(2,1)} %copy-done, bf16[256,2304]{1,0:T(8,128)(2,1)} %copy-done.2, bf16[256,2304]{1,0:T(8,128)(2,1)} %copy-done.2, ...), custom_call_target="tpu_custom_call" | custom-call | flops 123863 | bytes 309 | tf_op jit(solution)/shard_map/window_forward/pallas_call | solution.py:349
  69.1 17.1 %ffn_forward.2 = (f32[1008,768]{1,0:T(8,128)S(1)}, bf16[1008,768]{1,0:T(8,128)(2,1)S(1)}, bf16[1008,3072]{1,0:T(8,128)(2,1)S(1)}, bf16[1008,3072]{1,0:T(8,128)(2,1)}, bf16[1008,768]{1,0:T(8,128)(2,1)S(1)}) custom-call(bf16[1008,768]{1,0:T(8,128)(2,1)S(1)} %copy-done.7, bf16[1008,768]{1,0:T(8,128)(2,1)S(1)} %copy-done.25, bf16[2,768,768]{2,1,0:T(8,128)(2,1)S(1)} %copy-done.5, ...), custom_call_target="tpu_custom_call" | custom-call | flops 535088 | bytes 1555 | tf_op jit(solution)/shard_map/ffn_forward/pallas_call | solution.py:702
  86.2 5.5 %convolution_convert_fusion = bf16[3072,768]{1,0:T(8,128)(2,1)S(1)} fusion(bf16[1008,3072]{1,0:T(8,128)(2,1)S(1)} %get-tuple-element.245, bf16[1008,768]{1,0:T(8,128)(2,1)S(1)} %copy-done.13), kind=kOutput, calls=%fused_computation.1 | convolution fusion | flops 4758700032 | bytes 12460032 | tf_op jit(solution)/shard_map/dot_general | solution.py:42
  91.8 2.5 constant_dynamic-slice_fusion.45
  97.8 2.5 collective-permute-start.11
  105.1 17.0 %ffn_backward.2 = (bf16[4,1008,768]{2,1,0:T(8,128)(2,1)S(1)}, f32[1008,768]{1,0:T(8,128)S(1)}, bf16[1008,768]{1,0:T(8,128)(2,1)S(1)}, bf16[1008,768]{1,0:T(8,128)(2,1)S(1)}, f32[8,768]{1,0:T(8,128)S(1)}) custom-call(bf16[1008,768]{1,0:T(8,128)(2,1)S(1)} %copy-done.14, bf16[1008,3072]{1,0:T(8,128)(2,1)} %get-tuple-element.251.slope_ref, ...), custom_call_target="tpu_custom_call" | custom-call | flops 535088 | bytes 1633 | tf_op jit(solution)/shard_map/ffn_backward/pallas_call | solution.py:807
  123.9 3.2 fusion.24
  138.0 2.6 add_convert_fusion
  147.4 9.9 %ffn_forward.3 = (f32[256,768]{1,0:T(8,128)}, bf16[256,768]{1,0:T(8,128)(2,1)}, bf16[256,3072]{1,0:T(8,128)(2,1)}, bf16[256,3072]{1,0:T(8,128)(2,1)}, bf16[256,768]{1,0:T(8,128)(2,1)}) custom-call(bf16[256,768]{1,0:T(8,128)(2,1)} %bitcast.614, f32[256,896]{1,0:T(8,128)} %bitcast.605, bf16[2,768,768]{2,1,0:T(8,128)(2,1)} %wo_ref.7, f32[2,768]{1,0:T(2,128)} %bo_ref.3, ...), custom_call_target="tpu_custom_call" | custom-call | flops 135895 | bytes 747 | tf_op jit(solution)/shard_map/ffn_forward/pallas_call | solution.py:702
  158.1 2.9 collective-permute-done.16
  167.5 10.4 %ffn_backward.3 = (bf16[4,256,768]{2,1,0:T(8,128)(2,1)}, f32[256,768]{1,0:T(8,128)}, bf16[256,768]{1,0:T(8,128)(2,1)}, bf16[256,768]{1,0:T(8,128)(2,1)}, f32[8,768]{1,0:T(8,128)}) custom-call(bf16[256,768]{1,0:T(8,128)(2,1)} %bitcast.646, bf16[256,3072]{1,0:T(8,128)(2,1)} %get-tuple-element.286.slope_ref, f32[256,768]{1,0:T(8,128)} %get-tuple-element.287.x1_ref, ...), custom_call_target="tpu_custom_call" | custom-call | flops 135895 | bytes 766 | tf_op jit(solution)/shard_map/ffn_backward/pallas_call | solution.py:807
  194.2 16.3 %attention_backward.2 = (bf16[1008,768]{1,0:T(8,128)(2,1)S(1)}, bf16[1008,768]{1,0:T(8,128)(2,1)S(1)}, bf16[1008,768]{1,0:T(8,128)(2,1)S(1)}, bf16[256,384]{1,0:...) custom-call(bf16[1008,2304]{1,0:T(8,128)(2,1)S(1)} %bitcast.600, ...), custom_call_target="tpu_custom_call" | custom-call | flops 253919 | bytes 270 | tf_op jit(solution)/shard_map/attention_backward/pallas_call | solution.py:572
  218.7 2.5 maximum_bitcast_fusion
  224.1 16.1 %attention_backward.3 = (bf16[1008,768]{1,0:T(8,128)(2,1)S(1)}, bf16[1008,768]{1,0:T(8,128)(2,1)S(1)}, bf16[1008,768]{1,0:T(8,128)(2,1)S(1)}, bf16[256,384]{1,0:...) custom-call(bf16[1008,2304]{1,0:T(8,128)(2,1)S(1)} %bitcast.600, ...), custom_call_target="tpu_custom_call", output_to_operand_aliasing={{0}: (17, {}), {1}: (18, {}), {2}: (19, {})} | custom-call | flops 253919 | bytes 270 | tf_op jit(solution)/shard_map/attention_backward/pallas_call | solution.py:572
  251.1 5.5 %input_grad.2 = (bf16[1008,768]{1,0:T(8,128)(2,1)S(1)}, f32[8,768]{1,0:T(8,128)S(1)}) custom-call(bf16[1008,768]{1,0:T(8,128)(2,1)S(1)} %get-tuple-element.352.dq_ref, bf16[1008,768]{1,0:T(8,128)(2,1)S(1)} %get-tuple-element.342.dk_ref, bf16[1008,768]{1,0:T(8,128)(2,1)S(1)} %get-tuple-element.343.dv_ref, bf16[2,768,2304]{2,1,0:T(8,128)(2,1)S(1)} %bitcast.604, ...), custom_call_target="tpu_custom_call" | custom-call | flops 178362 | bytes 718 | tf_op jit(solution)/shard_map/input_grad/pallas_call | solution.py:866
  256.6 3.7 %collective-permute-done.33 = bf16[2,6,32,384]{3,2,1,0:T(8,128)(2,1)S(1)} collective-permute-done((bf16[2,6,32,384]{3,2,1,0:T(8,128)(2,1)S(1)}, bf16[2,6,32,384]{3,2,1,0:T(8,128)(2,1)S(1)}, u32[]{:S(2)}, u32[]{:S(2)}) %collective-permute-start.33) | collective-permute-done | bytes 294944 | tf_op jit(solution)/shard_map/ppermute | solution.py:902
  263.2 5.9 %collective-permute-done.34 = bf16[1,6,32,384]{3,2,1,0:T(8,128)(2,1)S(1)} collective-permute-done((bf16[1,6,32,384]{3,2,1,0:T(8,128)(2,1)S(1)}, bf16[1,6,32,384]{3,2,1,0:T(8,128)(2,1)S(1)}, u32[]{:S(2)}, u32[]{:S(2)}) %collective-permute-start.34) | collective-permute-done | bytes 147488 | tf_op jit(solution)/shard_map/ppermute | solution.py:902
  273.1 5.3 %collective-permute-done.37 = bf16[1,6,32,384]{3,2,1,0:T(8,128)(2,1)S(1)} collective-permute-done((bf16[1,6,32,384]{3,2,1,0:T(8,128)(2,1)S(1)}, bf16[1,6,32,384]{3,2,1,0:T(8,128)(2,1)S(1)}, u32[]{:S(2)}, u32[]{:S(2)}) %collective-permute-start.37) | collective-permute-done | bytes 147488 | tf_op jit(solution)/shard_map/ppermute | solution.py:902
  280.0 7.6 %collective-permute-done.40 = bf16[2,6,32,384]{3,2,1,0:T(8,128)(2,1)S(1)} collective-permute-done((bf16[2,6,32,384]{3,2,1,0:T(8,128)(2,1)S(1)}, bf16[2,6,32,384]{3,2,1,0:T(8,128)(2,1)S(1)}, u32[]{:S(2)}, u32[]{:S(2)}) %collective-permute-start.40) | collective-permute-done | bytes 294944 | tf_op jit(solution)/shard_map/ppermute | solution.py:902
  297.7 4.9 %collective-permute-done.51 = bf16[3,84,768]{2,1,0:T(8,128)(2,1)S(1)} collective-permute-done((bf16[3,84,768]{2,1,0:T(8,128)(2,1)S(1)}, bf16[3,84,768]{2,1,0:T(8,128)(2,1)S(1)}, u32[]{:S(2)}, u32[]{:S(2)}) %collective-permute-start.51) | collective-permute-done | bytes 387104 | tf_op jit(solution)/shard_map/ppermute | solution.py:897
  306.3 2.2 collective-permute-start.53
  311.1 2.7 collective-permute-done.53
  317.7 2.7 collective-permute-done.58
  324.7 4.8 %collective-permute-done.59 = bf16[3,84,768]{2,1,0:T(8,128)(2,1)S(1)} collective-permute-done((bf16[3,84,768]{2,1,0:T(8,128)(2,1)S(1)}, bf16[3,84,768]{2,1,0:T(8,128)(2,1)S(1)}, u32[]{:S(2)}, u32[]{:S(2)}) %collective-permute-start.59) | collective-permute-done | bytes 387104 | tf_op jit(solution)/shard_map/ppermute | solution.py:897
  (555 shorter events, 132.6 us)
Async XLA Ops:
  8.9 13.1 %collective-permute-start.4 = (bf16[6,84,768]{2,1,0:T(8,128)(2,1)}, bf16[6,84,768]{2,1,0:T(8,128)(2,1)}, u32[]{:S(2)}, u32[]{:S(2)}) collective-permute-start(bf16[6,84,768]{2,1,0:T(8,128)(2,1)} %slice_bitcast_fusion.1), channel_id=1, source_target_pairs={{0,7},{1,0},{2,1},{3,2},{4,3},{5,4},{6,5},{7,6},{8,15},{9,8},{10,9... | collective-permute-start | bytes 2322440 | tf_op jit(solution)/shard_map/ppermute | solution.py:897
  24.5 17.8 %collective-permute-start.5 = (bf16[6,84,768]{2,1,0:T(8,128)(2,1)S(1)}, bf16[6,84,768]{2,1,0:T(8,128)(2,1)S(1)}, u32[]{:S(2)}, u32[]{:S(2)}) collective-permute-start(bf16[6,84,768]{2,1,0:T(8,128)(2,1)S(1)} %copy-done.57), channel_id=1, source_target_pairs={{0,7},{1,0},{2,1},{3,2},{4,3},{5,4},{6,5},{7,6},{8,15},{9,8},{10,9... | collective-permute-start | bytes 2322440 | tf_op jit(solution)/shard_map/ppermute | solution.py:897
  48.2 16.5 %collective-permute-start.7 = (f32[4,32,896]{2,1,0:T(8,128)S(1)}, f32[4,32,896]{2,1,0:T(8,128)}, u32[]{:S(2)}, u32[]{:S(2)}) collective-permute-start(f32[4,32,896]{2,1,0:T(8,128)S(1)} %bitcast.618), channel_id=1, source_target_pairs={{0,2},{1,3},{2,0},{3,1},{4,6},{5,7},{6,4},{7,5},{8,10},{9,11},{10,... | collective-permute-start | bytes 1376264 | tf_op jit(solution)/shard_map/ppermute | solution.py:902
  66.6 25.2 %collective-permute-start.8 = (f32[4,32,896]{2,1,0:T(8,128)S(1)}, f32[4,32,896]{2,1,0:T(8,128)S(1)}, u32[]{:S(2)}, u32[]{:S(2)}) collective-permute-start(f32[4,32,896]{2,1,0:T(8,128)S(1)} %bitcast.619), channel_id=1, source_target_pairs={{0,4},{1,5},{2,6},{3,7},{4,0},{5,1},{6,2},{7,3},{8,12},{9,13},{10,... | collective-permute-start | bytes 1376264 | tf_op jit(solution)/shard_map/ppermute | solution.py:902
  94.3 29.6 %collective-permute-start.9 = (bf16[4,4,96,768]{3,2,1,0:T(8,128)(2,1)}, bf16[4,4,96,768]{3,2,1,0:T(8,128)(2,1)}, u32[]{:S(2)}, u32[]{:S(2)}) collective-permute-start(bf16[4,4,96,768]{3,2,1,0:T(8,128)(2,1)} %get-tuple-element.432), channel_id=1, source_target_pairs={{0,1},{1,0},{2,3},{3,2},{4,5},{5,4},{6,7},{7,6},{8,9},{9,8},{10,11... | collective-permute-start | bytes 7077896 | tf_op jit(solution)/shard_map/ppermute | solution.py:902
  95.1 28.8 %collective-permute-start.13 = (f32[4,32,896]{2,1,0:T(8,128)S(1)}, f32[4,32,896]{2,1,0:T(8,128)}, u32[]{:S(2)}, u32[]{:S(2)}) collective-permute-start(f32[4,32,896]{2,1,0:T(8,128)S(1)} %bitcast.616), channel_id=1, source_target_pairs={{0,1},{1,0},{2,3},{3,2},{4,5},{5,4},{6,7},{7,6},{8,9},{9,8},{10,11... | collective-permute-start | bytes 1376264 | tf_op jit(solution)/shard_map/ppermute | solution.py:902
  96.3 27.5 %collective-permute-start.10 = (bf16[32,768]{1,0:T(8,128)(2,1)S(1)}, bf16[32,768]{1,0:T(8,128)(2,1)S(1)}, u32[]{:S(2)}, u32[]{:S(2)}) collective-permute-start(bf16[32,768]{1,0:T(8,128)(2,1)S(1)} %bitcast.775), channel_id=1, source_target_pairs={{0,2},{1,3},{2,4},{3,5},{4,6},{5,7},{6,0},{7,1},{8,10},{9,11},{10,... | collective-permute-start | bytes 147464 | tf_op jit(solution)/shard_map/ppermute | solution.py:897
  97.8 26.0 %collective-permute-start.11 = (bf16[32,768]{1,0:T(8,128)(2,1)S(1)}, bf16[32,768]{1,0:T(8,128)(2,1)S(1)}, u32[]{:S(2)}, u32[]{:S(2)}) collective-permute-start(bf16[32,768]{1,0:T(8,128)(2,1)S(1)} %bitcast.776), channel_id=1, source_target_pairs={{0,4},{1,5},{2,6},{3,7},{4,0},{5,1},{6,2},{7,3},{8,12},{9,13},{10,... | collective-permute-start | bytes 147464 | tf_op jit(solution)/shard_map/ppermute | solution.py:897
  100.3 23.6 %collective-permute-start.12 = (bf16[32,768]{1,0:T(8,128)(2,1)S(1)}, bf16[32,768]{1,0:T(8,128)(2,1)S(1)}, u32[]{:S(2)}, u32[]{:S(2)}) collective-permute-start(bf16[32,768]{1,0:T(8,128)(2,1)S(1)} %bitcast.777), channel_id=1, source_target_pairs={{0,6},{1,7},{2,0},{3,1},{4,2},{5,3},{6,4},{7,5},{8,14},{9,15},{10,... | collective-permute-start | bytes 147464 | tf_op jit(solution)/shard_map/ppermute | solution.py:897
  132.4 28.6 %collective-permute-start.16 = (bf16[4,4,2,24,768]{4,3,1,0,2:T(8,128)(2,1)}, bf16[4,4,2,24,768]{4,3,1,0,2:T(8,128)(2,1)S(1)}, u32[]{:S(2)}, u32[]{:S(2)}) collective-permute-start(bf16[4,4,2,24,768]{4,3,1,0,2:T(8,128)(2,1)} %fusion.24), channel_id=1, source_target_pairs={{0,8},{8,0},{16,24},{24,16},{1,9},{9,1},{17,25},{25,17},{2,10},{10... | collective-permute-start | bytes 3538952 | tf_op jit(solution)/shard_map/ppermute | solution.py:902
  137.8 20.3 %collective-permute-start.17 = (bf16[4,32,768]{2,1,0:T(8,128)(2,1)S(1)}, bf16[4,32,768]{2,1,0:T(8,128)(2,1)S(1)}, u32[]{:S(2)}, u32[]{:S(2)}) collective-permute-start(bf16[4,32,768]{2,1,0:T(8,128)(2,1)S(1)} %constant_dynamic-slice_fusion.39), channel_id=1, source_target_pairs={{0,1},{1,0},{2,3},{3,2},{4,5},{5,4},{6,7},{7,6},{8,9},{9,8},{10,11... | collective-permute-start | bytes 589832 | tf_op jit(solution)/shard_map/ppermute | solution.py:902
  146.3 35.6 %collective-permute-start.18 = (bf16[3,2,96,768]{3,2,1,0:T(8,128)(2,1)}, bf16[3,2,96,768]{3,2,1,0:T(8,128)(2,1)}, u32[]{:S(2)}, u32[]{:S(2)}) collective-permute-start(bf16[3,2,96,768]{3,2,1,0:T(8,128)(2,1)} %get-tuple-element.434), channel_id=1, source_target_pairs={{0,2},{1,3},{2,0},{3,1},{4,6},{5,7},{6,4},{7,5},{8,10},{9,11},{10,... | collective-permute-start | bytes 2654216 | tf_op jit(solution)/shard_map/ppermute | solution.py:902
  163.1 18.8 %collective-permute-start.19 = (bf16[2,4,2,24,768]{4,3,1,0,2:T(8,128)(2,1)}, bf16[2,4,2,24,768]{4,3,1,0,2:T(8,128)(2,1)}, u32[]{:S(2)}, u32[]{:S(2)}) collective-permute-start(bf16[2,4,2,24,768]{4,3,1,0,2:T(8,128)(2,1)} %fusion.50), channel_id=1, source_target_pairs={{0,8},{8,0},{16,24},{24,16},{1,9},{9,1},{17,25},{25,17},{2,10},{10... | collective-permute-start | bytes 1769480 | tf_op jit(solution)/shard_map/ppermute | solution.py:902
  165.9 22.4 %collective-permute-start.20 = (bf16[4,4,24,768]{3,2,1,0:T(8,128)(2,1)}, bf16[4,4,24,768]{3,2,1,0:T(8,128)(2,1)}, u32[]{:S(2)}, u32[]{:S(2)}) collective-permute-start(bf16[4,4,24,768]{3,2,1,0:T(8,128)(2,1)} %get-tuple-element.438), channel_id=1, source_target_pairs={{0,16},{8,24},{16,0},{24,8},{1,17},{9,25},{17,1},{25,9},{2,18},{10... | collective-permute-start | bytes 1769480 | tf_op jit(solution)/shard_map/ppermute | solution.py:902
  167.4 44.4 %collective-permute-start.24 = (bf16[6,84,768]{2,1,0:T(8,128)(2,1)}, bf16[6,84,768]{2,1,0:T(8,128)(2,1)}, u32[]{:S(2)}, u32[]{:S(2)}) collective-permute-start(bf16[6,84,768]{2,1,0:T(8,128)(2,1)} %get-tuple-element.313), channel_id=1, source_target_pairs={{0,1},{1,2},{2,3},{3,4},{4,5},{5,6},{6,7},{7,0},{8,9},{9,10},{10,1... | collective-permute-start | bytes 2322440 | tf_op jit(solution)/shard_map/ppermute | solution.py:897
  183.2 28.6 %collective-permute-start.21 = (bf16[3,2,2,24,768]{4,3,2,1,0:T(8,128)(2,1)S(1)}, bf16[3,2,2,24,768]{4,3,2,1,0:T(8,128)(2,1)S(1)}, u32[]{:S(2)}, u32[]{:S(2)}) collective-permute-start(bf16[3,2,2,24,768]{4,3,2,1,0:T(8,128)(2,1)S(1)} %fusion.54), channel_id=1, source_target_pairs={{0,8},{8,0},{16,24},{24,16},{1,9},{9,1},{17,25},{25,17},{2,10},{10... | collective-permute-start | bytes 1327112 | tf_op jit(solution)/shard_map/ppermute | solution.py:902
  185.2 26.6 %collective-permute-start.22 = (bf16[2,4,24,768]{3,2,1,0:T(8,128)(2,1)S(1)}, bf16[2,4,24,768]{3,2,1,0:T(8,128)(2,1)S(1)}, u32[]{:S(2)}, u32[]{:S(2)}) collective-permute-start(bf16[2,4,24,768]{3,2,1,0:T(8,128)(2,1)S(1)} %get-tuple-element.458), channel_id=1, source_target_pairs={{0,16},{8,24},{16,0},{24,8},{1,17},{9,25},{17,1},{25,9},{2,18},{10... | collective-permute-start | bytes 884744 | tf_op jit(solution)/shard_map/ppermute | solution.py:902
  189.6 22.2 %collective-permute-start.23 = (bf16[2,4,24,768]{3,2,1,0:T(8,128)(2,1)S(1)}, bf16[2,4,24,768]{3,2,1,0:T(8,128)(2,1)S(1)}, u32[]{:S(2)}, u32[]{:S(2)}) collective-permute-start(bf16[2,4,24,768]{3,2,1,0:T(8,128)(2,1)S(1)} %fusion.68), channel_id=1, source_target_pairs={{0,2},{1,3},{2,0},{3,1},{4,6},{5,7},{6,4},{7,5},{8,10},{9,11},{10,... | collective-permute-start | bytes 884744 | tf_op jit(solution)/shard_map/ppermute | solution.py:902
  190.8 30.4 %collective-permute-start.25 = (bf16[9,2,24,768]{3,2,0,1:T(8,128)(2,1)S(1)}, bf16[9,2,24,768]{3,2,0,1:T(8,128)(2,1)S(1)}, u32[]{:S(2)}, u32[]{:S(2)}) collective-permute-start(bf16[9,2,24,768]{3,2,0,1:T(8,128)(2,1)S(1)} %copy_bitcast_fusion.2), channel_id=1, source_target_pairs={{0,8},{8,0},{16,24},{24,16},{1,9},{9,1},{17,25},{25,17},{2,10},{10... | collective-permute-start | bytes 1990664 | tf_op jit(solution)/shard_map/ppermute | solution.py:902
  215.8 24.5 %collective-permute-start.29 = (bf16[2,2,24,768]{3,2,1,0:T(8,128)(2,1)S(1)}, bf16[2,2,24,768]{3,2,1,0:T(8,128)(2,1)S(1)}, u32[]{:S(2)}, u32[]{:S(2)}) collective-permute-start(bf16[2,2,24,768]{3,2,1,0:T(8,128)(2,1)S(1)} %fusion.88), channel_id=1, source_target_pairs={{0,2},{1,3},{2,0},{3,1},{4,6},{5,7},{6,4},{7,5},{8,10},{9,11},{10,... | collective-permute-start | bytes 442376 | tf_op jit(solution)/shard_map/ppermute | solution.py:902
  216.9 23.4 %collective-permute-start.30 = (bf16[1,4,24,768]{3,2,1,0:T(8,128)(2,1)S(1)}, bf16[1,4,24,768]{3,2,1,0:T(8,128)(2,1)S(1)}, u32[]{:S(2)}, u32[]{:S(2)}) collective-permute-start(bf16[1,4,24,768]{3,2,1,0:T(8,128)(2,1)S(1)} %fusion.74), channel_id=1, source_target_pairs={{0,4},{1,5},{2,6},{3,7},{4,0},{5,1},{6,2},{7,3},{8,12},{9,13},{10,... | collective-permute-start | bytes 442376 | tf_op jit(solution)/shard_map/ppermute | solution.py:902
  221.5 18.8 %collective-permute-start.28 = (bf16[360,768]{1,0:T(8,128)(2,1)S(1)}, bf16[360,768]{1,0:T(8,128)(2,1)S(1)}, u32[]{:S(2)}, u32[]{:S(2)}) collective-permute-start(bf16[360,768]{1,0:T(8,128)(2,1)S(1)} %pad_maximum_fusion.7), channel_id=1, source_target_pairs={{0,16},{8,24},{16,0},{24,8},{1,17},{9,25},{17,1},{25,9},{2,18},{10... | collective-permute-start | bytes 1658888 | tf_op jit(solution)/shard_map/ppermute | solution.py:902
  223.2 17.1 %collective-permute-start.27 = (bf16[4,3,2,24,384]{4,3,2,1,0:T(8,128)(2,1)S(1)}, bf16[4,3,2,24,384]{4,3,2,1,0:T(8,128)(2,1)S(1)}, u32[]{:S(2)}, u32[]{:S(2)}) collective-permute-start(bf16[4,3,2,24,384]{4,3,2,1,0:T(8,128)(2,1)S(1)} %fusion.57), channel_id=1, source_target_pairs={{0,8},{8,0},{16,24},{24,16},{1,9},{9,1},{17,25},{25,17},{2,10},{10... | collective-permute-start | bytes 1327112 | tf_op jit(solution)/shard_map/ppermute | solution.py:902
  246.9 13.4 %collective-permute-start.33 = (bf16[2,6,32,384]{3,2,1,0:T(8,128)(2,1)S(1)}, bf16[2,6,32,384]{3,2,1,0:T(8,128)(2,1)S(1)}, u32[]{:S(2)}, u32[]{:S(2)}) collective-permute-start(bf16[2,6,32,384]{3,2,1,0:T(8,128)(2,1)S(1)} %get-tuple-element.454), channel_id=1, source_target_pairs={{0,2},{1,3},{2,0},{3,1},{4,6},{5,7},{6,4},{7,5},{8,10},{9,11},{10,... | collective-permute-start | bytes 884744 | tf_op jit(solution)/shard_map/ppermute | solution.py:902
  248.8 14.4 %collective-permute-start.36 = (bf16[120,768]{1,0:T(8,128)(2,1)S(1)}, bf16[120,768]{1,0:T(8,128)(2,1)S(1)}, u32[]{:S(2)}, u32[]{:S(2)}) collective-permute-start(bf16[120,768]{1,0:T(8,128)(2,1)S(1)} %pad_maximum_fusion.24), channel_id=1, source_target_pairs={{0,4},{1,5},{2,6},{3,7},{4,0},{5,1},{6,2},{7,3},{8,12},{9,13},{10,... | collective-permute-start | bytes 552968 | tf_op jit(solution)/shard_map/ppermute | solution.py:902
  249.7 19.4 %collective-permute-start.35 = (bf16[4,3,2,24,384]{4,3,2,1,0:T(8,128)(2,1)S(1)}, bf16[4,3,2,24,384]{4,3,2,1,0:T(8,128)(2,1)S(1)}, u32[]{:S(2)}, u32[]{:S(2)}) collective-permute-start(bf16[4,3,2,24,384]{4,3,2,1,0:T(8,128)(2,1)S(1)} %fusion.58), channel_id=1, source_target_pairs={{0,8},{8,0},{16,24},{24,16},{1,9},{9,1},{17,25},{25,17},{2,10},{10... | collective-permute-start | bytes 1327112 | tf_op jit(solution)/shard_map/ppermute | solution.py:902
  269.7 17.9 %collective-permute-start.42 = (bf16[576,384]{1,0:T(8,128)(2,1)S(1)}, bf16[576,384]{1,0:T(8,128)(2,1)S(1)}, u32[]{:S(2)}, u32[]{:S(2)}) collective-permute-start(bf16[576,384]{1,0:T(8,128)(2,1)S(1)} %pad_maximum_fusion.10), channel_id=1, source_target_pairs={{0,16},{8,24},{16,0},{24,8},{1,17},{9,25},{17,1},{25,9},{2,18},{10... | collective-permute-start | bytes 1327112 | tf_op jit(solution)/shard_map/ppermute | solution.py:902
  278.9 12.8 %collective-permute-start.45 = (bf16[4,2,24,768]{3,2,0,1:T(8,128)(2,1)S(1)}, bf16[4,2,24,768]{3,2,0,1:T(8,128)(2,1)S(1)}, u32[]{:S(2)}, u32[]{:S(2)}) collective-permute-start(bf16[4,2,24,768]{3,2,0,1:T(8,128)(2,1)S(1)} %pad_maximum_fusion.16), channel_id=1, source_target_pairs={{0,16},{8,24},{16,0},{24,8},{1,17},{9,25},{17,1},{25,9},{2,18},{10... | collective-permute-start | bytes 884744 | tf_op jit(solution)/shard_map/ppermute | solution.py:902
  308.8 13.2 %collective-permute-start.57 = (bf16[240,768]{1,0:T(8,128)(2,1)S(1)}, bf16[240,768]{1,0:T(8,128)(2,1)S(1)}, u32[]{:S(2)}, u32[]{:S(2)}) collective-permute-start(bf16[240,768]{1,0:T(8,128)(2,1)S(1)} %pad_maximum_fusion.14), channel_id=1, source_target_pairs={{0,16},{8,24},{16,0},{24,8},{1,17},{9,25},{17,1},{25,9},{2,18},{10... | collective-permute-start | bytes 1105928 | tf_op jit(solution)/shard_map/ppermute | solution.py:902
  314.1 16.7 %collective-permute-start.54 = (bf16[336,384]{1,0:T(8,128)(2,1)S(1)}, bf16[336,384]{1,0:T(8,128)(2,1)S(1)}, u32[]{:S(2)}, u32[]{:S(2)}) collective-permute-start(bf16[336,384]{1,0:T(8,128)(2,1)S(1)} %pad_maximum_fusion.18), channel_id=1, source_target_pairs={{0,8},{8,0},{16,24},{24,16},{1,9},{9,1},{17,25},{25,17},{2,10},{10... | collective-permute-start | bytes 774152 | tf_op jit(solution)/shard_map/ppermute | solution.py:902
  315.5 15.3 %collective-permute-start.55 = (bf16[336,384]{1,0:T(8,128)(2,1)S(1)}, bf16[336,384]{1,0:T(8,128)(2,1)S(1)}, u32[]{:S(2)}, u32[]{:S(2)}) collective-permute-start(bf16[336,384]{1,0:T(8,128)(2,1)S(1)} %pad_maximum_fusion.18), channel_id=1, source_target_pairs={{0,16},{8,24},{16,0},{24,8},{1,17},{9,25},{17,1},{25,9},{2,18},{10... | collective-permute-start | bytes 774152 | tf_op jit(solution)/shard_map/ppermute | solution.py:902
  317.1 13.8 %collective-permute-start.56 = (bf16[336,384]{1,0:T(8,128)(2,1)S(1)}, bf16[336,384]{1,0:T(8,128)(2,1)S(1)}, u32[]{:S(2)}, u32[]{:S(2)}) collective-permute-start(bf16[336,384]{1,0:T(8,128)(2,1)S(1)} %pad_maximum_fusion.18), channel_id=1, source_target_pairs={{0,24},{8,16},{16,8},{24,0},{1,25},{9,17},{17,9},{25,1},{2,26},{10... | collective-permute-start | bytes 774152 | tf_op jit(solution)/shard_map/ppermute | solution.py:902
  (110 other events, 736.5 us)
